TPU v7x, 32 devices: a whole 2x2x4 slice. The times are simulated.
32 devices in a mesh: rep: 2 (over y), lat: 8 (over z, x), blk: 2 (over core).
Axes of the slice: x: 2, y: 2, z: 4, core: 2. Of those that a mesh axis runs over, the one named last changes fastest.
Arguments:
- field: bfloat16 [32, 1440, 384], P(('rep', 'lat'), None, 'blk'), parts along dimension 0, may hold values from -6 to 6
- cotangent: bfloat16 [32, 1440, 384], P(('rep', 'lat'), None, 'blk'), parts along dimension 0, may hold values from -6 to 6
- first_weight: bfloat16 [4, 96, 192], replicated, may hold values from -0.4375 to 0.4375
- first_bias: float32 [4, 192], replicated, may hold values from -3 to 3
- second_weight: bfloat16 [4, 96, 192], replicated, may hold values from -0.4375 to 0.4375
- second_bias: float32 [4, 192], replicated, may hold values from -3 to 3
Outputs:
- mixed_field: bfloat16 [32, 1440, 384], P(('rep', 'lat'), None, 'blk'), parts along dimension 0
- field_gradient: bfloat16 [32, 1440, 384], P(('rep', 'lat'), None, 'blk'), parts along dimension 0
- first_gradient: float32 [8, 18432], P(('rep', 'blk'), 'lat'), parts along dimension 0
- second_gradient: float32 [8, 18432], P(('rep', 'blk'), 'lat'), parts along dimension 0
There are 2 independent parts, one for each index of `rep`. A program takes and returns all parts, laid end to end along the dimension named above; an argument that names none is the same for every part. Nothing has to cross between parts.
All inputs are finite; a program needn't handle non-finite values.
Results may differ from a plain program's by a relative error of at most 0.0075.
The roundings to bfloat16 on the way count: a program that leaves them out, or rounds other values in their place, can miss the bound.
Values may be sent and summed in bfloat16 or wider, within the bound.
No kernel may reach another device: no remote copies, remote signals or barrier semaphores. Data moves between devices by JAX's collectives and lax.ppermute only.
A program may use at most 128 MiB of HBM per device.

v0:
```python
import functools
import math

import jax
import jax.numpy as jnp
import numpy as np
from jax import lax
from jax.experimental import pallas as pl
from jax.experimental.pallas import tpu as pltpu
from jax.sharding import PartitionSpec as P

KW = 512
LANES = 128
HALF = 64
PACK = 16
VMEM_BYTES = 48 * 1024 * 1024

SHRINK = 0.01
GELU_SCALE = 0.7978845608028654
GELU_CUBIC = 0.044715
F32 = jnp.float32
BF16 = jnp.bfloat16


def zonal_waves(col_count, kept):
    column = np.arange(col_count, dtype=np.int64)
    wavenumber = np.arange(kept, dtype=np.int64)
    phases = column[:, None] * wavenumber[None, :] % col_count
    angles = phases.astype(np.float32) * np.float32(2.0 * math.pi / col_count)
    scaling = np.float32(1.0 / math.sqrt(col_count))
    cosine = np.cos(angles) * scaling
    sines = np.sin(angles) * scaling
    return np.stack([cosine, -sines], axis=1).astype(BF16)


def meridian_waves(row_count):
    indices = np.arange(row_count, dtype=np.int64)
    phases = indices[:, None] * indices[None, :] % row_count
    angles = phases.astype(np.float32) * np.float32(2.0 * math.pi / row_count)
    scaling = np.float32(1.0 / math.sqrt(row_count))
    return ((np.cos(angles) * scaling).astype(BF16), (np.sin(angles) * scaling).astype(BF16))


def wave_factor(kept):
    return np.where(np.arange(kept) == 0, 1.0, 2.0).astype(np.float32)


def mm(former, latter):
    return jnp.dot(former, latter, preferred_element_type=F32)


def swap_parts(values, first_sign):
    lane = lax.broadcasted_iota(jnp.int32, (1, LANES), 1)
    sign = jnp.where(lane < HALF, first_sign, -first_sign).astype(F32)
    return pltpu.roll(values, HALF, axis=1) * sign


def zonal_kernel(field_ref, table_ref, scale_ref, out_ref):
    result = (mm(field_ref[...], table_ref[...]) * scale_ref[...]).astype(BF16)
    for piece in range(out_ref.shape[0]):
        out_ref[piece] = result[:, piece * LANES : (piece + 1) * LANES]


def zonal(field_rows, table, scale, pieces):
    rows, col_count = field_rows.shape
    step = 2
    return pl.pallas_call(
        zonal_kernel,
        grid=(pieces // step,),
        in_specs=[
            pl.BlockSpec((rows, col_count), lambda i: (0, 0)),
            pl.BlockSpec((col_count, step * LANES), lambda i: (0, i)),
            pl.BlockSpec((1, step * LANES), lambda i: (0, i)),
        ],
        out_specs=pl.BlockSpec((step, rows, LANES), lambda i: (i, 0, 0)),
        out_shape=jax.ShapeDtypeStruct((pieces, rows, LANES), BF16),
        compiler_params=pltpu.CompilerParams(vmem_limit_bytes=VMEM_BYTES),
        cost_estimate=pl.CostEstimate(
            flops=2 * rows * col_count * pieces * LANES,
            bytes_accessed=2 * (rows * col_count + (col_count + rows) * pieces * LANES),
            transcendentals=0,
        ),
    )(field_rows, table, scale)


def inverse_kernel(scaled, modes_ref, table_ref, scale_ref, base_ref, out_ref):
    pieces = modes_ref.shape[0]
    modes = jnp.concatenate([modes_ref[piece] for piece in range(pieces)], axis=1)
    if scaled:
        modes = (modes.astype(F32) * scale_ref[...]).astype(BF16)
    out_ref[...] = (base_ref[...].astype(F32) + mm(modes, table_ref[...])).astype(BF16)


def inverse(modes, table, scale, base, scaled):
    pieces, rows, _ = modes.shape
    kept, col_count = table.shape
    width = 512
    return pl.pallas_call(
        functools.partial(inverse_kernel, scaled),
        grid=(pl.cdiv(col_count, width),),
        in_specs=[
            pl.BlockSpec((pieces, rows, LANES), lambda i: (0, 0, 0)),
            pl.BlockSpec((kept, width), lambda i: (0, i)),
            pl.BlockSpec((1, kept), lambda i: (0, 0)),
            pl.BlockSpec((rows, width), lambda i: (0, i)),
        ],
        out_specs=pl.BlockSpec((rows, width), lambda i: (0, i)),
        out_shape=jax.ShapeDtypeStruct((rows, col_count), BF16),
        compiler_params=pltpu.CompilerParams(vmem_limit_bytes=VMEM_BYTES),
        cost_estimate=pl.CostEstimate(
            flops=2 * rows * col_count * kept,
            bytes_accessed=2 * (2 * rows * col_count + (col_count + rows) * kept),
            transcendentals=0,
        ),
    )(modes, table, scale, base)


def meridian(load, mixer, first_sign, channels, store):
    count = mixer.shape[1] // PACK
    for start in range(0, channels, 2 * PACK):
        pair = jnp.concatenate(
            [load(start + shift).reshape(count * PACK, LANES) for shift in (0, PACK)], axis=1
        )
        both = mm(mixer[...], pair)
        for index in range(2):
            half = both[:, index * LANES : (index + 1) * LANES]
            value = half[: count * PACK] + swap_parts(half[count * PACK :], first_sign)
            store(start + index * PACK, value.reshape(count, PACK, LANES))


def complex_dot(weights, operand, first_sign):
    width = weights.shape[0] // 2
    both = mm(weights, jnp.concatenate(operand, axis=1))
    return [
        both[:width, i * LANES : (i + 1) * LANES]
        + swap_parts(both[width:, i * LANES : (i + 1) * LANES], first_sign)
        for i in range(len(operand))
    ]


def forward_kernel(
    modes_ref, mixer_ref, first_ref, first_bias_ref, second_ref, second_bias_ref,
    out_ref, harm_ref, hidden_ref, slope_ref, gate_ref, shrunk_ref,
):
    count, channels, _ = modes_ref.shape
    groups, _, width = first_ref.shape

    def keep(start, value):
        harm_ref[:, start : start + PACK, :] = value.astype(BF16)

    meridian(lambda c: modes_ref[:, c : c + PACK, :], mixer_ref, 1.0, channels, keep)
    for group in range(groups):
        span = slice(group * width, (group + 1) * width)
        for row in range(0, count, 2):
            pre = complex_dot(first_ref[group], [harm_ref[row + i, span, :] for i in range(2)], -1.0)
            hidden = []
            for i in range(2):
                v = pre[i] + first_bias_ref[group]
                square = v * v
                tangent = jnp.tanh(GELU_SCALE * (v + GELU_CUBIC * square * v))
                outer = 0.5 * (1.0 + tangent)
                inner = GELU_SCALE * (1.0 + 3.0 * GELU_CUBIC * square)
                hidden.append((v * outer).astype(BF16))
                hidden_ref[row + i, span, :] = hidden[i]
                slope_ref[row + i, span, :] = outer + 0.5 * v * (1.0 - tangent * tangent) * inner
            pre = complex_dot(second_ref[group], hidden, -1.0)
            for i in range(2):
                v = pre[i] + second_bias_ref[group]
                squashed = jnp.tanh(v * (1.0 / SHRINK))
                shrunk_ref[row + i, span, :] = (v - SHRINK * squashed).astype(BF16)
                gate_ref[row + i, span, :] = squashed * squashed

    def emit(start, value):
        out_ref[:, start : start + PACK, :] = value.astype(BF16)

    meridian(lambda c: shrunk_ref[:, c : c + PACK, :], mixer_ref, -1.0, channels, emit)


def whole(*shape):
    return pl.BlockSpec(shape, lambda: (0,) * len(shape))


def forward_middle(modes, mixer, first, first_bias, second, second_bias):
    shape = modes.shape
    size = math.prod(shape)
    kinds = (BF16, BF16, BF16, F32, F32)
    return pl.pallas_call(
        forward_kernel,
        in_specs=[whole(*a.shape) for a in (modes, mixer, first, first_bias, second, second_bias)],
        out_specs=[whole(*shape) for _ in kinds],
        out_shape=[jax.ShapeDtypeStruct(shape, kind) for kind in kinds],
        scratch_shapes=[pltpu.VMEM(shape, BF16)],
        compiler_params=pltpu.CompilerParams(vmem_limit_bytes=VMEM_BYTES),
        cost_estimate=pl.CostEstimate(
            flops=4 * size * 1024, bytes_accessed=16 * size, transcendentals=2 * size
        ),
    )(modes, mixer, first, first_bias, second, second_bias)


def nt(former, latter):
    return lax.dot_general(former, latter, (((1,), (1,)), ((), ())), preferred_element_type=F32)


def backward_kernel(
    normalizer, modes_ref, mixer_ref, first_ref, second_ref, harm_ref, hidden_ref, slope_ref, gate_ref,
    out_ref, grad_ref, adjoint_ref, back_ref,
):
    count, channels, _ = modes_ref.shape
    groups, _, width = first_ref.shape

    def keep(start, value):
        adjoint_ref[:, start : start + PACK, :] = value * gate_ref[:, start : start + PACK, :]

    meridian(lambda c: modes_ref[:, c : c + PACK, :], mixer_ref, 1.0, channels, keep)
    for group in range(groups):
        span = slice(group * width, (group + 1) * width)
        first_sum = jnp.zeros((width, 2 * width), F32)
        second_sum = jnp.zeros((width, 2 * width), F32)
        for row in range(0, count, 2):
            exact = [adjoint_ref[row + i, span, :] for i in range(2)]
            second_adjoint = [a.astype(BF16) for a in exact]
            turned = [swap_parts(a, 1.0).astype(BF16) for a in exact]
            stacked = jnp.concatenate(
                [jnp.concatenate(second_adjoint, axis=1), jnp.concatenate(turned, axis=1)], axis=0
            )
            hidden = jnp.concatenate([hidden_ref[row + i, span, :] for i in range(2)], axis=1)
            second_sum += nt(hidden, stacked)
            back = complex_dot(second_ref[group], second_adjoint, 1.0)
            exact = [back[i] * slope_ref[row + i, span, :] for i in range(2)]
            first_adjoint = [a.astype(BF16) for a in exact]
            turned = [swap_parts(a, 1.0).astype(BF16) for a in exact]
            stacked = jnp.concatenate(
                [jnp.concatenate(first_adjoint, axis=1), jnp.concatenate(turned, axis=1)], axis=0
            )
            inputs = jnp.concatenate([harm_ref[row + i, span, :] for i in range(2)], axis=1)
            first_sum += nt(inputs, stacked)
            back = complex_dot(first_ref[group], first_adjoint, 1.0)
            for i in range(2):
                back_ref[row + i, span, :] = back[i].astype(BF16)
        grad_ref[0, group] = first_sum * normalizer
        grad_ref[1, group] = second_sum * normalizer

    def emit(start, value):
        out_ref[:, start : start + PACK, :] = value.astype(BF16)

    meridian(lambda c: back_ref[:, c : c + PACK, :], mixer_ref, -1.0, channels, emit)


def backward_middle(modes, mixer, first, second, harm, hidden, slope, gate, normalizer):
    shape = modes.shape
    size = math.prod(shape)
    groups, twice, width = first.shape
    operands = (modes, mixer, first, second, harm, hidden, slope, gate)
    grad_shape = (2, groups, width, twice)
    return pl.pallas_call(
        functools.partial(backward_kernel, normalizer),
        in_specs=[whole(*a.shape) for a in operands],
        out_specs=[whole(*shape), whole(*grad_shape)],
        out_shape=[jax.ShapeDtypeStruct(shape, BF16), jax.ShapeDtypeStruct(grad_shape, F32)],
        scratch_shapes=[pltpu.VMEM(shape, F32), pltpu.VMEM(shape, BF16)],
        compiler_params=pltpu.CompilerParams(vmem_limit_bytes=VMEM_BYTES),
        cost_estimate=pl.CostEstimate(
            flops=4 * size * 1024, bytes_accessed=16 * size, transcendentals=0
        ),
    )(*operands)


def local_groups_of(array, groups):
    return lax.dynamic_slice_in_dim(array, lax.axis_index("blk") * groups, groups, axis=0)


def exchange(blocks):
    return lax.all_to_all(blocks, "lat", split_axis=0, concat_axis=0, tiled=True)


def reduce_gradients(grads, lat_count):
    kinds, groups, width, twice = grads.shape
    piece = width * twice // lat_count
    split = grads.reshape(kinds * groups, lat_count, piece).transpose(1, 0, 2)
    if kinds * groups * piece % LANES == 0:
        split = split.reshape(lat_count, kinds * groups * piece // LANES, LANES)
    total = jnp.sum(exchange(split), axis=0)
    return total.reshape(kinds, groups, piece)


def with_kernels(field, cotangent, first_weight, first_bias, second_weight, second_bias):
    local_rows, col_count, channels = field.shape
    width = first_weight.shape[1]
    groups = channels // width
    lat_count = lax.axis_size("lat")
    row_count = local_rows * lat_count
    sub_count = KW // lat_count
    waves = zonal_waves(col_count, KW)
    table = (
        waves.reshape(col_count, 2, lat_count, sub_count).transpose(0, 2, 1, 3).reshape(col_count, 2 * KW)
    )
    factor = np.repeat(wave_factor(KW).reshape(lat_count, 1, sub_count), 2, axis=1).reshape(1, 2 * KW)
    cosine, sines = meridian_waves(row_count)
    unit = np.eye(PACK, dtype=np.float32)
    mixer = np.concatenate(
        [np.kron(cosine.astype(np.float32), unit), np.kron(sines.astype(np.float32), unit)], axis=0
    ).astype(BF16)
    ahead, back = jnp.asarray(table), jnp.asarray(np.ascontiguousarray(table.T))
    factor, ones = jnp.asarray(factor), jnp.ones((1, 2 * KW), F32)
    mixer = jnp.asarray(mixer)

    def rows_of(array):
        return array.transpose(0, 2, 1).reshape(local_rows * channels, col_count)

    def grid_of(rows):
        return rows.reshape(local_rows, channels, col_count).transpose(0, 2, 1)

    def spread(blocks):
        return exchange(blocks).reshape(row_count, channels, LANES)

    def gather(modes):
        return exchange(modes.reshape(lat_count, local_rows * channels, LANES))

    def bias_lanes(bias):
        parts = local_groups_of(bias, groups).reshape(groups, 2, width, 1)
        wide = jnp.broadcast_to(parts, (groups, 2, width, sub_count))
        return wide.transpose(0, 2, 1, 3).reshape(groups, width, LANES)

    def tall(weight):
        return jnp.concatenate([weight[:, :, :width], weight[:, :, width:]], axis=1)

    own_first = local_groups_of(first_weight, groups)
    own_second = local_groups_of(second_weight, groups)
    field_rows, cotangent_rows = rows_of(field), rows_of(cotangent)
    modes = spread(zonal(field_rows, ahead, ones, lat_count))
    adjoint = spread(zonal(cotangent_rows, ahead, factor, lat_count))
    synthesis, harm, hidden, slope, gate = forward_middle(
        modes, mixer,
        own_first.transpose(0, 2, 1), bias_lanes(first_bias),
        own_second.transpose(0, 2, 1), bias_lanes(second_bias),
    )
    mixed_modes = gather(synthesis)
    returned, grads = backward_middle(
        adjoint, mixer, tall(own_first), tall(own_second), harm, hidden, slope, gate,
        1.0 / math.sqrt(row_count * KW),
    )
    return_modes = gather(returned)
    gradients = reduce_gradients(grads, lat_count)
    mixed = inverse(mixed_modes, back, factor, field_rows, True)
    field_gradient = inverse(return_modes, back, factor, cotangent_rows, False)
    return (grid_of(mixed), grid_of(field_gradient), gradients[0], gradients[1])


def gelu_value(values):
    tangent = jnp.tanh(GELU_SCALE * (values + GELU_CUBIC * values * values * values))
    return 0.5 * values * (1.0 + tangent)


def gelu_slope(values):
    tangent = jnp.tanh(GELU_SCALE * (values + GELU_CUBIC * values * values * values))
    inner = GELU_SCALE * (1.0 + 3.0 * GELU_CUBIC * values * values)
    return 0.5 * (1.0 + tangent) + 0.5 * values * (1.0 - tangent * tangent) * inner


def contract(pattern, former, latter):
    return jnp.einsum(pattern, former, latter, preferred_element_type=F32)


def complex_block(weights):
    width = weights.shape[1]
    real_part, imag_part = weights[:, :, :width], weights[:, :, width:]
    upper = jnp.stack([real_part, imag_part], axis=2)
    lower = jnp.stack([-imag_part, real_part], axis=2)
    return jnp.stack([upper, lower], axis=1)


def block_gradient(outer):
    real_part = outer[:, 0, :, 0, :] + outer[:, 1, :, 1, :]
    imag_part = outer[:, 0, :, 1, :] - outer[:, 1, :, 0, :]
    return jnp.concatenate([real_part, imag_part], axis=2)


def bias_layout(bias):
    groups, twice = bias.shape
    return bias.reshape(groups, 2, twice // 2).transpose(1, 0, 2)[None, :, None]


def plain(field, cotangent, first_weight, first_bias, second_weight, second_bias):
    local_rows, col_count, channels = field.shape
    width = first_weight.shape[1]
    groups = channels // width
    lat_count = lax.axis_size("lat")
    row_count = local_rows * lat_count
    ahead = jnp.asarray(zonal_waves(col_count, KW))
    factor = jnp.asarray(wave_factor(KW))
    cosine, sines = (jnp.asarray(t) for t in meridian_waves(row_count))
    forth = jnp.stack(
        [jnp.stack([cosine, sines], axis=-1), jnp.stack([-sines, cosine], axis=-1)], axis=1
    )
    first_block = complex_block(local_groups_of(first_weight, groups))
    second_block = complex_block(local_groups_of(second_weight, groups))

    def swap(array, split, concat):
        return lax.all_to_all(array, "lat", split_axis=split, concat_axis=concat, tiled=True)

    spectrum = contract("hwc,wrk->hrkc", field, ahead).astype(BF16)
    adjoint = (contract("hwc,wrk->hrkc", cotangent, ahead) * factor[:, None]).astype(BF16)
    modes, adjoint = swap(spectrum, 2, 0), swap(adjoint, 2, 0)
    block_shape = (row_count, 2, modes.shape[2], groups, width)
    inputs = contract("mphr,hrkc->mpkc", forth, modes).astype(BF16).reshape(block_shape)
    harmonic_adjoint = contract("mphr,hrkc->mpkc", forth, adjoint).reshape(block_shape)
    pre_first = contract("mrkgc,grcsd->mskgd", inputs, first_block) + bias_layout(
        local_groups_of(first_bias, groups)
    )
    hidden = gelu_value(pre_first).astype(BF16)
    pre_second = contract("mrkgc,grcsd->mskgd", hidden, second_block) + bias_layout(
        local_groups_of(second_bias, groups)
    )
    squashed = jnp.tanh(pre_second / SHRINK)
    shrunk = (pre_second - SHRINK * squashed).astype(BF16).reshape(modes.shape)
    second_adjoint = (harmonic_adjoint * (squashed * squashed)).astype(BF16)
    second_grad = block_gradient(contract("mrkgc,mskgd->grcsd", hidden, second_adjoint))
    hidden_adjoint = contract("mskgd,grcsd->mrkgc", second_adjoint, second_block)
    first_adjoint = (hidden_adjoint * gelu_slope(pre_first)).astype(BF16)
    first_grad = block_gradient(contract("mrkgc,mskgd->grcsd", inputs, first_adjoint))
    harmonics_adjoint = contract("mskgd,grcsd->mrkgc", first_adjoint, first_block).astype(BF16)
    synthesis = contract("mphr,mpkc->hrkc", forth, shrunk).astype(BF16)
    returned = contract(
        "mphr,mpkc->hrkc", forth, harmonics_adjoint.reshape(modes.shape)
    ).astype(BF16)
    mixed_modes, return_modes = swap(synthesis, 0, 2), swap(returned, 0, 2)
    gradients = reduce_gradients(
        jnp.stack([first_grad, second_grad]) * (1.0 / math.sqrt(row_count * KW)), lat_count
    )
    mixed_modes = (mixed_modes.astype(F32) * factor[:, None]).astype(BF16)
    mixed = (field.astype(F32) + contract("hrkc,wrk->hwc", mixed_modes, ahead)).astype(BF16)
    field_gradient = (
        cotangent.astype(F32) + contract("hrkc,wrk->hwc", return_modes, ahead)
    ).astype(BF16)
    return (mixed, field_gradient, gradients[0], gradients[1])


def on_device(field, *rest):
    local_rows, _, channels = field.shape
    lat_count = lax.axis_size("lat")
    fits = (
        KW == HALF * lat_count
        and channels % (2 * PACK) == 0
        and local_rows * lat_count % 2 == 0
        and rest[1].shape[1] % PACK == 0
        and local_rows * lat_count * PACK <= 512
    )
    return (with_kernels if fits else plain)(field, *rest)


def solution(mesh):
    placed = (P(("rep", "lat"), None, "blk"), P(("rep", "lat"), None, "blk"), P(), P(), P(), P())
    return jax.shard_map(
        on_device,
        mesh=mesh,
        in_specs=placed,
        out_specs=(
            P(("rep", "lat"), None, "blk"),
            P(("rep", "lat"), None, "blk"),
            P(("rep", "blk"), "lat"),
            P(("rep", "blk"), "lat"),
        ),
        check_vma=False,
    )
```

profile of v0, /device:TPU:0, one launch (start us, length us, event | category | flops | bytes accessed | tf_op | source)
XLA Modules:
  0.0 137.4 jit_solution(9253245836930066215)
XLA Ops:
  0.6 0.0 copy-start.1
  0.7 1.8 %copy-done.1 = bf16[1440,1024]{1,0:T(8,128)(2,1)S(1)} copy-done((bf16[1440,1024]{1,0:T(8,128)(2,1)S(1)}, bf16[1440,1024]{1,0:T(8,128)(2,1)}, u32[]{:S(2)}) %copy-start.1) | copy-done | bytes 2949144
  2.5 1.3 copy-done.5
  3.8 2.3 %shard_map.129 = bf16[8,384,128]{2,1,0:T(8,128)(2,1)S(1)} custom-call(bf16[384,1440]{1,0:T(8,128)(2,1)S(1)} %bitcast.33, bf16[1440,1024]{1,0:T(8,128)(2,1)S(1)} %copy-done.1, f32[1,1024]{1,0:T(1,128)S(1)} %broadcast_in_dim.17.scale_ref), custom_call_target="tpu_custom_call" | custom-call | flops 1132462080 | bytes 4841472 | tf_op jit(solution)/shard_map/pallas_call | solution.py:67
  6.1 0.9 copy-done.9
  7.0 7.4 %all-to-all-start = ((bf16[8,384,128]{2,1,0:T(8,128)(2,1)}), bf16[8,384,128]{2,1,0:T(8,128)(2,1)}, u32[]{:S(2)}, u32[]{:S(2)}) async-start(bf16[8,384,128]{2,1,0:T(8,128)(2,1)} %copy-done.9), calls=%async_computation | async-start | bytes 1572864 | tf_op jit(solution)/shard_map/all_to_all | solution.py:273
  14.4 1.3 copy-done.3
  15.7 2.3 %shard_map.132 = bf16[8,384,128]{2,1,0:T(8,128)(2,1)S(1)} custom-call(bf16[384,1440]{1,0:T(8,128)(2,1)S(1)} %bitcast.31, bf16[1440,1024]{1,0:T(8,128)(2,1)S(1)} %copy-done.2, f32[1,1024]{1,0:T(1,128)S(1)} %copy-done.21), custom_call_target="tpu_custom_call" | custom-call | flops 1132462080 | bytes 4841472 | tf_op jit(solution)/shard_map/pallas_call | solution.py:67
  18.0 0.9 copy-done.7
  18.9 0.0 copy-start.16
  18.9 15.7 %all-to-all-done = bf16[8,384,128]{2,1,0:T(8,128)(2,1)} async-done(((bf16[8,384,128]{2,1,0:T(8,128)(2,1)}), bf16[8,384,128]{2,1,0:T(8,128)(2,1)}, u32[]{:S(2)}, u32[]{:S(2)}) %all-to-all-start) | async-done | bytes 786464 | tf_op jit(solution)/shard_map/all_to_all | solution.py:273
  34.7 3.6 %all-to-all-start.2 = ((bf16[8,384,128]{2,1,0:T(8,128)(2,1)}), bf16[8,384,128]{2,1,0:T(8,128)(2,1)S(1)}, u32[]{:S(2)}, u32[]{:S(2)}) async-start(bf16[8,384,128]{2,1,0:T(8,128)(2,1)} %copy-done.7), calls=%async_computation.2 | async-start | bytes 1572864 | tf_op jit(solution)/shard_map/all_to_all | solution.py:273
  38.3 0.1 broadcast_in_dim.20
  38.3 0.1 broadcast_in_dim.18
  38.4 0.1 copy.17.first_bias_ref
  38.6 0.7 copy.19.second_bias_ref
  39.3 0.7 copy.18.second_ref
  40.1 0.7 copy.16.first_ref
  40.8 0.1 constant_dynamic-slice_fusion.1
  40.9 0.7 pad_maximum_fusion.1.second_ref
  41.6 0.6 pad_maximum_fusion.first_ref
  42.2 0.9 copy-done.18
  43.1 0.9 copy-done.19
  44.0 0.9 copy-done.20
  44.9 5.5 %shard_map.130 = (bf16[16,192,128]{2,1,0:T(8,128)(2,1)S(1)}, bf16[16,192,128]{2,1,0:T(8,128)(2,1)S(1)}, bf16[16,192,128]{2,1,0:T(8,128)(2,1)S(1)}, f32[16,192,128]{2,1,0:T(8,128)S(1)}, f32[16,192,128]{2,1,0:T(8,128)}) custom-call(bf16[16,192,128]{2,1,0:T(8,128)(2,1)} %bitcast.2.modes_ref, bf16[512,256]{1,0:T(8,128)(2,1)S(1)} %copy-done.16, ...), custom_call_target="tpu_custom_call" | custom-call | flops 1610612736 | bytes 6291456 | tf_op jit(solution)/shard_map/pallas_call | solution.py:187
  50.4 0.9 copy-done.10
  51.3 0.9 copy-done.12
  52.1 6.5 %all-to-all-done.2 = bf16[8,384,128]{2,1,0:T(8,128)(2,1)S(1)} async-done(((bf16[8,384,128]{2,1,0:T(8,128)(2,1)}), bf16[8,384,128]{2,1,0:T(8,128)(2,1)S(1)}, u32[]{:S(2)}, u32[]{:S(2)}) %all-to-all-start.2) | async-done | bytes 786464 | tf_op jit(solution)/shard_map/all_to_all | solution.py:273
  58.6 1.1 copy-done.13
  59.7 0.9 copy-done.14
  60.6 0.9 copy-done.15
  61.5 0.9 copy-done.17
  62.5 7.9 %shard_map.133 = (bf16[16,192,128]{2,1,0:T(8,128)(2,1)S(1)}, f32[2,2,96,192]{3,2,1,0:T(8,128)S(1)}) custom-call(bf16[16,192,128]{2,1,0:T(8,128)(2,1)S(1)} %bitcast.35, bf16[512,256]{1,0:T(8,128)(2,1)S(1)} %copy-done.17, bf16[2,192,96]{2,1,0:T(8,128)(2,1)S(1)} %copy-done.15, bf16[2,192,96]{2,1,0:T(8,128)(2,1)S(1)} %copy-done.14, ...), custom_call_target="tpu_custom_call" | custom-call | flops 1610612736 | bytes 6291456 | tf_op jit(solution)/shard_map/pallas_call | solution.py:255
  70.4 0.9 copy-done.11
  71.3 0.2 reshape.63
  71.5 0.1 copy.22
  71.6 0.1 reshape.64
  71.7 13.9 %all_to_all.25 = f32[8,72,128]{2,1,0:T(8,128)S(1)} all-to-all(f32[8,72,128]{2,1,0:T(8,128)S(1)} %reshape.64), channel_id=1, replica_groups=mesh['rep'=2,'lat'=8,'blk'=2] {'lat'}, dimensions={0} | all-to-all | bytes 589824 | tf_op jit(solution)/shard_map/all_to_all | solution.py:273
  85.6 23.3 %all_to_all.26.modes_ref = bf16[8,384,128]{2,1,0:T(8,128)(2,1)} all-to-all(bf16[8,384,128]{2,1,0:T(8,128)(2,1)} %bitcast.37), channel_id=1, replica_groups=mesh['rep'=2,'lat'=8,'blk'=2] {'lat'}, dimensions={0} | all-to-all | bytes 1572864 | tf_op jit(solution)/shard_map/all_to_all | solution.py:273
  108.8 4.2 %all-to-all-start.1 = ((bf16[8,384,128]{2,1,0:T(8,128)(2,1)}), bf16[8,384,128]{2,1,0:T(8,128)(2,1)}, u32[]{:S(2)}, u32[]{:S(2)}) async-start(bf16[8,384,128]{2,1,0:T(8,128)(2,1)} %bitcast.36), calls=%async_computation.1 | async-start | bytes 1572864 | tf_op jit(solution)/shard_map/all_to_all | solution.py:273
  113.1 0.6 squeeze.7
  113.7 0.6 squeeze.6
  114.3 1.3 copy-done.4
  115.6 1.1 copy-done.8
  116.7 2.8 %shard_map.134 = bf16[384,1440]{1,0:T(8,128)(2,1)} custom-call(bf16[8,384,128]{2,1,0:T(8,128)(2,1)S(1)} %copy-done.8, bf16[1024,1440]{1,0:T(8,128)(2,1)S(1)} %copy-done, f32[1,1024]{1,0:T(1,128)S(1)} %copy-done.21, bf16[384,1440]{1,0:T(8,128)(2,1)S(1)} %bitcast.32), custom_call_target="tpu_custom_call" | custom-call | flops 1132462080 | bytes 5947392 | tf_op jit(solution)/shard_map/pallas_call | solution.py:98
  119.6 12.7 %all-to-all-done.1.modes_ref = bf16[8,384,128]{2,1,0:T(8,128)(2,1)} async-done(((bf16[8,384,128]{2,1,0:T(8,128)(2,1)}), bf16[8,384,128]{2,1,0:T(8,128)(2,1)}, u32[]{:S(2)}, u32[]{:S(2)}) %all-to-all-start.1) | async-done | bytes 786464 | tf_op jit(solution)/shard_map/all_to_all | solution.py:273
  132.3 1.3 copy-done.6
  133.6 3.9 %shard_map.131 = bf16[384,1440]{1,0:T(8,128)(2,1)} custom-call(bf16[8,384,128]{2,1,0:T(8,128)(2,1)} %all-to-all-done.1.modes_ref, bf16[1024,1440]{1,0:T(8,128)(2,1)S(1)} %copy-done, f32[1,1024]{1,0:T(1,128)S(1)} %copy-done.21, bf16[384,1440]{1,0:T(8,128)(2,1)S(1)} %bitcast.34), custom_call_target="tpu_custom_call" | custom-call | flops 1132462080 | bytes 5947392 | tf_op jit(solution)/shard_map/pallas_call | solution.py:98
  (39 shorter events, 0.1 us)
Async XLA Ops:
  0.6 1.8 %copy-start.1 = (bf16[1440,1024]{1,0:T(8,128)(2,1)S(1)}, bf16[1440,1024]{1,0:T(8,128)(2,1)}, u32[]{:S(2)}) copy-start(bf16[1440,1024]{1,0:T(8,128)(2,1)} %constant.22.clone.table_ref) | copy-start | bytes 8847364
  2.5 1.3 copy-start.5
  3.8 10.6 %copy-start.2 = (bf16[1440,1024]{1,0:T(8,128)(2,1)S(1)}, bf16[1440,1024]{1,0:T(8,128)(2,1)}, u32[]{:S(2)}) copy-start(bf16[1440,1024]{1,0:T(8,128)(2,1)} %constant.22.clone.table_ref) | copy-start | bytes 8847364
  6.1 0.9 copy-start.9
  7.0 7.4 %copy-start.21 = (f32[1,1024]{1,0:T(1,128)S(1)}, f32[1,1024]{1,0:T(1,128)}, u32[]{:S(2)}) copy-start(f32[1,1024]{1,0:T(1,128)} %constant.24.clone.scale_ref) | copy-start | bytes 12292
  7.0 27.7 %all-to-all-start = ((bf16[8,384,128]{2,1,0:T(8,128)(2,1)}), bf16[8,384,128]{2,1,0:T(8,128)(2,1)}, u32[]{:S(2)}, u32[]{:S(2)}) async-start(bf16[8,384,128]{2,1,0:T(8,128)(2,1)} %copy-done.9), calls=%async_computation | async-start | bytes 1572864 | tf_op jit(solution)/shard_map/all_to_all | solution.py:273
  14.4 1.3 copy-start.3
  18.0 0.9 copy-start.7
  18.9 19.3 %copy-start.24 = (f32[4,192]{1,0:T(4,128)S(1)}, f32[4,192]{1,0:T(4,128)}, u32[]{:S(2)}) copy-start(f32[4,192]{1,0:T(4,128)} %param.15) | copy-start | bytes 9220
  18.9 19.3 %copy-start.25 = (f32[4,192]{1,0:T(4,128)S(1)}, f32[4,192]{1,0:T(4,128)}, u32[]{:S(2)}) copy-start(f32[4,192]{1,0:T(4,128)} %param.13) | copy-start | bytes 9220
  18.9 20.4 %copy-start.22 = (bf16[4,96,192]{2,1,0:T(8,128)(2,1)S(1)}, bf16[4,96,192]{2,1,0:T(8,128)(2,1)}, u32[]{:S(2)}) copy-start(bf16[4,96,192]{2,1,0:T(8,128)(2,1)} %param.14) | copy-start | bytes 442372
  18.9 20.4 %copy-start.23 = (bf16[4,96,192]{2,1,0:T(8,128)(2,1)S(1)}, bf16[4,96,192]{2,1,0:T(8,128)(2,1)}, u32[]{:S(2)}) copy-start(bf16[4,96,192]{2,1,0:T(8,128)(2,1)} %param.12) | copy-start | bytes 442372
  18.9 23.3 %copy-start.16 = (bf16[512,256]{1,0:T(8,128)(2,1)S(1)}, bf16[512,256]{1,0:T(8,128)(2,1)}, u32[]{:S(2)}) copy-start(bf16[512,256]{1,0:T(8,128)(2,1)} %constant.25.clone.mixer_ref) | copy-start | bytes 786436
  34.7 23.9 %all-to-all-start.2 = ((bf16[8,384,128]{2,1,0:T(8,128)(2,1)}), bf16[8,384,128]{2,1,0:T(8,128)(2,1)S(1)}, u32[]{:S(2)}, u32[]{:S(2)}) async-start(bf16[8,384,128]{2,1,0:T(8,128)(2,1)} %copy-done.7), calls=%async_computation.2 | async-start | bytes 1572864 | tf_op jit(solution)/shard_map/all_to_all | solution.py:273
  42.2 0.9 copy-start.18
  43.1 0.9 copy-start.19
  44.0 0.9 copy-start.20
  50.4 0.9 copy-start.10
  51.2 0.9 copy-start.12
  58.6 1.1 copy-start.13
  59.7 0.9 copy-start.14
  60.6 0.9 copy-start.15
  61.5 0.9 copy-start.17
  70.4 0.9 copy-start.11
  85.6 28.8 %copy-start = (bf16[1024,1440]{1,0:T(8,128)(2,1)S(1)}, bf16[1024,1440]{1,0:T(8,128)(2,1)}, u32[]{:S(2)}) copy-start(bf16[1024,1440]{1,0:T(8,128)(2,1)} %constant.23.clone.table_ref) | copy-start | bytes 8847364
  108.8 23.4 %all-to-all-start.1 = ((bf16[8,384,128]{2,1,0:T(8,128)(2,1)}), bf16[8,384,128]{2,1,0:T(8,128)(2,1)}, u32[]{:S(2)}, u32[]{:S(2)}) async-start(bf16[8,384,128]{2,1,0:T(8,128)(2,1)} %bitcast.36), calls=%async_computation.1 | async-start | bytes 1572864 | tf_op jit(solution)/shard_map/all_to_all | solution.py:273
  114.3 1.3 copy-start.4
  115.6 1.1 copy-start.8
  132.3 1.3 copy-start.6
where the time goes:
time: 138 us; the launch traced here: 137 us
  blocking collectives  37.1 us (27%)
  waiting for transfers between devices  34.9 us (25%)
  Pallas kernels  24.8 us (18%)
  local copies, waits for them, and re-layouts  23.3 us (17%)
  starting transfers between devices  15.2 us (11%)
    all_to_all x2, blocking collectives, exchange(): lax.all_to_all(blocks, 'lat', split_axis=0, concat_axis=0, tiled=True)  37.1 us
    all_to_all x3, waiting for transfers between devices, exchange(): lax.all_to_all(blocks, 'lat', split_axis=0, concat_axis=0, tiled=True)  34.9 us
    unnamed x52, local copies, waits for them, and re-layouts  19 us
    all_to_all x3, starting transfers between devices, exchange(): lax.all_to_all(blocks, 'lat', split_axis=0, concat_axis=0, tiled=True)  15.2 us
    pallas_call x1, Pallas kernels, backward_middle(): pl.pallas_call(functools.partial(backward_kernel, normalizer), in_specs=[...  7.91 us
    pallas_call x2, Pallas kernels, inverse(): pl.pallas_call(functools.partial(inverse_kernel, scaled), grid=(pl.cdiv(c...  6.74 us
    pallas_call x1, Pallas kernels, forward_middle(): pl.pallas_call(forward_kernel, in_specs=[whole(*a.shape) for a in (modes,...  5.48 us
    pallas_call x2, Pallas kernels, zonal(): pl.pallas_call(zonal_kernel, grid=(pieces // step,), in_specs=[pl.BlockSp...  4.69 us
  transfers between devices with their start and end apart: 3, of which 3 were waited for; matrix products, arithmetic and copies ran while one was open for 4% of the time, Pallas kernels for 8%

commit v1 on v0

--- a/solution.py
+++ b/solution.py
@@ -13,7 +13,7 @@
 LANES = 128
 HALF = 64
 PACK = 16
-VMEM_BYTES = 48 * 1024 * 1024
+VMEM_BYTES = 60 * 1024 * 1024
 
 SHRINK = 0.01
 GELU_SCALE = 0.7978845608028654
@@ -55,64 +55,94 @@
     return pltpu.roll(values, HALF, axis=1) * sign
 
 
-def zonal_kernel(field_ref, table_ref, scale_ref, out_ref):
+def relative(mine, shift):
+    return jnp.bitwise_xor(mine, shift)
+
+
+def zonal_kernel(mine_ref, field_ref, table_ref, scale_ref, *rest):
+    outs, pair_ref = rest[:-1], rest[-1]
+    odd = jnp.bitwise_and(mine_ref[0], 1)
     result = (mm(field_ref[...], table_ref[...]) * scale_ref[...]).astype(BF16)
-    for piece in range(out_ref.shape[0]):
-        out_ref[piece] = result[:, piece * LANES : (piece + 1) * LANES]
-
-
-def zonal(field_rows, table, scale, pieces):
+    for piece in range(2):
+        pair_ref[piece] = result[:, piece * LANES : (piece + 1) * LANES]
+    step = pl.program_id(0)
+    for place in range(len(outs) // 2):
+
+        @pl.when(step == place)
+        def _():
+            outs[2 * place][...] = pair_ref[odd]
+            outs[2 * place + 1][...] = pair_ref[1 - odd]
+
+
+def zonal(mine, field_rows, table, scale, pieces):
     rows, col_count = field_rows.shape
-    step = 2
+    wide = 2 * LANES
+
+    def block_of(i, place):
+        return (0, jnp.bitwise_xor(lax.shift_right_logical(place[0], 1), i))
+
     return pl.pallas_call(
         zonal_kernel,
-        grid=(pieces // step,),
-        in_specs=[
-            pl.BlockSpec((rows, col_count), lambda i: (0, 0)),
-            pl.BlockSpec((col_count, step * LANES), lambda i: (0, i)),
-            pl.BlockSpec((1, step * LANES), lambda i: (0, i)),
-        ],
-        out_specs=pl.BlockSpec((step, rows, LANES), lambda i: (i, 0, 0)),
-        out_shape=jax.ShapeDtypeStruct((pieces, rows, LANES), BF16),
+        grid_spec=pltpu.PrefetchScalarGridSpec(
+            num_scalar_prefetch=1,
+            grid=(pieces // 2,),
+            in_specs=[
+                pl.BlockSpec((rows, col_count), lambda i, place: (0, 0)),
+                pl.BlockSpec((col_count, wide), block_of),
+                pl.BlockSpec((1, wide), block_of),
+            ],
+            out_specs=[pl.BlockSpec((rows, LANES), lambda i, place: (0, 0)) for _ in range(pieces)],
+            scratch_shapes=[pltpu.VMEM((2, rows, LANES), BF16)],
+        ),
+        out_shape=[jax.ShapeDtypeStruct((rows, LANES), BF16) for _ in range(pieces)],
         compiler_params=pltpu.CompilerParams(vmem_limit_bytes=VMEM_BYTES),
         cost_estimate=pl.CostEstimate(
             flops=2 * rows * col_count * pieces * LANES,
             bytes_accessed=2 * (rows * col_count + (col_count + rows) * pieces * LANES),
             transcendentals=0,
         ),
-    )(field_rows, table, scale)
-
-
-def inverse_kernel(scaled, modes_ref, table_ref, scale_ref, base_ref, out_ref):
-    pieces = modes_ref.shape[0]
+    )(mine, field_rows, table, scale)
+
+
+def inverse_kernel(scaled, pieces, *refs):
+    blocks, (table_ref, scale_ref, base_ref, out_ref, modes_ref) = refs[:pieces], refs[pieces:]
+
+    @pl.when(pl.program_id(0) == 0)
+    def _():
+        mine = lax.axis_index("lat")
+        for shift in range(pieces):
+            modes_ref[relative(mine, shift)] = blocks[shift][...]
+
     modes = jnp.concatenate([modes_ref[piece] for piece in range(pieces)], axis=1)
     if scaled:
         modes = (modes.astype(F32) * scale_ref[...]).astype(BF16)
     out_ref[...] = (base_ref[...].astype(F32) + mm(modes, table_ref[...])).astype(BF16)
 
 
-def inverse(modes, table, scale, base, scaled):
-    pieces, rows, _ = modes.shape
+def inverse(blocks, table, scale, base, scaled):
+    pieces = len(blocks)
+    rows, _ = blocks[0].shape
     kept, col_count = table.shape
     width = 512
     return pl.pallas_call(
-        functools.partial(inverse_kernel, scaled),
+        functools.partial(inverse_kernel, scaled, pieces),
         grid=(pl.cdiv(col_count, width),),
-        in_specs=[
-            pl.BlockSpec((pieces, rows, LANES), lambda i: (0, 0, 0)),
+        in_specs=[pl.BlockSpec((rows, LANES), lambda i: (0, 0)) for _ in blocks]
+        + [
             pl.BlockSpec((kept, width), lambda i: (0, i)),
             pl.BlockSpec((1, kept), lambda i: (0, 0)),
             pl.BlockSpec((rows, width), lambda i: (0, i)),
         ],
         out_specs=pl.BlockSpec((rows, width), lambda i: (0, i)),
         out_shape=jax.ShapeDtypeStruct((rows, col_count), BF16),
+        scratch_shapes=[pltpu.VMEM((pieces, rows, LANES), BF16)],
         compiler_params=pltpu.CompilerParams(vmem_limit_bytes=VMEM_BYTES),
         cost_estimate=pl.CostEstimate(
             flops=2 * rows * col_count * kept,
             bytes_accessed=2 * (2 * rows * col_count + (col_count + rows) * kept),
             transcendentals=0,
         ),
-    )(modes, table, scale, base)
+    )(*blocks, table, scale, base)
 
 
 def meridian(load, mixer, first_sign, channels, store):
@@ -138,10 +168,30 @@
     ]
 
 
-def forward_kernel(
-    modes_ref, mixer_ref, first_ref, first_bias_ref, second_ref, second_bias_ref,
-    out_ref, harm_ref, hidden_ref, slope_ref, gate_ref, shrunk_ref,
-):
+def collect(blocks, modes_ref):
+    mine = lax.axis_index("lat")
+    rows = modes_ref.shape[0] // len(blocks)
+    for shift, block in enumerate(blocks):
+        for row in range(rows):
+            channels = modes_ref.shape[1]
+            modes_ref[relative(mine, shift) * rows + row] = block[row * channels : (row + 1) * channels]
+
+
+def distribute(modes_ref, outs):
+    mine = lax.axis_index("lat")
+    rows = modes_ref.shape[0] // len(outs)
+    channels = modes_ref.shape[1]
+    for shift, out in enumerate(outs):
+        for row in range(rows):
+            out[row * channels : (row + 1) * channels] = modes_ref[relative(mine, shift) * rows + row]
+
+
+def forward_kernel(pieces, *refs):
+    blocks, refs = refs[:pieces], refs[pieces:]
+    (mixer_ref, first_ref, first_bias_ref, second_ref, second_bias_ref), refs = refs[:5], refs[5:]
+    outs, refs = refs[:pieces], refs[pieces:]
+    harm_ref, hidden_ref, slope_ref, gate_ref, modes_ref, shrunk_ref = refs
+    collect(blocks, modes_ref)
     count, channels, _ = modes_ref.shape
     groups, _, width = first_ref.shape
 
@@ -171,40 +221,48 @@
                 gate_ref[row + i, span, :] = squashed * squashed
 
     def emit(start, value):
-        out_ref[:, start : start + PACK, :] = value.astype(BF16)
+        modes_ref[:, start : start + PACK, :] = value.astype(BF16)
 
     meridian(lambda c: shrunk_ref[:, c : c + PACK, :], mixer_ref, -1.0, channels, emit)
+    distribute(modes_ref, outs)
 
 
 def whole(*shape):
     return pl.BlockSpec(shape, lambda: (0,) * len(shape))
 
 
-def forward_middle(modes, mixer, first, first_bias, second, second_bias):
-    shape = modes.shape
+def forward_middle(blocks, channels, mixer, first, first_bias, second, second_bias):
+    pieces = len(blocks)
+    shape = (pieces * blocks[0].shape[0] // channels, channels, LANES)
     size = math.prod(shape)
-    kinds = (BF16, BF16, BF16, F32, F32)
-    return pl.pallas_call(
-        forward_kernel,
-        in_specs=[whole(*a.shape) for a in (modes, mixer, first, first_bias, second, second_bias)],
-        out_specs=[whole(*shape) for _ in kinds],
-        out_shape=[jax.ShapeDtypeStruct(shape, kind) for kind in kinds],
-        scratch_shapes=[pltpu.VMEM(shape, BF16)],
+    kinds = (BF16, BF16, F32, F32)
+    operands = (*blocks, mixer, first, first_bias, second, second_bias)
+    results = pl.pallas_call(
+        functools.partial(forward_kernel, pieces),
+        in_specs=[whole(*a.shape) for a in operands],
+        out_specs=[whole(*a.shape) for a in blocks] + [whole(*shape) for _ in kinds],
+        out_shape=[jax.ShapeDtypeStruct(a.shape, BF16) for a in blocks]
+        + [jax.ShapeDtypeStruct(shape, kind) for kind in kinds],
+        scratch_shapes=[pltpu.VMEM(shape, BF16), pltpu.VMEM(shape, BF16)],
         compiler_params=pltpu.CompilerParams(vmem_limit_bytes=VMEM_BYTES),
         cost_estimate=pl.CostEstimate(
             flops=4 * size * 1024, bytes_accessed=16 * size, transcendentals=2 * size
         ),
-    )(modes, mixer, first, first_bias, second, second_bias)
+    )(*operands)
+    return results[:pieces], results[pieces:]
 
 
 def nt(former, latter):
     return lax.dot_general(former, latter, (((1,), (1,)), ((), ())), preferred_element_type=F32)
 
 
-def backward_kernel(
-    normalizer, modes_ref, mixer_ref, first_ref, second_ref, harm_ref, hidden_ref, slope_ref, gate_ref,
-    out_ref, grad_ref, adjoint_ref, back_ref,
-):
+def backward_kernel(normalizer, pieces, *refs):
+    blocks, refs = refs[:pieces], refs[pieces:]
+    mixer_ref, first_ref, second_ref, harm_ref, hidden_ref, slope_ref, gate_ref = refs[:7]
+    outs, grad_ref = refs[7 : 7 + pieces], refs[7 + pieces]
+    modes_ref, adjoint_ref, back_ref = refs[8 + pieces :]
+    collect(blocks, modes_ref)
+    mine = lax.axis_index("lat")
     count, channels, _ = modes_ref.shape
     groups, _, width = first_ref.shape
 
@@ -237,32 +295,41 @@
             back = complex_dot(first_ref[group], first_adjoint, 1.0)
             for i in range(2):
                 back_ref[row + i, span, :] = back[i].astype(BF16)
-        grad_ref[0, group] = first_sum * normalizer
-        grad_ref[1, group] = second_sum * normalizer
+        part = width // pieces
+        for kind, total in enumerate((first_sum * normalizer, second_sum * normalizer)):
+            begin = (kind * groups + group) * part
+            for piece in range(pieces):
+                grad_ref[relative(mine, piece), begin : begin + part, :] = total[
+                    piece * part : (piece + 1) * part
+                ]
 
     def emit(start, value):
-        out_ref[:, start : start + PACK, :] = value.astype(BF16)
+        modes_ref[:, start : start + PACK, :] = value.astype(BF16)
 
     meridian(lambda c: back_ref[:, c : c + PACK, :], mixer_ref, -1.0, channels, emit)
-
-
-def backward_middle(modes, mixer, first, second, harm, hidden, slope, gate, normalizer):
-    shape = modes.shape
+    distribute(modes_ref, outs)
+
+
+def backward_middle(blocks, channels, mixer, first, second, saved, normalizer):
+    pieces = len(blocks)
+    shape = (pieces * blocks[0].shape[0] // channels, channels, LANES)
     size = math.prod(shape)
     groups, twice, width = first.shape
-    operands = (modes, mixer, first, second, harm, hidden, slope, gate)
-    grad_shape = (2, groups, width, twice)
-    return pl.pallas_call(
-        functools.partial(backward_kernel, normalizer),
+    operands = (*blocks, mixer, first, second, *saved)
+    grad_shape = (pieces, 2 * groups * width // pieces, twice)
+    results = pl.pallas_call(
+        functools.partial(backward_kernel, normalizer, pieces),
         in_specs=[whole(*a.shape) for a in operands],
-        out_specs=[whole(*shape), whole(*grad_shape)],
-        out_shape=[jax.ShapeDtypeStruct(shape, BF16), jax.ShapeDtypeStruct(grad_shape, F32)],
-        scratch_shapes=[pltpu.VMEM(shape, F32), pltpu.VMEM(shape, BF16)],
+        out_specs=[whole(*a.shape) for a in blocks] + [whole(*grad_shape)],
+        out_shape=[jax.ShapeDtypeStruct(a.shape, BF16) for a in blocks]
+        + [jax.ShapeDtypeStruct(grad_shape, F32)],
+        scratch_shapes=[pltpu.VMEM(shape, BF16), pltpu.VMEM(shape, F32), pltpu.VMEM(shape, BF16)],
         compiler_params=pltpu.CompilerParams(vmem_limit_bytes=VMEM_BYTES),
         cost_estimate=pl.CostEstimate(
             flops=4 * size * 1024, bytes_accessed=16 * size, transcendentals=0
         ),
     )(*operands)
+    return results[:pieces], results[pieces]
 
 
 def local_groups_of(array, groups):
@@ -271,6 +338,31 @@
 
 def exchange(blocks):
     return lax.all_to_all(blocks, "lat", split_axis=0, concat_axis=0, tiled=True)
+
+
+def pass_to(block, shift):
+    count = lax.axis_size("lat")
+    return lax.ppermute(block, "lat", [(place, place ^ shift) for place in range(count)])
+
+
+ORDER = (4, 5, 6, 7, 2, 3, 1)
+
+
+def swap_blocks(blocks):
+    result = list(blocks)
+    for shift in sorted(range(1, len(blocks)), key=lambda s: ORDER.index(s) if s in ORDER else s):
+        result[shift] = pass_to(blocks[shift], shift)
+    return result
+
+
+def halve_gradients(grads):
+    count = grads.shape[0]
+    bit = 1
+    while bit < count:
+        pairs = grads.reshape(-1, 2, *grads.shape[1:])
+        grads = pairs[:, 0] + pass_to(pairs[:, 1], bit)
+        bit *= 2
+    return grads[0]
 
 
 def reduce_gradients(grads, lat_count):
@@ -310,12 +402,6 @@
     def grid_of(rows):
         return rows.reshape(local_rows, channels, col_count).transpose(0, 2, 1)
 
-    def spread(blocks):
-        return exchange(blocks).reshape(row_count, channels, LANES)
-
-    def gather(modes):
-        return exchange(modes.reshape(lat_count, local_rows * channels, LANES))
-
     def bias_lanes(bias):
         parts = local_groups_of(bias, groups).reshape(groups, 2, width, 1)
         wide = jnp.broadcast_to(parts, (groups, 2, width, sub_count))
@@ -327,20 +413,21 @@
     own_first = local_groups_of(first_weight, groups)
     own_second = local_groups_of(second_weight, groups)
     field_rows, cotangent_rows = rows_of(field), rows_of(cotangent)
-    modes = spread(zonal(field_rows, ahead, ones, lat_count))
-    adjoint = spread(zonal(cotangent_rows, ahead, factor, lat_count))
-    synthesis, harm, hidden, slope, gate = forward_middle(
-        modes, mixer,
+    mine = lax.axis_index("lat").astype(jnp.int32).reshape(1)
+    modes = swap_blocks(zonal(mine, field_rows, ahead, ones, lat_count))
+    adjoint = swap_blocks(zonal(mine, cotangent_rows, ahead, factor, lat_count))
+    synthesis, saved = forward_middle(
+        modes, channels, mixer,
         own_first.transpose(0, 2, 1), bias_lanes(first_bias),
         own_second.transpose(0, 2, 1), bias_lanes(second_bias),
     )
-    mixed_modes = gather(synthesis)
+    mixed_modes = swap_blocks(synthesis)
     returned, grads = backward_middle(
-        adjoint, mixer, tall(own_first), tall(own_second), harm, hidden, slope, gate,
+        adjoint, channels, mixer, tall(own_first), tall(own_second), saved,
         1.0 / math.sqrt(row_count * KW),
     )
-    return_modes = gather(returned)
-    gradients = reduce_gradients(grads, lat_count)
+    return_modes = swap_blocks(returned)
+    gradients = halve_gradients(grads).reshape(2, groups, 2 * width * width // lat_count)
     mixed = inverse(mixed_modes, back, factor, field_rows, True)
     field_gradient = inverse(return_modes, back, factor, cotangent_rows, False)
     return (grid_of(mixed), grid_of(field_gradient), gradients[0], gradients[1])
@@ -444,6 +531,8 @@
         and local_rows * lat_count % 2 == 0
         and rest[1].shape[1] % PACK == 0
         and local_rows * lat_count * PACK <= 512
+        and lat_count & (lat_count - 1) == 0
+        and rest[1].shape[1] // 2 % lat_count == 0
     )
     return (with_kernels if fits else plain)(field, *rest)
 

time: 138 us -> 115 us (0.83)
  blocking collectives: 37.1 us -> 0 us
  starting transfers between devices: 15.2 us -> 52.3 us
  waiting for transfers between devices: 34.9 us -> 13.6 us
  local copies, waits for them, and re-layouts: 23.3 us -> 7.65 us
  Pallas kernels: 24.8 us -> 37.2 us
    ppermute x0 -> x31, starting transfers between devices: none -> 52.3 us  [pass_to(): lax.ppermute(block, 'lat', [(place, place ^ shift) for place in range(cou...]
    all_to_all x2 -> x0, blocking collectives: 37.1 us -> none  [exchange(): lax.all_to_all(blocks, 'lat', split_axis=0, concat_axis=0, tiled=True)]
    all_to_all x3 -> x0, waiting for transfers between devices: 34.9 us -> none  [exchange(): lax.all_to_all(blocks, 'lat', split_axis=0, concat_axis=0, tiled=True)]
    unnamed x52 -> x82, local copies, waits for them, and re-layouts: 19 us -> 1.47 us
    all_to_all x3 -> x0, starting transfers between devices: 15.2 us -> none  [exchange(): lax.all_to_all(blocks, 'lat', split_axis=0, concat_axis=0, tiled=True)]
    ppermute x0 -> x31, waiting for transfers between devices: none -> 13.6 us  [pass_to(): lax.ppermute(block, 'lat', [(place, place ^ shift) for place in range(cou...]
    pallas_call x6, Pallas kernels: 24.8 us -> 37.2 us  [the longest x2 10.5 us: zonal(): pl.pallas_call(zonal_kernel, grid_spec=pltpu.PrefetchScalarGridSpec(num_s...]
  transfers between devices with their start and end apart: 3 -> 31, of which waited for: 3 -> 4; matrix products, arithmetic and copies ran while one was open for 4% -> 5% of each run, Pallas kernels for 8% -> 19%
where the time goes in v1:
time: 115 us; the launch traced here: 114 us
  starting transfers between devices  52.3 us (45%)
  Pallas kernels  37.2 us (32%)
  waiting for transfers between devices  13.6 us (12%)
  local copies, waits for them, and re-layouts  7.65 us (7%)
  other arithmetic  2.3 us (2%)
    ppermute x31, starting transfers between devices, pass_to(): lax.ppermute(block, 'lat', [(place, place ^ shift) for place in range(cou...  52.3 us
    ppermute x31, waiting for transfers between devices, pass_to(): lax.ppermute(block, 'lat', [(place, place ^ shift) for place in range(cou...  13.6 us
    pallas_call x2, Pallas kernels, zonal(): pl.pallas_call(zonal_kernel, grid_spec=pltpu.PrefetchScalarGridSpec(num_s...  10.5 us
    pallas_call x1, Pallas kernels, backward_middle(): pl.pallas_call(functools.partial(backward_kernel, normalizer, pieces), in...  10.5 us
    pallas_call x2, Pallas kernels, inverse(): pl.pallas_call(functools.partial(inverse_kernel, scaled, pieces), grid=(p...  10.1 us
    pallas_call x1, Pallas kernels, forward_middle(): pl.pallas_call(functools.partial(forward_kernel, pieces), in_specs=[whole...  6.14 us
  transfers between devices with their start and end apart: 31, of which 4 were waited for; matrix products, arithmetic and copies ran while one was open for 5% of the time, Pallas kernels for 19%

profile of v1, /device:TPU:0, one launch (start us, length us, event | category | flops | bytes accessed | tf_op | source)
XLA Modules:
  0.0 114.1 jit_solution(5519944362651929273)
XLA Ops:
  0.6 0.6 broadcast_in_dim.17.scale_ref
  1.2 5.2 %shard_map.129 = (bf16[384,128]{1,0:T(8,128)(2,1)}, bf16[384,128]{1,0:T(8,128)(2,1)}, bf16[384,128]{1,0:T(8,128)(2,1)}, bf16[384,128]{1,0:T(8,128)(2,1)}, bf16[3...) custom-call(s32[1]{0:T(128)} %bitcast.mine_ref, ...), custom_call_target="tpu_custom_call" | custom-call | flops 1132462080 | bytes 4841472 | tf_op jit(solution)/shard_map/pallas_call | solution.py:84
  6.5 2.9 %collective-permute-start = (bf16[384,128]{1,0:T(8,128)(2,1)}, bf16[384,128]{1,0:T(8,128)(2,1)S(1)}, u32[]{:S(2)}, u32[]{:S(2)}) collective-permute-start(bf16[384,128]{1,0:T(8,128)(2,1)} %get-tuple-element.42), channel_id=1, source_target_pairs={{0,2},{2,0},{4,6},{6,4},{8,10},{10,8},{12,14},{14,12},{1,3},{3,1},... | collective-permute-start | bytes 294920 | tf_op jit(solution)/shard_map/ppermute | solution.py:345
  9.4 1.6 %collective-permute-start.1 = (bf16[384,128]{1,0:T(8,128)(2,1)}, bf16[384,128]{1,0:T(8,128)(2,1)S(1)}, u32[]{:S(2)}, u32[]{:S(2)}) collective-permute-start(bf16[384,128]{1,0:T(8,128)(2,1)} %get-tuple-element.43), channel_id=1, source_target_pairs={{0,4},{2,6},{4,0},{6,2},{8,12},{10,14},{12,8},{14,10},{1,5},{3,7},... | collective-permute-start | bytes 294920 | tf_op jit(solution)/shard_map/ppermute | solution.py:345
  11.0 3.0 %collective-permute-start.3 = (bf16[384,128]{1,0:T(8,128)(2,1)}, bf16[384,128]{1,0:T(8,128)(2,1)S(1)}, u32[]{:S(2)}, u32[]{:S(2)}) collective-permute-start(bf16[384,128]{1,0:T(8,128)(2,1)} %get-tuple-element.45), channel_id=1, source_target_pairs={{0,8},{2,10},{4,12},{6,14},{8,0},{10,2},{12,4},{14,6},{1,9},{3,11}... | collective-permute-start | bytes 294920 | tf_op jit(solution)/shard_map/ppermute | solution.py:345
  14.0 1.3 %collective-permute-start.4 = (bf16[384,128]{1,0:T(8,128)(2,1)}, bf16[384,128]{1,0:T(8,128)(2,1)S(1)}, u32[]{:S(2)}, u32[]{:S(2)}) collective-permute-start(bf16[384,128]{1,0:T(8,128)(2,1)} %get-tuple-element.46), channel_id=1, source_target_pairs={{0,10},{2,8},{4,14},{6,12},{8,2},{10,0},{12,6},{14,4},{1,11},{3,9}... | collective-permute-start | bytes 294920 | tf_op jit(solution)/shard_map/ppermute | solution.py:345
  15.5 0.7 copy.20.refs_10_
  16.2 0.7 copy.22.refs_12_
  16.9 0.1 constant_dynamic-slice_fusion.1
  17.1 0.7 copy.21.refs_11_
  17.8 0.7 copy.19.refs_9_
  18.5 0.7 pad_maximum_fusion.1.refs_10_
  19.2 5.3 %shard_map.132 = (bf16[384,128]{1,0:T(8,128)(2,1)}, bf16[384,128]{1,0:T(8,128)(2,1)}, bf16[384,128]{1,0:T(8,128)(2,1)}, bf16[384,128]{1,0:T(8,128)(2,1)}, bf16[3...) custom-call(s32[1]{0:T(128)} %bitcast.mine_ref, ...), custom_call_target="tpu_custom_call" | custom-call | flops 1132462080 | bytes 4841472 | tf_op jit(solution)/shard_map/pallas_call | solution.py:84
  24.5 3.7 %collective-permute-start.5 = (bf16[384,128]{1,0:T(8,128)(2,1)S(1)}, bf16[384,128]{1,0:T(8,128)(2,1)S(1)}, u32[]{:S(2)}, u32[]{:S(2)}) collective-permute-start(bf16[384,128]{1,0:T(8,128)(2,1)S(1)} %copy-done.38), channel_id=1, source_target_pairs={{0,12},{2,14},{4,8},{6,10},{8,4},{10,6},{12,0},{14,2},{1,13},{3,15... | collective-permute-start | bytes 294920 | tf_op jit(solution)/shard_map/ppermute | solution.py:345
  28.2 1.7 %collective-permute-start.14 = (bf16[384,128]{1,0:T(8,128)(2,1)}, bf16[384,128]{1,0:T(8,128)(2,1)S(1)}, u32[]{:S(2)}, u32[]{:S(2)}) collective-permute-start(bf16[384,128]{1,0:T(8,128)(2,1)} %get-tuple-element.58), channel_id=1, source_target_pairs={{0,2},{2,0},{4,6},{6,4},{8,10},{10,8},{12,14},{14,12},{1,3},{3,1},... | collective-permute-start | bytes 294920 | tf_op jit(solution)/shard_map/ppermute | solution.py:345
  29.9 0.7 pad_maximum_fusion.refs_9_
  30.6 1.9 %collective-permute-start.16 = (bf16[384,128]{1,0:T(8,128)(2,1)}, bf16[384,128]{1,0:T(8,128)(2,1)S(1)}, u32[]{:S(2)}, u32[]{:S(2)}) collective-permute-start(bf16[384,128]{1,0:T(8,128)(2,1)} %get-tuple-element.60), channel_id=1, source_target_pairs={{0,6},{2,4},{4,2},{6,0},{8,14},{10,12},{12,10},{14,8},{1,7},{3,5},... | collective-permute-start | bytes 294920 | tf_op jit(solution)/shard_map/ppermute | solution.py:345
  32.5 2.4 %collective-permute-start.17 = (bf16[384,128]{1,0:T(8,128)(2,1)}, bf16[384,128]{1,0:T(8,128)(2,1)S(1)}, u32[]{:S(2)}, u32[]{:S(2)}) collective-permute-start(bf16[384,128]{1,0:T(8,128)(2,1)} %get-tuple-element.61), channel_id=1, source_target_pairs={{0,8},{2,10},{4,12},{6,14},{8,0},{10,2},{12,4},{14,6},{1,9},{3,11}... | collective-permute-start | bytes 294920 | tf_op jit(solution)/shard_map/ppermute | solution.py:345
  34.8 1.1 collective-permute-done.6.refs_7_
  36.0 2.3 %collective-permute-start.18 = (bf16[384,128]{1,0:T(8,128)(2,1)}, bf16[384,128]{1,0:T(8,128)(2,1)S(1)}, u32[]{:S(2)}, u32[]{:S(2)}) collective-permute-start(bf16[384,128]{1,0:T(8,128)(2,1)} %get-tuple-element.62), channel_id=1, source_target_pairs={{0,10},{2,8},{4,14},{6,12},{8,2},{10,0},{12,6},{14,4},{1,11},{3,9}... | collective-permute-start | bytes 294920 | tf_op jit(solution)/shard_map/ppermute | solution.py:345
  38.2 1.8 %collective-permute-start.19 = (bf16[384,128]{1,0:T(8,128)(2,1)}, bf16[384,128]{1,0:T(8,128)(2,1)S(1)}, u32[]{:S(2)}, u32[]{:S(2)}) collective-permute-start(bf16[384,128]{1,0:T(8,128)(2,1)} %get-tuple-element.63), channel_id=1, source_target_pairs={{0,12},{2,14},{4,8},{6,10},{8,4},{10,6},{12,0},{14,2},{1,13},{3,15... | collective-permute-start | bytes 294920 | tf_op jit(solution)/shard_map/ppermute | solution.py:345
  40.0 1.7 %collective-permute-start.20 = (bf16[384,128]{1,0:T(8,128)(2,1)}, bf16[384,128]{1,0:T(8,128)(2,1)S(1)}, u32[]{:S(2)}, u32[]{:S(2)}) collective-permute-start(bf16[384,128]{1,0:T(8,128)(2,1)} %get-tuple-element.64), channel_id=1, source_target_pairs={{0,14},{2,12},{4,10},{6,8},{8,6},{10,4},{12,2},{14,0},{1,15},{3,13... | collective-permute-start | bytes 294920 | tf_op jit(solution)/shard_map/ppermute | solution.py:345
  41.8 6.1 %shard_map.130 = (bf16[384,128]{1,0:T(8,128)(2,1)}, bf16[384,128]{1,0:T(8,128)(2,1)}, bf16[384,128]{1,0:T(8,128)(2,1)}, bf16[384,128]{1,0:T(8,128)(2,1)}, bf16[3...) custom-call(bf16[384,128]{1,0:T(8,128)(2,1)} %get-tuple-element.41.r, ...), custom_call_target="tpu_custom_call" | custom-call | flops 1610612736 | bytes 6291456 | tf_op jit(solution)/shard_map/pallas_call | solution.py:240
  48.0 2.3 %collective-permute-done.18.refs_5_ = bf16[384,128]{1,0:T(8,128)(2,1)S(1)} collective-permute-done((bf16[384,128]{1,0:T(8,128)(2,1)}, bf16[384,128]{1,0:T(8,128)(2,1)S(1)}, u32[]{:S(2)}, u32[]{:S(2)}) %collective-permute-start.18) | collective-permute-done | bytes 98336 | tf_op jit(solution)/shard_map/ppermute | solution.py:345
  50.4 0.6 copy-done.10
  51.1 10.5 %shard_map.133 = (bf16[384,128]{1,0:T(8,128)(2,1)}, bf16[384,128]{1,0:T(8,128)(2,1)}, bf16[384,128]{1,0:T(8,128)(2,1)}, bf16[384,128]{1,0:T(8,128)(2,1)}, bf16[3...) custom-call(bf16[384,128]{1,0:T(8,128)(2,1)} %get-tuple-element.57.r, ...), custom_call_target="tpu_custom_call" | custom-call | flops 1610612736 | bytes 6291456 | tf_op jit(solution)/shard_map/pallas_call | solution.py:320
  61.6 0.9 slice_bitcast_fusion
  62.5 0.4 collective-permute-start.28
  62.9 1.7 %collective-permute-start.21 = (bf16[384,128]{1,0:T(8,128)(2,1)}, bf16[384,128]{1,0:T(8,128)(2,1)S(1)}, u32[]{:S(2)}, u32[]{:S(2)}) collective-permute-start(bf16[384,128]{1,0:T(8,128)(2,1)} %get-tuple-element.70), channel_id=1, source_target_pairs={{0,2},{2,0},{4,6},{6,4},{8,10},{10,8},{12,14},{14,12},{1,3},{3,1},... | collective-permute-start | bytes 294920 | tf_op jit(solution)/shard_map/ppermute | solution.py:345
  64.6 3.2 %collective-permute-start.22 = (bf16[384,128]{1,0:T(8,128)(2,1)}, bf16[384,128]{1,0:T(8,128)(2,1)S(1)}, u32[]{:S(2)}, u32[]{:S(2)}) collective-permute-start(bf16[384,128]{1,0:T(8,128)(2,1)} %get-tuple-element.71), channel_id=1, source_target_pairs={{0,4},{2,6},{4,0},{6,2},{8,12},{10,14},{12,8},{14,10},{1,5},{3,7},... | collective-permute-start | bytes 294920 | tf_op jit(solution)/shard_map/ppermute | solution.py:345
  67.8 2.7 %collective-permute-start.24 = (bf16[384,128]{1,0:T(8,128)(2,1)}, bf16[384,128]{1,0:T(8,128)(2,1)S(1)}, u32[]{:S(2)}, u32[]{:S(2)}) collective-permute-start(bf16[384,128]{1,0:T(8,128)(2,1)} %get-tuple-element.73), channel_id=1, source_target_pairs={{0,8},{2,10},{4,12},{6,14},{8,0},{10,2},{12,4},{14,6},{1,9},{3,11}... | collective-permute-start | bytes 294920 | tf_op jit(solution)/shard_map/ppermute | solution.py:345
  70.5 3.2 %collective-permute-start.25 = (bf16[384,128]{1,0:T(8,128)(2,1)}, bf16[384,128]{1,0:T(8,128)(2,1)S(1)}, u32[]{:S(2)}, u32[]{:S(2)}) collective-permute-start(bf16[384,128]{1,0:T(8,128)(2,1)} %get-tuple-element.74), channel_id=1, source_target_pairs={{0,10},{2,8},{4,14},{6,12},{8,2},{10,0},{12,6},{14,4},{1,11},{3,9}... | collective-permute-start | bytes 294920 | tf_op jit(solution)/shard_map/ppermute | solution.py:345
  73.8 1.0 fusion
  74.7 1.8 %collective-permute-start.26 = (bf16[384,128]{1,0:T(8,128)(2,1)}, bf16[384,128]{1,0:T(8,128)(2,1)S(1)}, u32[]{:S(2)}, u32[]{:S(2)}) collective-permute-start(bf16[384,128]{1,0:T(8,128)(2,1)} %get-tuple-element.75), channel_id=1, source_target_pairs={{0,12},{2,14},{4,8},{6,10},{8,4},{10,6},{12,0},{14,2},{1,13},{3,15... | collective-permute-start | bytes 294920 | tf_op jit(solution)/shard_map/ppermute | solution.py:345
  76.6 2.1 %collective-permute-start.27 = (bf16[384,128]{1,0:T(8,128)(2,1)}, bf16[384,128]{1,0:T(8,128)(2,1)S(1)}, u32[]{:S(2)}, u32[]{:S(2)}) collective-permute-start(bf16[384,128]{1,0:T(8,128)(2,1)} %get-tuple-element.76), channel_id=1, source_target_pairs={{0,14},{2,12},{4,10},{6,8},{8,6},{10,4},{12,2},{14,0},{1,15},{3,13... | collective-permute-start | bytes 294920 | tf_op jit(solution)/shard_map/ppermute | solution.py:345
  78.7 1.5 %collective-permute-start.7 = (bf16[384,128]{1,0:T(8,128)(2,1)S(1)}, bf16[384,128]{1,0:T(8,128)(2,1)S(1)}, u32[]{:S(2)}, u32[]{:S(2)}) collective-permute-start(bf16[384,128]{1,0:T(8,128)(2,1)S(1)} %copy-done.31), channel_id=1, source_target_pairs={{0,2},{2,0},{4,6},{6,4},{8,10},{10,8},{12,14},{14,12},{1,3},{3,1},... | collective-permute-start | bytes 294920 | tf_op jit(solution)/shard_map/ppermute | solution.py:345
  80.3 4.5 %collective-permute-done.25.refs_5_ = bf16[384,128]{1,0:T(8,128)(2,1)S(1)} collective-permute-done((bf16[384,128]{1,0:T(8,128)(2,1)}, bf16[384,128]{1,0:T(8,128)(2,1)S(1)}, u32[]{:S(2)}, u32[]{:S(2)}) %collective-permute-start.25) | collective-permute-done | bytes 98336 | tf_op jit(solution)/shard_map/ppermute | solution.py:345
  84.8 3.3 %collective-permute-start.10 = (bf16[384,128]{1,0:T(8,128)(2,1)S(1)}, bf16[384,128]{1,0:T(8,128)(2,1)S(1)}, u32[]{:S(2)}, u32[]{:S(2)}) collective-permute-start(bf16[384,128]{1,0:T(8,128)(2,1)S(1)} %copy-done.28), channel_id=1, source_target_pairs={{0,8},{2,10},{4,12},{6,14},{8,0},{10,2},{12,4},{14,6},{1,9},{3,11}... | collective-permute-start | bytes 294920 | tf_op jit(solution)/shard_map/ppermute | solution.py:345
  88.1 1.8 %collective-permute-start.29 = (f32[2,48,192]{2,1,0:T(8,128)S(1)}, f32[2,48,192]{2,1,0:T(8,128)S(1)}, u32[]{:S(2)}, u32[]{:S(2)}) collective-permute-start(f32[2,48,192]{2,1,0:T(8,128)S(1)} %slice_bitcast_fusion.2), channel_id=1, source_target_pairs={{0,4},{2,6},{4,0},{6,2},{8,12},{10,14},{12,8},{14,10},{1,5},{3,7},... | collective-permute-start | bytes 221192 | tf_op jit(solution)/shard_map/ppermute | solution.py:345
  89.9 5.1 %shard_map.134 = bf16[384,1440]{1,0:T(8,128)(2,1)} custom-call(bf16[384,128]{1,0:T(8,128)(2,1)} %get-tuple-element.69.refs_0_, bf16[384,128]{1,0:T(8,128)(2,1)} %copy-done.9, bf16[384,128]{1,0:T(8,128)(2,1)} %copy-done.11, bf16[384,128]{1,0:T(8,128)(2,1)} %copy-done.13, bf16[384,128]{1,0:T(8,128)(2,1)} %copy-done.15, bf16[384,128]{1,0:T(8,128)(2,1)} %copy-done.17, ...), custom_call_target="tpu_custom_call" | custom-call | flops 1132462080 | bytes 5947392 | tf_op jit(solution)/shard_map/pallas_call | solution.py:127
  95.1 1.6 %collective-permute-start.11 = (bf16[384,128]{1,0:T(8,128)(2,1)S(1)}, bf16[384,128]{1,0:T(8,128)(2,1)S(1)}, u32[]{:S(2)}, u32[]{:S(2)}) collective-permute-start(bf16[384,128]{1,0:T(8,128)(2,1)S(1)} %copy-done.27), channel_id=1, source_target_pairs={{0,10},{2,8},{4,14},{6,12},{8,2},{10,0},{12,6},{14,4},{1,11},{3,9}... | collective-permute-start | bytes 294920 | tf_op jit(solution)/shard_map/ppermute | solution.py:345
  96.7 1.7 %collective-permute-start.12 = (bf16[384,128]{1,0:T(8,128)(2,1)S(1)}, bf16[384,128]{1,0:T(8,128)(2,1)S(1)}, u32[]{:S(2)}, u32[]{:S(2)}) collective-permute-start(bf16[384,128]{1,0:T(8,128)(2,1)S(1)} %copy-done.26), channel_id=1, source_target_pairs={{0,12},{2,14},{4,8},{6,10},{8,4},{10,6},{12,0},{14,2},{1,13},{3,15... | collective-permute-start | bytes 294920 | tf_op jit(solution)/shard_map/ppermute | solution.py:345
  98.4 2.8 %collective-permute-start.13 = (bf16[384,128]{1,0:T(8,128)(2,1)S(1)}, bf16[384,128]{1,0:T(8,128)(2,1)S(1)}, u32[]{:S(2)}, u32[]{:S(2)}) collective-permute-start(bf16[384,128]{1,0:T(8,128)(2,1)S(1)} %copy-done.25), channel_id=1, source_target_pairs={{0,14},{2,12},{4,10},{6,8},{8,6},{10,4},{12,2},{14,0},{1,15},{3,13... | collective-permute-start | bytes 294920 | tf_op jit(solution)/shard_map/ppermute | solution.py:345
  101.4 5.6 %collective-permute-done.11.refs_5_ = bf16[384,128]{1,0:T(8,128)(2,1)S(1)} collective-permute-done((bf16[384,128]{1,0:T(8,128)(2,1)S(1)}, bf16[384,128]{1,0:T(8,128)(2,1)S(1)}, u32[]{:S(2)}, u32[]{:S(2)}) %collective-permute-start.11) | collective-permute-done | bytes 98336 | tf_op jit(solution)/shard_map/ppermute | solution.py:345
  107.1 0.6 copy-done.19
  107.7 5.0 %shard_map.131 = bf16[384,1440]{1,0:T(8,128)(2,1)} custom-call(bf16[384,128]{1,0:T(8,128)(2,1)} %get-tuple-element.49.refs_0_, bf16[384,128]{1,0:T(8,128)(2,1)} %copy-done.4, bf16[384,128]{1,0:T(8,128)(2,1)} %copy-done.6, bf16[384,128]{1,0:T(8,128)(2,1)} %copy-done.8, bf16[384,128]{1,0:T(8,128)(2,1)} %copy-done.12, bf16[384,128]{1,0:T(8,128)(2,1)} %copy-done.19, ...), custom_call_target="tpu_custom_call" | custom-call | flops 1132462080 | bytes 5947392 | tf_op jit(solution)/shard_map/pallas_call | solution.py:127
  112.8 0.7 squeeze.31
  113.5 0.7 squeeze.30
  (125 shorter events, 0.8 us)
Async XLA Ops:
  1.2 14.0 %copy-start.23 = (f32[4,192]{1,0:T(4,128)S(1)}, f32[4,192]{1,0:T(4,128)}, u32[]{:S(2)}) copy-start(f32[4,192]{1,0:T(4,128)} %param.15) | copy-start | bytes 9220
  1.2 14.0 %copy-start.24 = (f32[4,192]{1,0:T(4,128)S(1)}, f32[4,192]{1,0:T(4,128)}, u32[]{:S(2)}) copy-start(f32[4,192]{1,0:T(4,128)} %param.13) | copy-start | bytes 9220
  1.2 15.7 %copy-start = (bf16[4,96,192]{2,1,0:T(8,128)(2,1)S(1)}, bf16[4,96,192]{2,1,0:T(8,128)(2,1)}, u32[]{:S(2)}) copy-start(bf16[4,96,192]{2,1,0:T(8,128)(2,1)} %param.14) | copy-start | bytes 442372
  1.2 15.7 %copy-start.1 = (bf16[4,96,192]{2,1,0:T(8,128)(2,1)S(1)}, bf16[4,96,192]{2,1,0:T(8,128)(2,1)}, u32[]{:S(2)}) copy-start(bf16[4,96,192]{2,1,0:T(8,128)(2,1)} %param.12) | copy-start | bytes 442372
  6.5 18.0 %collective-permute-start = (bf16[384,128]{1,0:T(8,128)(2,1)}, bf16[384,128]{1,0:T(8,128)(2,1)S(1)}, u32[]{:S(2)}, u32[]{:S(2)}) collective-permute-start(bf16[384,128]{1,0:T(8,128)(2,1)} %get-tuple-element.42), channel_id=1, source_target_pairs={{0,2},{2,0},{4,6},{6,4},{8,10},{10,8},{12,14},{14,12},{1,3},{3,1},... | collective-permute-start | bytes 294920 | tf_op jit(solution)/shard_map/ppermute | solution.py:345
  9.4 18.7 %collective-permute-start.1 = (bf16[384,128]{1,0:T(8,128)(2,1)}, bf16[384,128]{1,0:T(8,128)(2,1)S(1)}, u32[]{:S(2)}, u32[]{:S(2)}) collective-permute-start(bf16[384,128]{1,0:T(8,128)(2,1)} %get-tuple-element.43), channel_id=1, source_target_pairs={{0,4},{2,6},{4,0},{6,2},{8,12},{10,14},{12,8},{14,10},{1,5},{3,7},... | collective-permute-start | bytes 294920 | tf_op jit(solution)/shard_map/ppermute | solution.py:345
  11.0 17.2 %collective-permute-start.2 = (bf16[384,128]{1,0:T(8,128)(2,1)}, bf16[384,128]{1,0:T(8,128)(2,1)S(1)}, u32[]{:S(2)}, u32[]{:S(2)}) collective-permute-start(bf16[384,128]{1,0:T(8,128)(2,1)} %get-tuple-element.44), channel_id=1, source_target_pairs={{0,6},{2,4},{4,2},{6,0},{8,14},{10,12},{12,10},{14,8},{1,7},{3,5},... | collective-permute-start | bytes 294920 | tf_op jit(solution)/shard_map/ppermute | solution.py:345
  11.0 18.9 %collective-permute-start.3 = (bf16[384,128]{1,0:T(8,128)(2,1)}, bf16[384,128]{1,0:T(8,128)(2,1)S(1)}, u32[]{:S(2)}, u32[]{:S(2)}) collective-permute-start(bf16[384,128]{1,0:T(8,128)(2,1)} %get-tuple-element.45), channel_id=1, source_target_pairs={{0,8},{2,10},{4,12},{6,14},{8,0},{10,2},{12,4},{14,6},{1,9},{3,11}... | collective-permute-start | bytes 294920 | tf_op jit(solution)/shard_map/ppermute | solution.py:345
  14.0 16.6 %collective-permute-start.4 = (bf16[384,128]{1,0:T(8,128)(2,1)}, bf16[384,128]{1,0:T(8,128)(2,1)S(1)}, u32[]{:S(2)}, u32[]{:S(2)}) collective-permute-start(bf16[384,128]{1,0:T(8,128)(2,1)} %get-tuple-element.46), channel_id=1, source_target_pairs={{0,10},{2,8},{4,14},{6,12},{8,2},{10,0},{12,6},{14,4},{1,11},{3,9}... | collective-permute-start | bytes 294920 | tf_op jit(solution)/shard_map/ppermute | solution.py:345
  24.5 17.3 %copy-start.32 = (bf16[384,128]{1,0:T(8,128)(2,1)}, bf16[384,128]{1,0:T(8,128)(2,1)S(1)}, u32[]{:S(2)}) copy-start(bf16[384,128]{1,0:T(8,128)(2,1)S(1)} %collective-permute-done.refs_1_) | copy-start | bytes 294916
  24.5 8.0 %collective-permute-start.5 = (bf16[384,128]{1,0:T(8,128)(2,1)S(1)}, bf16[384,128]{1,0:T(8,128)(2,1)S(1)}, u32[]{:S(2)}, u32[]{:S(2)}) collective-permute-start(bf16[384,128]{1,0:T(8,128)(2,1)S(1)} %copy-done.38), channel_id=1, source_target_pairs={{0,12},{2,14},{4,8},{6,10},{8,4},{10,6},{12,0},{14,2},{1,13},{3,15... | collective-permute-start | bytes 294920 | tf_op jit(solution)/shard_map/ppermute | solution.py:345
  28.1 13.6 %copy-start.33 = (bf16[384,128]{1,0:T(8,128)(2,1)}, bf16[384,128]{1,0:T(8,128)(2,1)S(1)}, u32[]{:S(2)}) copy-start(bf16[384,128]{1,0:T(8,128)(2,1)S(1)} %collective-permute-done.1.refs_2_) | copy-start | bytes 294916
  28.2 7.8 %collective-permute-start.6 = (bf16[384,128]{1,0:T(8,128)(2,1)S(1)}, bf16[384,128]{1,0:T(8,128)(2,1)S(1)}, u32[]{:S(2)}, u32[]{:S(2)}) collective-permute-start(bf16[384,128]{1,0:T(8,128)(2,1)S(1)} %copy-done.37), channel_id=1, source_target_pairs={{0,14},{2,12},{4,10},{6,8},{8,6},{10,4},{12,2},{14,0},{1,15},{3,13... | collective-permute-start | bytes 294920 | tf_op jit(solution)/shard_map/ppermute | solution.py:345
  28.2 13.5 %copy-start.34 = (bf16[384,128]{1,0:T(8,128)(2,1)}, bf16[384,128]{1,0:T(8,128)(2,1)S(1)}, u32[]{:S(2)}) copy-start(bf16[384,128]{1,0:T(8,128)(2,1)S(1)} %collective-permute-done.2.refs_3_) | copy-start | bytes 294916
  28.2 10.0 %collective-permute-start.14 = (bf16[384,128]{1,0:T(8,128)(2,1)}, bf16[384,128]{1,0:T(8,128)(2,1)S(1)}, u32[]{:S(2)}, u32[]{:S(2)}) collective-permute-start(bf16[384,128]{1,0:T(8,128)(2,1)} %get-tuple-element.58), channel_id=1, source_target_pairs={{0,2},{2,0},{4,6},{6,4},{8,10},{10,8},{12,14},{14,12},{1,3},{3,1},... | collective-permute-start | bytes 294920 | tf_op jit(solution)/shard_map/ppermute | solution.py:345
  29.9 11.9 %copy-start.35 = (bf16[384,128]{1,0:T(8,128)(2,1)}, bf16[384,128]{1,0:T(8,128)(2,1)S(1)}, u32[]{:S(2)}) copy-start(bf16[384,128]{1,0:T(8,128)(2,1)S(1)} %collective-permute-done.3.refs_4_) | copy-start | bytes 294916
  29.9 10.1 %collective-permute-start.15 = (bf16[384,128]{1,0:T(8,128)(2,1)}, bf16[384,128]{1,0:T(8,128)(2,1)S(1)}, u32[]{:S(2)}, u32[]{:S(2)}) collective-permute-start(bf16[384,128]{1,0:T(8,128)(2,1)} %get-tuple-element.59), channel_id=1, source_target_pairs={{0,4},{2,6},{4,0},{6,2},{8,12},{10,14},{12,8},{14,10},{1,5},{3,7},... | collective-permute-start | bytes 294920 | tf_op jit(solution)/shard_map/ppermute | solution.py:345
  30.6 11.2 %copy-start.36 = (bf16[384,128]{1,0:T(8,128)(2,1)}, bf16[384,128]{1,0:T(8,128)(2,1)S(1)}, u32[]{:S(2)}) copy-start(bf16[384,128]{1,0:T(8,128)(2,1)S(1)} %collective-permute-done.4.refs_5_) | copy-start | bytes 294916
  30.6 17.4 %collective-permute-start.16 = (bf16[384,128]{1,0:T(8,128)(2,1)}, bf16[384,128]{1,0:T(8,128)(2,1)S(1)}, u32[]{:S(2)}, u32[]{:S(2)}) collective-permute-start(bf16[384,128]{1,0:T(8,128)(2,1)} %get-tuple-element.60), channel_id=1, source_target_pairs={{0,6},{2,4},{4,2},{6,0},{8,14},{10,12},{12,10},{14,8},{1,7},{3,5},... | collective-permute-start | bytes 294920 | tf_op jit(solution)/shard_map/ppermute | solution.py:345
  32.5 15.5 %collective-permute-start.17 = (bf16[384,128]{1,0:T(8,128)(2,1)}, bf16[384,128]{1,0:T(8,128)(2,1)S(1)}, u32[]{:S(2)}, u32[]{:S(2)}) collective-permute-start(bf16[384,128]{1,0:T(8,128)(2,1)} %get-tuple-element.61), channel_id=1, source_target_pairs={{0,8},{2,10},{4,12},{6,14},{8,0},{10,2},{12,4},{14,6},{1,9},{3,11}... | collective-permute-start | bytes 294920 | tf_op jit(solution)/shard_map/ppermute | solution.py:345
  36.0 14.4 %collective-permute-start.18 = (bf16[384,128]{1,0:T(8,128)(2,1)}, bf16[384,128]{1,0:T(8,128)(2,1)S(1)}, u32[]{:S(2)}, u32[]{:S(2)}) collective-permute-start(bf16[384,128]{1,0:T(8,128)(2,1)} %get-tuple-element.62), channel_id=1, source_target_pairs={{0,10},{2,8},{4,14},{6,12},{8,2},{10,0},{12,6},{14,4},{1,11},{3,9}... | collective-permute-start | bytes 294920 | tf_op jit(solution)/shard_map/ppermute | solution.py:345
  38.2 12.1 %collective-permute-start.19 = (bf16[384,128]{1,0:T(8,128)(2,1)}, bf16[384,128]{1,0:T(8,128)(2,1)S(1)}, u32[]{:S(2)}, u32[]{:S(2)}) collective-permute-start(bf16[384,128]{1,0:T(8,128)(2,1)} %get-tuple-element.63), channel_id=1, source_target_pairs={{0,12},{2,14},{4,8},{6,10},{8,4},{10,6},{12,0},{14,2},{1,13},{3,15... | collective-permute-start | bytes 294920 | tf_op jit(solution)/shard_map/ppermute | solution.py:345
  40.0 10.3 %collective-permute-start.20 = (bf16[384,128]{1,0:T(8,128)(2,1)}, bf16[384,128]{1,0:T(8,128)(2,1)S(1)}, u32[]{:S(2)}, u32[]{:S(2)}) collective-permute-start(bf16[384,128]{1,0:T(8,128)(2,1)} %get-tuple-element.64), channel_id=1, source_target_pairs={{0,14},{2,12},{4,10},{6,8},{8,6},{10,4},{12,2},{14,0},{1,15},{3,13... | collective-permute-start | bytes 294920 | tf_op jit(solution)/shard_map/ppermute | solution.py:345
  51.1 27.6 %copy-start.31 = (bf16[384,128]{1,0:T(8,128)(2,1)S(1)}, bf16[384,128]{1,0:T(8,128)(2,1)}, u32[]{:S(2)}) copy-start(bf16[384,128]{1,0:T(8,128)(2,1)} %get-tuple-element.50) | copy-start | bytes 294916
  51.1 29.1 %copy-start.30 = (bf16[384,128]{1,0:T(8,128)(2,1)S(1)}, bf16[384,128]{1,0:T(8,128)(2,1)}, u32[]{:S(2)}) copy-start(bf16[384,128]{1,0:T(8,128)(2,1)} %get-tuple-element.51) | copy-start | bytes 294916
  51.1 33.7 %copy-start.29 = (bf16[384,128]{1,0:T(8,128)(2,1)S(1)}, bf16[384,128]{1,0:T(8,128)(2,1)}, u32[]{:S(2)}) copy-start(bf16[384,128]{1,0:T(8,128)(2,1)} %get-tuple-element.52) | copy-start | bytes 294916
  51.1 33.7 %copy-start.28 = (bf16[384,128]{1,0:T(8,128)(2,1)S(1)}, bf16[384,128]{1,0:T(8,128)(2,1)}, u32[]{:S(2)}) copy-start(bf16[384,128]{1,0:T(8,128)(2,1)} %get-tuple-element.53) | copy-start | bytes 294916
  62.5 8.0 %collective-permute-start.28 = (f32[4,48,192]{2,1,0:T(8,128)S(1)}, f32[4,48,192]{2,1,0:T(8,128)S(1)}, u32[]{:S(2)}, u32[]{:S(2)}) collective-permute-start(f32[4,48,192]{2,1,0:T(8,128)S(1)} %slice_bitcast_fusion), channel_id=1, source_target_pairs={{0,2},{2,0},{4,6},{6,4},{8,10},{10,8},{12,14},{14,12},{1,3},{3,1},... | collective-permute-start | bytes 442376 | tf_op jit(solution)/shard_map/ppermute | solution.py:345
  62.9 11.8 %collective-permute-start.21 = (bf16[384,128]{1,0:T(8,128)(2,1)}, bf16[384,128]{1,0:T(8,128)(2,1)S(1)}, u32[]{:S(2)}, u32[]{:S(2)}) collective-permute-start(bf16[384,128]{1,0:T(8,128)(2,1)} %get-tuple-element.70), channel_id=1, source_target_pairs={{0,2},{2,0},{4,6},{6,4},{8,10},{10,8},{12,14},{14,12},{1,3},{3,1},... | collective-permute-start | bytes 294920 | tf_op jit(solution)/shard_map/ppermute | solution.py:345
  64.6 12.0 %collective-permute-start.22 = (bf16[384,128]{1,0:T(8,128)(2,1)}, bf16[384,128]{1,0:T(8,128)(2,1)S(1)}, u32[]{:S(2)}, u32[]{:S(2)}) collective-permute-start(bf16[384,128]{1,0:T(8,128)(2,1)} %get-tuple-element.71), channel_id=1, source_target_pairs={{0,4},{2,6},{4,0},{6,2},{8,12},{10,14},{12,8},{14,10},{1,5},{3,7},... | collective-permute-start | bytes 294920 | tf_op jit(solution)/shard_map/ppermute | solution.py:345
  67.8 10.8 %collective-permute-start.23 = (bf16[384,128]{1,0:T(8,128)(2,1)}, bf16[384,128]{1,0:T(8,128)(2,1)S(1)}, u32[]{:S(2)}, u32[]{:S(2)}) collective-permute-start(bf16[384,128]{1,0:T(8,128)(2,1)} %get-tuple-element.72), channel_id=1, source_target_pairs={{0,6},{2,4},{4,2},{6,0},{8,14},{10,12},{12,10},{14,8},{1,7},{3,5},... | collective-permute-start | bytes 294920 | tf_op jit(solution)/shard_map/ppermute | solution.py:345
  67.8 12.4 %collective-permute-start.24 = (bf16[384,128]{1,0:T(8,128)(2,1)}, bf16[384,128]{1,0:T(8,128)(2,1)S(1)}, u32[]{:S(2)}, u32[]{:S(2)}) collective-permute-start(bf16[384,128]{1,0:T(8,128)(2,1)} %get-tuple-element.73), channel_id=1, source_target_pairs={{0,8},{2,10},{4,12},{6,14},{8,0},{10,2},{12,4},{14,6},{1,9},{3,11}... | collective-permute-start | bytes 294920 | tf_op jit(solution)/shard_map/ppermute | solution.py:345
  70.5 14.2 %collective-permute-start.25 = (bf16[384,128]{1,0:T(8,128)(2,1)}, bf16[384,128]{1,0:T(8,128)(2,1)S(1)}, u32[]{:S(2)}, u32[]{:S(2)}) collective-permute-start(bf16[384,128]{1,0:T(8,128)(2,1)} %get-tuple-element.74), channel_id=1, source_target_pairs={{0,10},{2,8},{4,14},{6,12},{8,2},{10,0},{12,6},{14,4},{1,11},{3,9}... | collective-permute-start | bytes 294920 | tf_op jit(solution)/shard_map/ppermute | solution.py:345
  74.7 15.2 %copy-start.9 = (bf16[384,128]{1,0:T(8,128)(2,1)}, bf16[384,128]{1,0:T(8,128)(2,1)S(1)}, u32[]{:S(2)}) copy-start(bf16[384,128]{1,0:T(8,128)(2,1)S(1)} %collective-permute-done.21.refs_1_) | copy-start | bytes 294916
  74.7 10.0 %collective-permute-start.26 = (bf16[384,128]{1,0:T(8,128)(2,1)}, bf16[384,128]{1,0:T(8,128)(2,1)S(1)}, u32[]{:S(2)}, u32[]{:S(2)}) collective-permute-start(bf16[384,128]{1,0:T(8,128)(2,1)} %get-tuple-element.75), channel_id=1, source_target_pairs={{0,12},{2,14},{4,8},{6,10},{8,4},{10,6},{12,0},{14,2},{1,13},{3,15... | collective-permute-start | bytes 294920 | tf_op jit(solution)/shard_map/ppermute | solution.py:345
  76.6 13.3 %copy-start.11 = (bf16[384,128]{1,0:T(8,128)(2,1)}, bf16[384,128]{1,0:T(8,128)(2,1)S(1)}, u32[]{:S(2)}) copy-start(bf16[384,128]{1,0:T(8,128)(2,1)S(1)} %collective-permute-done.22.refs_2_) | copy-start | bytes 294916
  76.6 11.5 %collective-permute-start.27 = (bf16[384,128]{1,0:T(8,128)(2,1)}, bf16[384,128]{1,0:T(8,128)(2,1)S(1)}, u32[]{:S(2)}, u32[]{:S(2)}) collective-permute-start(bf16[384,128]{1,0:T(8,128)(2,1)} %get-tuple-element.76), channel_id=1, source_target_pairs={{0,14},{2,12},{4,10},{6,8},{8,6},{10,4},{12,2},{14,0},{1,15},{3,13... | collective-permute-start | bytes 294920 | tf_op jit(solution)/shard_map/ppermute | solution.py:345
  78.7 11.2 %copy-start.13 = (bf16[384,128]{1,0:T(8,128)(2,1)}, bf16[384,128]{1,0:T(8,128)(2,1)S(1)}, u32[]{:S(2)}) copy-start(bf16[384,128]{1,0:T(8,128)(2,1)S(1)} %collective-permute-done.23.refs_3_) | copy-start | bytes 294916
  78.7 18.0 %collective-permute-start.7 = (bf16[384,128]{1,0:T(8,128)(2,1)S(1)}, bf16[384,128]{1,0:T(8,128)(2,1)S(1)}, u32[]{:S(2)}, u32[]{:S(2)}) collective-permute-start(bf16[384,128]{1,0:T(8,128)(2,1)S(1)} %copy-done.31), channel_id=1, source_target_pairs={{0,2},{2,0},{4,6},{6,4},{8,10},{10,8},{12,14},{14,12},{1,3},{3,1},... | collective-permute-start | bytes 294920 | tf_op jit(solution)/shard_map/ppermute | solution.py:345
  80.2 18.2 %collective-permute-start.8 = (bf16[384,128]{1,0:T(8,128)(2,1)S(1)}, bf16[384,128]{1,0:T(8,128)(2,1)S(1)}, u32[]{:S(2)}, u32[]{:S(2)}) collective-permute-start(bf16[384,128]{1,0:T(8,128)(2,1)S(1)} %copy-done.30), channel_id=1, source_target_pairs={{0,4},{2,6},{4,0},{6,2},{8,12},{10,14},{12,8},{14,10},{1,5},{3,7},... | collective-permute-start | bytes 294920 | tf_op jit(solution)/shard_map/ppermute | solution.py:345
  84.7 16.5 %collective-permute-start.9 = (bf16[384,128]{1,0:T(8,128)(2,1)S(1)}, bf16[384,128]{1,0:T(8,128)(2,1)S(1)}, u32[]{:S(2)}, u32[]{:S(2)}) collective-permute-start(bf16[384,128]{1,0:T(8,128)(2,1)S(1)} %copy-done.29), channel_id=1, source_target_pairs={{0,6},{2,4},{4,2},{6,0},{8,14},{10,12},{12,10},{14,8},{1,7},{3,5},... | collective-permute-start | bytes 294920 | tf_op jit(solution)/shard_map/ppermute | solution.py:345
  84.8 16.6 %collective-permute-start.10 = (bf16[384,128]{1,0:T(8,128)(2,1)S(1)}, bf16[384,128]{1,0:T(8,128)(2,1)S(1)}, u32[]{:S(2)}, u32[]{:S(2)}) collective-permute-start(bf16[384,128]{1,0:T(8,128)(2,1)S(1)} %copy-done.28), channel_id=1, source_target_pairs={{0,8},{2,10},{4,12},{6,14},{8,0},{10,2},{12,4},{14,6},{1,9},{3,11}... | collective-permute-start | bytes 294920 | tf_op jit(solution)/shard_map/ppermute | solution.py:345
  88.1 6.9 %collective-permute-start.29 = (f32[2,48,192]{2,1,0:T(8,128)S(1)}, f32[2,48,192]{2,1,0:T(8,128)S(1)}, u32[]{:S(2)}, u32[]{:S(2)}) collective-permute-start(f32[2,48,192]{2,1,0:T(8,128)S(1)} %slice_bitcast_fusion.2), channel_id=1, source_target_pairs={{0,4},{2,6},{4,0},{6,2},{8,12},{10,14},{12,8},{14,10},{1,5},{3,7},... | collective-permute-start | bytes 221192 | tf_op jit(solution)/shard_map/ppermute | solution.py:345
  95.1 11.9 %collective-permute-start.11 = (bf16[384,128]{1,0:T(8,128)(2,1)S(1)}, bf16[384,128]{1,0:T(8,128)(2,1)S(1)}, u32[]{:S(2)}, u32[]{:S(2)}) collective-permute-start(bf16[384,128]{1,0:T(8,128)(2,1)S(1)} %copy-done.27), channel_id=1, source_target_pairs={{0,10},{2,8},{4,14},{6,12},{8,2},{10,0},{12,6},{14,4},{1,11},{3,9}... | collective-permute-start | bytes 294920 | tf_op jit(solution)/shard_map/ppermute | solution.py:345
  96.7 10.3 %copy-start.4 = (bf16[384,128]{1,0:T(8,128)(2,1)}, bf16[384,128]{1,0:T(8,128)(2,1)S(1)}, u32[]{:S(2)}) copy-start(bf16[384,128]{1,0:T(8,128)(2,1)S(1)} %collective-permute-done.7.refs_1_) | copy-start | bytes 294916
  96.7 10.3 %collective-permute-start.12 = (bf16[384,128]{1,0:T(8,128)(2,1)S(1)}, bf16[384,128]{1,0:T(8,128)(2,1)S(1)}, u32[]{:S(2)}, u32[]{:S(2)}) collective-permute-start(bf16[384,128]{1,0:T(8,128)(2,1)S(1)} %copy-done.26), channel_id=1, source_target_pairs={{0,12},{2,14},{4,8},{6,10},{8,4},{10,6},{12,0},{14,2},{1,13},{3,15... | collective-permute-start | bytes 294920 | tf_op jit(solution)/shard_map/ppermute | solution.py:345
  98.4 8.6 %collective-permute-start.13 = (bf16[384,128]{1,0:T(8,128)(2,1)S(1)}, bf16[384,128]{1,0:T(8,128)(2,1)S(1)}, u32[]{:S(2)}, u32[]{:S(2)}) collective-permute-start(bf16[384,128]{1,0:T(8,128)(2,1)S(1)} %copy-done.25), channel_id=1, source_target_pairs={{0,14},{2,12},{4,10},{6,8},{8,6},{10,4},{12,2},{14,0},{1,15},{3,13... | collective-permute-start | bytes 294920 | tf_op jit(solution)/shard_map/ppermute | solution.py:345
  101.3 11.4 %collective-permute-start.30 = (f32[1,48,192]{2,1,0:T(8,128)S(1)}, f32[1,48,192]{2,1,0:T(8,128)S(1)}, u32[]{:S(2)}, u32[]{:S(2)}) collective-permute-start(f32[1,48,192]{2,1,0:T(8,128)S(1)} %slice_bitcast_fusion.4), channel_id=1, source_target_pairs={{0,8},{2,10},{4,12},{6,14},{8,0},{10,2},{12,4},{14,6},{1,9},{3,11}... | collective-permute-start | bytes 110600 | tf_op jit(solution)/shard_map/ppermute | solution.py:345
  (24 other events, 118.0 us)

commit v2 on v0

v2 whole, which is shorter than its diff:
```python
import functools
import math

import jax
import jax.numpy as jnp
import numpy as np
from jax import lax
from jax.experimental import pallas as pl
from jax.experimental.pallas import tpu as pltpu
from jax.sharding import PartitionSpec as P

KW = 512
LANES = 128
HALF = 64
PACK = 16
MIB = 1024 * 1024
ZONAL_MIB = 60
MIDDLE_MIB = 24
INVERSE_MIB = 24

SHRINK = 0.01
GELU_SCALE = 0.7978845608028654
GELU_CUBIC = 0.044715
F32 = jnp.float32
BF16 = jnp.bfloat16


def zonal_waves(col_count, kept):
    column = np.arange(col_count, dtype=np.int64)
    wavenumber = np.arange(kept, dtype=np.int64)
    phases = column[:, None] * wavenumber[None, :] % col_count
    angles = phases.astype(np.float32) * np.float32(2.0 * math.pi / col_count)
    scaling = np.float32(1.0 / math.sqrt(col_count))
    cosine = np.cos(angles) * scaling
    sines = np.sin(angles) * scaling
    return np.stack([cosine, -sines], axis=1).astype(BF16)


def meridian_waves(row_count):
    indices = np.arange(row_count, dtype=np.int64)
    phases = indices[:, None] * indices[None, :] % row_count
    angles = phases.astype(np.float32) * np.float32(2.0 * math.pi / row_count)
    scaling = np.float32(1.0 / math.sqrt(row_count))
    return ((np.cos(angles) * scaling).astype(BF16), (np.sin(angles) * scaling).astype(BF16))


def wave_factor(kept):
    return np.where(np.arange(kept) == 0, 1.0, 2.0).astype(np.float32)


def mm(former, latter):
    return jnp.dot(former, latter, preferred_element_type=F32)


def swap_parts(values, first_sign):
    lane = lax.broadcasted_iota(jnp.int32, (1, LANES), 1)
    sign = jnp.where(lane < HALF, first_sign, -first_sign).astype(F32)
    return pltpu.roll(values, HALF, axis=1) * sign


def slots(pieces):
    return (0, 7, 1, 6, 2, 5, 3, 4) if pieces == 8 else tuple(range(pieces))


def relative(mine, shift):
    return jnp.bitwise_xor(mine, shift)


def limits(mebibytes):
    return pltpu.CompilerParams(vmem_limit_bytes=mebibytes * MIB)


def zonal_kernel(mine_ref, field_ref, cotangent_ref, table_ref, scale_ref, *rest):
    outs, (rows_ref, pair_ref) = rest[:-2], rest[-2:]
    step = pl.program_id(0)
    lines, width, col_count = field_ref.shape
    half = lines * width

    @pl.when(step == 0)
    def _():
        rows_ref[:half] = field_ref[...].reshape(half, col_count)
        rows_ref[half:] = cotangent_ref[...].reshape(half, col_count)

    odd = jnp.bitwise_and(mine_ref[0], 1)
    result = mm(rows_ref[...], table_ref[...])
    for piece in range(2):
        lanes = slice(piece * LANES, (piece + 1) * LANES)
        pair_ref[piece, :half] = result[:half, lanes].astype(BF16)
        pair_ref[piece, half:] = (result[half:, lanes] * scale_ref[:, lanes]).astype(BF16)
    for place in range(len(outs) // 2):

        @pl.when(step == place)
        def _():
            where = slots(len(outs))
            outs[where.index(2 * place)][...] = pair_ref[odd]
            outs[where.index(2 * place + 1)][...] = pair_ref[1 - odd]


def zonal(mine, field, cotangent, table, scale, group, width, pieces):
    lines, _, col_count = field.shape
    rows = 2 * lines * width
    wide = 2 * LANES

    def block_of(i, place):
        return (0, jnp.bitwise_xor(lax.shift_right_logical(place[0], 1), i))

    own = pl.BlockSpec((lines, width, col_count), lambda i, place: (0, group, 0))
    return pl.pallas_call(
        zonal_kernel,
        grid_spec=pltpu.PrefetchScalarGridSpec(
            num_scalar_prefetch=1,
            grid=(pieces // 2,),
            in_specs=[
                own,
                own,
                pl.BlockSpec((col_count, wide), block_of),
                pl.BlockSpec((1, wide), block_of),
            ],
            out_specs=[pl.BlockSpec((rows, LANES), lambda i, place: (0, 0)) for _ in range(pieces)],
            scratch_shapes=[pltpu.VMEM((rows, col_count), BF16), pltpu.VMEM((2, rows, LANES), BF16)],
        ),
        out_shape=[jax.ShapeDtypeStruct((rows, LANES), BF16) for _ in range(pieces)],
        compiler_params=limits(ZONAL_MIB),
        cost_estimate=pl.CostEstimate(flops=4 * 10**9, bytes_accessed=4 * MIB, transcendentals=0),
    )(mine, field, cotangent, table, scale)


def inverse_kernel(pieces, given, group, *refs):
    blocks = refs[:pieces]
    table_ref, scale_ref, field_ref, cotangent_ref = refs[pieces : pieces + 4]
    before = refs[pieces + 4 : pieces + 4 + given]
    mixed_ref, gradient_ref, first_ref, second_ref, modes_ref = refs[pieces + 4 + given :]
    rows = modes_ref.shape[1]
    half = rows // 2

    @pl.when(pl.program_id(0) == 0)
    def _():
        mine = lax.axis_index("lat")
        for block, shift in zip(blocks, slots(pieces)):
            place = relative(mine, shift)
            scale = scale_ref[pl.ds(place, 1), :]
            modes_ref[place, :half] = (block[:half].astype(F32) * scale).astype(BF16)
            modes_ref[place, half:] = block[half:rows]
        total = blocks[0][rows:].astype(F32)
        for block in blocks[1:]:
            total += block[rows:].astype(F32)
        spread_gradient(total, 0, group, before[2:3], first_ref)
        spread_gradient(total, 1, group, before[3:4], second_ref)

    modes = jnp.concatenate([modes_ref[piece] for piece in range(pieces)], axis=1)
    result = mm(modes, table_ref[...])
    shape = field_ref.shape
    mixed_ref[...] = (field_ref[...].astype(F32) + result[:half].reshape(shape)).astype(BF16)
    gradient_ref[...] = (cotangent_ref[...].astype(F32) + result[half:].reshape(shape)).astype(BF16)


def spread_gradient(total, kind, group, before, out_ref):
    for member in range(group):
        out_ref[member : member + 1] = before[0][member : member + 1]
    lines = []
    for line in range(out_ref.shape[1] // (LANES + HALF)):
        lines.append(total[kind * PACK + line : kind * PACK + line + 1])
        lines.append(total[2 * PACK + line : 2 * PACK + line + 1, kind * HALF : (kind + 1) * HALF])
    out_ref[group : group + 1] = jnp.concatenate(lines, axis=1)


def pack_gradients(sums_ref, packed_ref):
    pieces = packed_ref.shape[0]
    part = (sums_ref.shape[1] - PACK) // pieces
    for piece in range(pieces):
        lines = slice(piece * part, piece * part + PACK)
        both = [sums_ref[kind, lines, :] for kind in range(2)]
        for kind in range(2):
            packed_ref[piece, kind * PACK : (kind + 1) * PACK] = both[kind][:, :LANES].astype(BF16)
        tails = jnp.concatenate([value[:, LANES:] for value in both], axis=1)
        packed_ref[piece, 2 * PACK :] = tails.astype(BF16)


def inverse(blocks, table, scale, field, cotangent, group, groups, gradient_size, before):
    pieces = len(blocks)
    kept, col_count = table.shape
    lines, channels, _ = field.shape
    width = channels // groups
    rows = 2 * lines * width
    wide = 512
    own = pl.BlockSpec((lines, width, wide), lambda i: (0, group, i))
    anywhere = pl.BlockSpec(memory_space=pl.ANY)
    gradient = pl.BlockSpec((groups, gradient_size), lambda i: (0, 0))
    return pl.pallas_call(
        functools.partial(inverse_kernel, pieces, len(before), group),
        grid=(pl.cdiv(col_count, wide),),
        in_specs=[pl.BlockSpec(block.shape, lambda i: (0, 0)) for block in blocks]
        + [
            pl.BlockSpec((kept, wide), lambda i: (0, i)),
            pl.BlockSpec(scale.shape, lambda i: (0, 0)),
            own,
            own,
        ]
        + ([anywhere, anywhere, gradient, gradient] if before else []),
        out_specs=[own, own, gradient, gradient],
        out_shape=[jax.ShapeDtypeStruct(field.shape, BF16) for _ in range(2)]
        + [jax.ShapeDtypeStruct((groups, gradient_size), F32) for _ in range(2)],
        scratch_shapes=[pltpu.VMEM((pieces, rows, LANES), BF16)],
        input_output_aliases={pieces + 4 + i: i for i in range(2)} if before else {},
        compiler_params=limits(INVERSE_MIB),
        cost_estimate=pl.CostEstimate(flops=4 * 10**9, bytes_accessed=5 * MIB, transcendentals=0),
    )(*blocks, table, scale, field, cotangent, *before)


def meridian(load, mixer, first_sign, channels, store):
    count = mixer.shape[1] // PACK
    for start in range(0, channels, 2 * PACK):
        pair = jnp.concatenate(
            [load(start + shift).reshape(count * PACK, LANES) for shift in (0, PACK)], axis=1
        )
        both = mm(mixer[...], pair)
        for index in range(2):
            half = both[:, index * LANES : (index + 1) * LANES]
            value = half[: count * PACK] + swap_parts(half[count * PACK :], first_sign)
            store(start + index * PACK, value.reshape(count, PACK, LANES))


def complex_dot(weights, operand, first_sign):
    width = weights.shape[0] // 2
    both = mm(weights, jnp.concatenate(operand, axis=1))
    return [
        both[:width, i * LANES : (i + 1) * LANES]
        + swap_parts(both[width:, i * LANES : (i + 1) * LANES], first_sign)
        for i in range(len(operand))
    ]


def nt(former, latter):
    return lax.dot_general(former, latter, (((1,), (1,)), ((), ())), preferred_element_type=F32)


def side_by_side(pieces):
    return jnp.concatenate(pieces, axis=1)


def bias_lanes(bias_ref, index):
    tall = jnp.broadcast_to(bias_ref[pl.ds(index, 1), :], (LANES, bias_ref.shape[1])).T
    width = bias_ref.shape[1] // 2
    lane = lax.broadcasted_iota(jnp.int32, (1, LANES), 1)
    return jnp.where(lane < HALF, tall[:width], tall[width:])


def stacked(weight):
    width = weight.shape[0]
    return jnp.concatenate([weight[:, :width], weight[:, width:]], axis=0)


def middle_kernel(group, groups, normalizer, pieces, *refs):
    blocks, refs = refs[:pieces], refs[pieces:]
    (mixer_ref, first_ref, first_bias_ref, second_ref, second_bias_ref), refs = refs[:5], refs[5:]
    outs, refs = refs[:pieces], refs[pieces:]
    modes_ref, adjoint_ref, harm_ref, shrunk_ref, exact_ref, sums_ref, packed_ref = refs
    mine = lax.axis_index("lat")
    index = lax.axis_index("blk") * groups + group
    count, width, _ = modes_ref.shape
    lines = count // pieces
    for block, shift in zip(blocks, slots(pieces)):
        for line in range(lines):
            row = relative(mine, shift) * lines + line
            modes_ref[row] = block[line * width : (line + 1) * width]
            adjoint_ref[row] = block[(lines + line) * width : (lines + line + 1) * width]

    first, second = first_ref[index], second_ref[index]
    first_ahead, second_ahead = first.T, second.T
    first_back, second_back = stacked(first), stacked(second)
    first_bias, second_bias = bias_lanes(first_bias_ref, index), bias_lanes(second_bias_ref, index)

    def keep(start, value):
        harm_ref[:, start : start + PACK, :] = value.astype(BF16)

    meridian(lambda c: modes_ref[:, c : c + PACK, :], mixer_ref, 1.0, width, keep)

    def keep_adjoint(start, value):
        exact_ref[:, start : start + PACK, :] = value

    meridian(lambda c: adjoint_ref[:, c : c + PACK, :], mixer_ref, 1.0, width, keep_adjoint)

    first_sum = jnp.zeros((width, 2 * width), F32)
    second_sum = jnp.zeros((width, 2 * width), F32)
    for row in range(0, count, 2):
        both = range(2)
        inputs = [harm_ref[row + i] for i in both]
        pre = complex_dot(first_ahead, inputs, -1.0)
        hidden, slope = [], []
        for i in both:
            v = pre[i] + first_bias
            square = v * v
            tangent = jnp.tanh(GELU_SCALE * (v + GELU_CUBIC * square * v))
            outer = 0.5 * (1.0 + tangent)
            inner = GELU_SCALE * (1.0 + 3.0 * GELU_CUBIC * square)
            hidden.append((v * outer).astype(BF16))
            slope.append(outer + 0.5 * v * (1.0 - tangent * tangent) * inner)
        pre = complex_dot(second_ahead, hidden, -1.0)
        exact = []
        for i in both:
            v = pre[i] + second_bias
            squashed = jnp.tanh(v * (1.0 / SHRINK))
            shrunk_ref[row + i] = (v - SHRINK * squashed).astype(BF16)
            exact.append(exact_ref[row + i] * (squashed * squashed))
        second_adjoint = [a.astype(BF16) for a in exact]
        turned = [swap_parts(a, 1.0).astype(BF16) for a in exact]
        pairs = jnp.concatenate([side_by_side(second_adjoint), side_by_side(turned)], axis=0)
        second_sum += nt(side_by_side(hidden), pairs)
        back = complex_dot(second_back, second_adjoint, 1.0)
        exact = [back[i] * slope[i] for i in both]
        first_adjoint = [a.astype(BF16) for a in exact]
        turned = [swap_parts(a, 1.0).astype(BF16) for a in exact]
        pairs = jnp.concatenate([side_by_side(first_adjoint), side_by_side(turned)], axis=0)
        first_sum += nt(side_by_side(inputs), pairs)
        back = complex_dot(first_back, first_adjoint, 1.0)
        for i in both:
            harm_ref[row + i] = back[i].astype(BF16)

    sums_ref[0, :width] = first_sum * normalizer
    sums_ref[1, :width] = second_sum * normalizer
    sums_ref[:, width:] = jnp.zeros((2, PACK, 2 * width), F32)
    pack_gradients(sums_ref, packed_ref)

    def emit(start, value):
        modes_ref[:, start : start + PACK, :] = value.astype(BF16)

    def emit_adjoint(start, value):
        adjoint_ref[:, start : start + PACK, :] = value.astype(BF16)

    meridian(lambda c: shrunk_ref[:, c : c + PACK, :], mixer_ref, -1.0, width, emit)
    meridian(lambda c: harm_ref[:, c : c + PACK, :], mixer_ref, -1.0, width, emit_adjoint)
    for out, shift in zip(outs, slots(pieces)):
        for line in range(lines):
            row = relative(mine, shift) * lines + line
            out[line * width : (line + 1) * width] = modes_ref[row]
            out[(lines + line) * width : (lines + line + 1) * width] = adjoint_ref[row]
        out[2 * lines * width :] = packed_ref[relative(mine, shift)]


def whole(*shape):
    return pl.BlockSpec(shape, lambda: (0,) * len(shape))


def middle(blocks, lines, mixer, first, first_bias, second, second_bias, group, groups, normalizer):
    pieces = len(blocks)
    width = first.shape[1]
    shape = (pieces * lines, width, LANES)
    operands = (*blocks, mixer, first, first_bias, second, second_bias)
    longer = (blocks[0].shape[0] + 3 * PACK, LANES)
    return pl.pallas_call(
        functools.partial(middle_kernel, group, groups, normalizer, pieces),
        in_specs=[whole(*a.shape) for a in operands],
        out_specs=[whole(*longer) for _ in blocks],
        out_shape=[jax.ShapeDtypeStruct(longer, BF16) for _ in blocks],
        scratch_shapes=[pltpu.VMEM(shape, BF16) for _ in range(4)]
        + [
            pltpu.VMEM(shape, F32),
            pltpu.VMEM((2, width + PACK, 2 * width), F32),
            pltpu.VMEM((pieces, 3 * PACK, LANES), BF16),
        ],
        compiler_params=limits(MIDDLE_MIB),
        cost_estimate=pl.CostEstimate(flops=7 * 10**9, bytes_accessed=4 * MIB, transcendentals=0),
    )(*operands)


def local_groups_of(array, groups):
    return lax.dynamic_slice_in_dim(array, lax.axis_index("blk") * groups, groups, axis=0)


def exchange(blocks):
    return lax.all_to_all(blocks, "lat", split_axis=0, concat_axis=0, tiled=True)


def pass_to(block, shift):
    count = lax.axis_size("lat")
    return lax.ppermute(block, "lat", [(place, place ^ shift) for place in range(count)])


def swap_blocks(blocks):
    return [pass_to(block, shift) if shift else block for block, shift in zip(blocks, slots(len(blocks)))]


def reduce_gradients(grads, lat_count):
    kinds, groups, width, twice = grads.shape
    piece = width * twice // lat_count
    split = grads.reshape(kinds * groups, lat_count, piece).transpose(1, 0, 2)
    if kinds * groups * piece % LANES == 0:
        split = split.reshape(lat_count, kinds * groups * piece // LANES, LANES)
    total = jnp.sum(exchange(split), axis=0)
    return total.reshape(kinds, groups, piece)


def with_kernels(field, cotangent, first_weight, first_bias, second_weight, second_bias):
    local_rows, col_count, channels = field.shape
    width = first_weight.shape[1]
    groups = channels // width
    lat_count = lax.axis_size("lat")
    row_count = local_rows * lat_count
    sub_count = KW // lat_count
    waves = zonal_waves(col_count, KW)
    table = (
        waves.reshape(col_count, 2, lat_count, sub_count).transpose(0, 2, 1, 3).reshape(col_count, 2 * KW)
    )
    factor = np.repeat(wave_factor(KW).reshape(lat_count, 1, sub_count), 2, axis=1)
    cosine, sines = meridian_waves(row_count)
    unit = np.eye(PACK, dtype=np.float32)
    mixer = np.concatenate(
        [np.kron(cosine.astype(np.float32), unit), np.kron(sines.astype(np.float32), unit)], axis=0
    ).astype(BF16)
    ahead, back = jnp.asarray(table), jnp.asarray(np.ascontiguousarray(table.T))
    wide_factor = jnp.asarray(factor.reshape(1, 2 * KW))
    tall_factor = jnp.asarray(factor.reshape(lat_count, 2 * sub_count))
    mixer = jnp.asarray(mixer)
    normalizer = 1.0 / math.sqrt(row_count * KW)
    mine = lax.axis_index("lat").astype(jnp.int32).reshape(1)
    field, cotangent = field.transpose(0, 2, 1), cotangent.transpose(0, 2, 1)

    arrived = [
        swap_blocks(zonal(mine, field, cotangent, ahead, wide_factor, group, width, lat_count))
        for group in range(groups)
    ]
    returned = [
        swap_blocks(
            middle(
                arrived[group], local_rows, mixer, first_weight, first_bias, second_weight, second_bias,
                group, groups, normalizer,
            )
        )
        for group in range(groups)
    ]
    results = []
    for group in range(groups):
        results = inverse(
            returned[group], back, tall_factor, field, cotangent, group, groups,
            2 * width * width // lat_count, results,
        )
    mixed, field_gradient = (result.transpose(0, 2, 1) for result in results[:2])
    return (mixed, field_gradient, results[2], results[3])


def gelu_value(values):
    tangent = jnp.tanh(GELU_SCALE * (values + GELU_CUBIC * values * values * values))
    return 0.5 * values * (1.0 + tangent)


def gelu_slope(values):
    tangent = jnp.tanh(GELU_SCALE * (values + GELU_CUBIC * values * values * values))
    inner = GELU_SCALE * (1.0 + 3.0 * GELU_CUBIC * values * values)
    return 0.5 * (1.0 + tangent) + 0.5 * values * (1.0 - tangent * tangent) * inner


def contract(pattern, former, latter):
    return jnp.einsum(pattern, former, latter, preferred_element_type=F32)


def complex_block(weights):
    width = weights.shape[1]
    real_part, imag_part = weights[:, :, :width], weights[:, :, width:]
    upper = jnp.stack([real_part, imag_part], axis=2)
    lower = jnp.stack([-imag_part, real_part], axis=2)
    return jnp.stack([upper, lower], axis=1)


def block_gradient(outer):
    real_part = outer[:, 0, :, 0, :] + outer[:, 1, :, 1, :]
    imag_part = outer[:, 0, :, 1, :] - outer[:, 1, :, 0, :]
    return jnp.concatenate([real_part, imag_part], axis=2)


def bias_layout(bias):
    groups, twice = bias.shape
    return bias.reshape(groups, 2, twice // 2).transpose(1, 0, 2)[None, :, None]


def plain(field, cotangent, first_weight, first_bias, second_weight, second_bias):
    local_rows, col_count, channels = field.shape
    width = first_weight.shape[1]
    groups = channels // width
    lat_count = lax.axis_size("lat")
    row_count = local_rows * lat_count
    ahead = jnp.asarray(zonal_waves(col_count, KW))
    factor = jnp.asarray(wave_factor(KW))
    cosine, sines = (jnp.asarray(t) for t in meridian_waves(row_count))
    forth = jnp.stack(
        [jnp.stack([cosine, sines], axis=-1), jnp.stack([-sines, cosine], axis=-1)], axis=1
    )
    first_block = complex_block(local_groups_of(first_weight, groups))
    second_block = complex_block(local_groups_of(second_weight, groups))

    def swap(array, split, concat):
        return lax.all_to_all(array, "lat", split_axis=split, concat_axis=concat, tiled=True)

    spectrum = contract("hwc,wrk->hrkc", field, ahead).astype(BF16)
    adjoint = (contract("hwc,wrk->hrkc", cotangent, ahead) * factor[:, None]).astype(BF16)
    modes, adjoint = swap(spectrum, 2, 0), swap(adjoint, 2, 0)
    block_shape = (row_count, 2, modes.shape[2], groups, width)
    inputs = contract("mphr,hrkc->mpkc", forth, modes).astype(BF16).reshape(block_shape)
    harmonic_adjoint = contract("mphr,hrkc->mpkc", forth, adjoint).reshape(block_shape)
    pre_first = contract("mrkgc,grcsd->mskgd", inputs, first_block) + bias_layout(
        local_groups_of(first_bias, groups)
    )
    hidden = gelu_value(pre_first).astype(BF16)
    pre_second = contract("mrkgc,grcsd->mskgd", hidden, second_block) + bias_layout(
        local_groups_of(second_bias, groups)
    )
    squashed = jnp.tanh(pre_second / SHRINK)
    shrunk = (pre_second - SHRINK * squashed).astype(BF16).reshape(modes.shape)
    second_adjoint = (harmonic_adjoint * (squashed * squashed)).astype(BF16)
    second_grad = block_gradient(contract("mrkgc,mskgd->grcsd", hidden, second_adjoint))
    hidden_adjoint = contract("mskgd,grcsd->mrkgc", second_adjoint, second_block)
    first_adjoint = (hidden_adjoint * gelu_slope(pre_first)).astype(BF16)
    first_grad = block_gradient(contract("mrkgc,mskgd->grcsd", inputs, first_adjoint))
    harmonics_adjoint = contract("mskgd,grcsd->mrkgc", first_adjoint, first_block).astype(BF16)
    synthesis = contract("mphr,mpkc->hrkc", forth, shrunk).astype(BF16)
    returned = contract(
        "mphr,mpkc->hrkc", forth, harmonics_adjoint.reshape(modes.shape)
    ).astype(BF16)
    mixed_modes, return_modes = swap(synthesis, 0, 2), swap(returned, 0, 2)
    gradients = reduce_gradients(
        jnp.stack([first_grad, second_grad]) * (1.0 / math.sqrt(row_count * KW)), lat_count
    )
    mixed_modes = (mixed_modes.astype(F32) * factor[:, None]).astype(BF16)
    mixed = (field.astype(F32) + contract("hrkc,wrk->hwc", mixed_modes, ahead)).astype(BF16)
    field_gradient = (
        cotangent.astype(F32) + contract("hrkc,wrk->hwc", return_modes, ahead)
    ).astype(BF16)
    return (mixed, field_gradient, gradients[0], gradients[1])


def on_device(field, *rest):
    local_rows, _, channels = field.shape
    lat_count = lax.axis_size("lat")
    fits = (
        KW == HALF * lat_count
        and channels == 2 * rest[1].shape[1]
        and local_rows * lat_count % 2 == 0
        and rest[1].shape[1] % (2 * PACK) == 0
        and local_rows * lat_count * PACK <= 512
        and lat_count & (lat_count - 1) == 0
        and rest[1].shape[1] % lat_count == 0
        and rest[1].shape[1] // lat_count <= PACK
        and 2 * rest[1].shape[1] == LANES + HALF
    )
    return (with_kernels if fits else plain)(field, *rest)


def solution(mesh):
    placed = (P(("rep", "lat"), None, "blk"), P(("rep", "lat"), None, "blk"), P(), P(), P(), P())
    return jax.shard_map(
        on_device,
        mesh=mesh,
        in_specs=placed,
        out_specs=(
            P(("rep", "lat"), None, "blk"),
            P(("rep", "lat"), None, "blk"),
            P(("rep", "blk"), "lat"),
            P(("rep", "blk"), "lat"),
        ),
        check_vma=False,
    )
```

time: 138 us -> 91 us (0.66)
  blocking collectives: 37.1 us -> 0 us
  starting transfers between devices: 15.2 us -> 43.8 us
  local copies, waits for them, and re-layouts: 23.3 us -> 0.07 us
  waiting for transfers between devices: 34.9 us -> 14.1 us
  Pallas kernels: 24.8 us -> 31.9 us
    ppermute x0 -> x28, starting transfers between devices: none -> 43.8 us  [pass_to(): lax.ppermute(block, 'lat', [(place, place ^ shift) for place in range(cou...]
    all_to_all x2 -> x0, blocking collectives: 37.1 us -> none  [exchange(): lax.all_to_all(blocks, 'lat', split_axis=0, concat_axis=0, tiled=True)]
    all_to_all x3 -> x0, waiting for transfers between devices: 34.9 us -> none  [exchange(): lax.all_to_all(blocks, 'lat', split_axis=0, concat_axis=0, tiled=True)]
    unnamed x52 -> x26, local copies, waits for them, and re-layouts: 19 us -> 0.07 us
    all_to_all x3 -> x0, starting transfers between devices: 15.2 us -> none  [exchange(): lax.all_to_all(blocks, 'lat', split_axis=0, concat_axis=0, tiled=True)]
    ppermute x0 -> x28, waiting for transfers between devices: none -> 14.1 us  [pass_to(): lax.ppermute(block, 'lat', [(place, place ^ shift) for place in range(cou...]
    pallas_call x6, Pallas kernels: 24.8 us -> 31.9 us  [the longest x2 15.3 us: middle(): pl.pallas_call(functools.partial(middle_kernel, group, groups, normalizer...]
    transpose x3 -> x0, local copies, waits for them, and re-layouts: 1.5 us -> none  [the longest x2 0.76 us: with_kernels(): own_second.transpose(0, 2, 1)]
  transfers between devices with their start and end apart: 3 -> 28, of which waited for: 3 -> 7; matrix products, arithmetic and copies ran while one was open for 4% -> 0% of each run, Pallas kernels for 8% -> 26%
where the time goes in v2:
time: 91 us; the launch traced here: 90.7 us
  starting transfers between devices  43.8 us (48%)
  Pallas kernels  31.9 us (35%)
  waiting for transfers between devices  14.1 us (15%)
    ppermute x28, starting transfers between devices, pass_to(): lax.ppermute(block, 'lat', [(place, place ^ shift) for place in range(cou...  43.8 us
    pallas_call x2, Pallas kernels, middle(): pl.pallas_call(functools.partial(middle_kernel, group, groups, normalizer...  15.3 us
    ppermute x28, waiting for transfers between devices, pass_to(): lax.ppermute(block, 'lat', [(place, place ^ shift) for place in range(cou...  14.1 us
    pallas_call x2, Pallas kernels, zonal(): pl.pallas_call(zonal_kernel, grid_spec=pltpu.PrefetchScalarGridSpec(num_s...  10.6 us
    pallas_call x2, Pallas kernels, inverse(): pl.pallas_call(functools.partial(inverse_kernel, pieces, len(before), gro...  6.05 us
  transfers between devices with their start and end apart: 28, of which 7 were waited for; matrix products, arithmetic and copies ran while one was open for 0% of the time, Pallas kernels for 26%

profile of v2, /device:TPU:0, one launch (start us, length us, event | category | flops | bytes accessed | tf_op | source)
XLA Modules:
  0.0 90.7 jit_solution(6444195178316314139)
XLA Ops:
  0.6 5.3 %shard_map.140 = (bf16[384,128]{1,0:T(8,128)(2,1)}, bf16[384,128]{1,0:T(8,128)(2,1)}, bf16[384,128]{1,0:T(8,128)(2,1)}, bf16[384,128]{1,0:T(8,128)(2,1)}, bf16[3...) custom-call(s32[1]{0:T(128)} %bitcast.mine_ref, ...), custom_call_target="tpu_custom_call" | custom-call | flops 4000000000 | bytes 4194304 | tf_op jit(solution)/shard_map/pallas_call | solution.py:108
  6.0 6.0 %collective-permute-start.14 = (bf16[384,128]{1,0:T(8,128)(2,1)}, bf16[384,128]{1,0:T(8,128)(2,1)S(1)}, u32[]{:S(2)}, u32[]{:S(2)}) collective-permute-start(bf16[384,128]{1,0:T(8,128)(2,1)} %get-tuple-element.61), channel_id=1, source_target_pairs={{0,14},{2,12},{4,10},{6,8},{8,6},{10,4},{12,2},{14,0},{1,15},{3,13... | collective-permute-start | bytes 294920 | tf_op jit(solution)/shard_map/ppermute | solution.py:376
  11.9 0.5 collective-permute-start.15
  12.5 0.1 collective-permute-start.16
  12.6 0.0 copy-start.3
  12.6 0.0 copy-start.4
  12.6 0.0 copy-start.5
  12.6 0.0 copy-start.7
  12.7 5.3 %collective-permute-start.18 = (bf16[384,128]{1,0:T(8,128)(2,1)}, bf16[384,128]{1,0:T(8,128)(2,1)S(1)}, u32[]{:S(2)}, u32[]{:S(2)}) collective-permute-start(bf16[384,128]{1,0:T(8,128)(2,1)} %get-tuple-element.65), channel_id=1, source_target_pairs={{0,10},{2,8},{4,14},{6,12},{8,2},{10,0},{12,6},{14,4},{1,11},{3,9}... | collective-permute-start | bytes 294920 | tf_op jit(solution)/shard_map/ppermute | solution.py:376
  17.9 5.2 %shard_map.138 = (bf16[384,128]{1,0:T(8,128)(2,1)}, bf16[384,128]{1,0:T(8,128)(2,1)}, bf16[384,128]{1,0:T(8,128)(2,1)}, bf16[384,128]{1,0:T(8,128)(2,1)}, bf16[3...) custom-call(s32[1]{0:T(128)} %bitcast.mine_ref, ...), custom_call_target="tpu_custom_call" | custom-call | flops 4000000000 | bytes 4194304 | tf_op jit(solution)/shard_map/pallas_call | solution.py:108
  23.2 0.1 collective-permute-start.19
  23.2 0.0 collective-permute-done.15.refs_2_
  23.3 0.6 collective-permute-start.20
  23.9 0.0 collective-permute-done.16.refs_3_
  23.9 4.6 %collective-permute-start = (bf16[384,128]{1,0:T(8,128)(2,1)}, bf16[384,128]{1,0:T(8,128)(2,1)S(1)}, u32[]{:S(2)}, u32[]{:S(2)}) collective-permute-start(bf16[384,128]{1,0:T(8,128)(2,1)} %get-tuple-element.45), channel_id=1, source_target_pairs={{0,14},{2,12},{4,10},{6,8},{8,6},{10,4},{12,2},{14,0},{1,15},{3,13... | collective-permute-start | bytes 294920 | tf_op jit(solution)/shard_map/ppermute | solution.py:376
  28.5 0.5 collective-permute-start.1
  29.1 0.1 collective-permute-start.2
  29.2 0.7 collective-permute-done.19.refs_6_
  29.9 0.0 collective-permute-start.3
  29.9 6.6 %collective-permute-done.20.refs_7_ = bf16[384,128]{1,0:T(8,128)(2,1)S(1)} collective-permute-done((bf16[384,128]{1,0:T(8,128)(2,1)S(1)}, bf16[384,128]{1,0:T(8,128)(2,1)S(1)}, u32[]{:S(2)}, u32[]{:S(2)}) %collective-permute-start.20) | collective-permute-done | bytes 98336 | tf_op jit(solution)/shard_map/ppermute | solution.py:376
  36.5 0.0 collective-permute-start.4
  36.5 3.6 %collective-permute-start.5 = (bf16[384,128]{1,0:T(8,128)(2,1)}, bf16[384,128]{1,0:T(8,128)(2,1)S(1)}, u32[]{:S(2)}, u32[]{:S(2)}) collective-permute-start(bf16[384,128]{1,0:T(8,128)(2,1)} %get-tuple-element.50), channel_id=1, source_target_pairs={{0,6},{2,4},{4,2},{6,0},{8,14},{10,12},{12,10},{14,8},{1,7},{3,5},... | collective-permute-start | bytes 294920 | tf_op jit(solution)/shard_map/ppermute | solution.py:376
  40.2 0.0 copy-start.9
  40.3 7.7 %shard_map.141 = (bf16[432,128]{1,0:T(8,128)(2,1)S(1)}, bf16[432,128]{1,0:T(8,128)(2,1)S(1)}, bf16[432,128]{1,0:T(8,128)(2,1)S(1)}, bf16[432,128]{1,0:T(8,128)(2...) custom-call(bf16[384,128]{1,0:T(8,128)(2,1)S(1)} %copy-done.10, ...), custom_call_target="tpu_custom_call" | custom-call | flops 7000000000 | bytes 4194304 | tf_op jit(solution)/shard_map/pallas_call | solution.py:350
  47.9 0.0 collective-permute-done.2.refs_3_
  47.9 2.4 %collective-permute-start.21 = (bf16[432,128]{1,0:T(8,128)(2,1)S(1)}, bf16[432,128]{1,0:T(8,128)(2,1)S(1)}, u32[]{:S(2)}, u32[]{:S(2)}) collective-permute-start(bf16[432,128]{1,0:T(8,128)(2,1)S(1)} %get-tuple-element.69), channel_id=1, source_target_pairs={{0,14},{2,12},{4,10},{6,8},{8,6},{10,4},{12,2},{14,0},{1,15},{3,13... | collective-permute-start | bytes 331784 | tf_op jit(solution)/shard_map/ppermute | solution.py:376
  50.4 2.1 %collective-permute-start.22 = (bf16[432,128]{1,0:T(8,128)(2,1)S(1)}, bf16[432,128]{1,0:T(8,128)(2,1)S(1)}, u32[]{:S(2)}, u32[]{:S(2)}) collective-permute-start(bf16[432,128]{1,0:T(8,128)(2,1)S(1)} %get-tuple-element.70), channel_id=1, source_target_pairs={{0,2},{2,0},{4,6},{6,4},{8,10},{10,8},{12,14},{14,12},{1,3},{3,1},... | collective-permute-start | bytes 331784 | tf_op jit(solution)/shard_map/ppermute | solution.py:376
  52.5 1.0 %collective-permute-start.23 = (bf16[432,128]{1,0:T(8,128)(2,1)S(1)}, bf16[432,128]{1,0:T(8,128)(2,1)S(1)}, u32[]{:S(2)}, u32[]{:S(2)}) collective-permute-start(bf16[432,128]{1,0:T(8,128)(2,1)S(1)} %get-tuple-element.71), channel_id=1, source_target_pairs={{0,12},{2,14},{4,8},{6,10},{8,4},{10,6},{12,0},{14,2},{1,13},{3,15... | collective-permute-start | bytes 331784 | tf_op jit(solution)/shard_map/ppermute | solution.py:376
  53.5 0.2 collective-permute-start.24
  53.7 2.7 %collective-permute-start.25 = (bf16[432,128]{1,0:T(8,128)(2,1)S(1)}, bf16[432,128]{1,0:T(8,128)(2,1)S(1)}, u32[]{:S(2)}, u32[]{:S(2)}) collective-permute-start(bf16[432,128]{1,0:T(8,128)(2,1)S(1)} %get-tuple-element.73), channel_id=1, source_target_pairs={{0,10},{2,8},{4,14},{6,12},{8,2},{10,0},{12,6},{14,4},{1,11},{3,9}... | collective-permute-start | bytes 331784 | tf_op jit(solution)/shard_map/ppermute | solution.py:376
  56.4 0.0 copy-start.8
  56.4 7.7 %shard_map.139 = (bf16[432,128]{1,0:T(8,128)(2,1)S(1)}, bf16[432,128]{1,0:T(8,128)(2,1)S(1)}, bf16[432,128]{1,0:T(8,128)(2,1)S(1)}, bf16[432,128]{1,0:T(8,128)(2...) custom-call(bf16[384,128]{1,0:T(8,128)(2,1)S(1)} %copy-done.9, ...), custom_call_target="tpu_custom_call" | custom-call | flops 7000000000 | bytes 4194304 | tf_op jit(solution)/shard_map/pallas_call | solution.py:350
  64.1 1.5 %collective-permute-start.26 = (bf16[432,128]{1,0:T(8,128)(2,1)S(1)}, bf16[432,128]{1,0:T(8,128)(2,1)S(1)}, u32[]{:S(2)}, u32[]{:S(2)}) collective-permute-start(bf16[432,128]{1,0:T(8,128)(2,1)S(1)} %get-tuple-element.74), channel_id=1, source_target_pairs={{0,6},{2,4},{4,2},{6,0},{8,14},{10,12},{12,10},{14,8},{1,7},{3,5},... | collective-permute-start | bytes 331784 | tf_op jit(solution)/shard_map/ppermute | solution.py:376
  65.6 1.5 %collective-permute-start.27 = (bf16[432,128]{1,0:T(8,128)(2,1)S(1)}, bf16[432,128]{1,0:T(8,128)(2,1)S(1)}, u32[]{:S(2)}, u32[]{:S(2)}) collective-permute-start(bf16[432,128]{1,0:T(8,128)(2,1)S(1)} %get-tuple-element.75), channel_id=1, source_target_pairs={{0,8},{2,10},{4,12},{6,14},{8,0},{10,2},{12,4},{14,6},{1,9},{3,11}... | collective-permute-start | bytes 331784 | tf_op jit(solution)/shard_map/ppermute | solution.py:376
  67.1 2.3 %collective-permute-start.7 = (bf16[432,128]{1,0:T(8,128)(2,1)S(1)}, bf16[432,128]{1,0:T(8,128)(2,1)S(1)}, u32[]{:S(2)}, u32[]{:S(2)}) collective-permute-start(bf16[432,128]{1,0:T(8,128)(2,1)S(1)} %get-tuple-element.53), channel_id=1, source_target_pairs={{0,14},{2,12},{4,10},{6,8},{8,6},{10,4},{12,2},{14,0},{1,15},{3,13... | collective-permute-start | bytes 331784 | tf_op jit(solution)/shard_map/ppermute | solution.py:376
  69.5 2.0 %collective-permute-start.8 = (bf16[432,128]{1,0:T(8,128)(2,1)S(1)}, bf16[432,128]{1,0:T(8,128)(2,1)S(1)}, u32[]{:S(2)}, u32[]{:S(2)}) collective-permute-start(bf16[432,128]{1,0:T(8,128)(2,1)S(1)} %get-tuple-element.54), channel_id=1, source_target_pairs={{0,2},{2,0},{4,6},{6,4},{8,10},{10,8},{12,14},{14,12},{1,3},{3,1},... | collective-permute-start | bytes 331784 | tf_op jit(solution)/shard_map/ppermute | solution.py:376
  71.4 1.0 %collective-permute-start.9 = (bf16[432,128]{1,0:T(8,128)(2,1)S(1)}, bf16[432,128]{1,0:T(8,128)(2,1)S(1)}, u32[]{:S(2)}, u32[]{:S(2)}) collective-permute-start(bf16[432,128]{1,0:T(8,128)(2,1)S(1)} %get-tuple-element.55), channel_id=1, source_target_pairs={{0,12},{2,14},{4,8},{6,10},{8,4},{10,6},{12,0},{14,2},{1,13},{3,15... | collective-permute-start | bytes 331784 | tf_op jit(solution)/shard_map/ppermute | solution.py:376
  72.4 1.1 %collective-permute-done.26.refs_6_ = bf16[432,128]{1,0:T(8,128)(2,1)S(1)} collective-permute-done((bf16[432,128]{1,0:T(8,128)(2,1)S(1)}, bf16[432,128]{1,0:T(8,128)(2,1)S(1)}, u32[]{:S(2)}, u32[]{:S(2)}) %collective-permute-start.26) | collective-permute-done | bytes 110624 | tf_op jit(solution)/shard_map/ppermute | solution.py:376
  73.5 0.1 collective-permute-start.10
  73.6 2.3 %collective-permute-done.27.refs_7_ = bf16[432,128]{1,0:T(8,128)(2,1)S(1)} collective-permute-done((bf16[432,128]{1,0:T(8,128)(2,1)S(1)}, bf16[432,128]{1,0:T(8,128)(2,1)S(1)}, u32[]{:S(2)}, u32[]{:S(2)}) %collective-permute-start.27) | collective-permute-done | bytes 110624 | tf_op jit(solution)/shard_map/ppermute | solution.py:376
  75.9 0.1 collective-permute-start.11
  76.0 0.8 collective-permute-done.7.refs_1_
  76.8 5.3 %collective-permute-start.12 = (bf16[432,128]{1,0:T(8,128)(2,1)S(1)}, bf16[432,128]{1,0:T(8,128)(2,1)S(1)}, u32[]{:S(2)}, u32[]{:S(2)}) collective-permute-start(bf16[432,128]{1,0:T(8,128)(2,1)S(1)} %get-tuple-element.58), channel_id=1, source_target_pairs={{0,6},{2,4},{4,2},{6,0},{8,14},{10,12},{12,10},{14,8},{1,7},{3,5},... | collective-permute-start | bytes 331784 | tf_op jit(solution)/shard_map/ppermute | solution.py:376
  82.0 0.1 collective-permute-start.13
  82.1 3.0 %shard_map.142 = (bf16[2,192,1440]{2,1,0:T(8,128)(2,1)}, bf16[2,192,1440]{2,1,0:T(8,128)(2,1)}, f32[2,2304]{1,0:T(2,128)S(1)}, f32[2,2304]{1,0:T(2,128)S(1)}) custom-call(bf16[432,128]{1,0:T(8,128)(2,1)S(1)} %get-tuple-element.68.refs_0_, bf16[432,128]{1,0:T(8,128)(2,1)S(1)} %collective-permute-done.21.refs_1_, ...), custom_call_target="tpu_custom_call" | custom-call | flops 4000000000 | bytes 5242880 | tf_op jit(solution)/shard_map/pallas_call | solution.py:189
  85.2 0.3 collective-permute-done.12.refs_6_
  85.4 2.3 %collective-permute-done.13.refs_7_ = bf16[432,128]{1,0:T(8,128)(2,1)S(1)} collective-permute-done((bf16[432,128]{1,0:T(8,128)(2,1)S(1)}, bf16[432,128]{1,0:T(8,128)(2,1)S(1)}, u32[]{:S(2)}, u32[]{:S(2)}) %collective-permute-start.13) | collective-permute-done | bytes 110624 | tf_op jit(solution)/shard_map/ppermute | solution.py:376
  87.7 3.0 %shard_map.143 = (bf16[2,192,1440]{2,1,0:T(8,128)(2,1)}, bf16[2,192,1440]{2,1,0:T(8,128)(2,1)}, f32[2,2304]{1,0:T(2,128)}, f32[2,2304]{1,0:T(2,128)}) custom-call(bf16[432,128]{1,0:T(8,128)(2,1)S(1)} %get-tuple-element.52.refs_0_, bf16[432,128]{1,0:T(8,128)(2,1)S(1)} %collective-permute-done.7.refs_1_, ...), custom_call_target="tpu_custom_call", output_to_operand_aliasing={{0}: (12, {}), {1}: (13, {})} | custom-call | flops 4000000000 | bytes 5242880 | tf_op jit(solution)/shard_map/pallas_call | solution.py:189
  (40 shorter events, 0.1 us)
Async XLA Ops:
  6.0 17.2 %collective-permute-start.14 = (bf16[384,128]{1,0:T(8,128)(2,1)}, bf16[384,128]{1,0:T(8,128)(2,1)S(1)}, u32[]{:S(2)}, u32[]{:S(2)}) collective-permute-start(bf16[384,128]{1,0:T(8,128)(2,1)} %get-tuple-element.61), channel_id=1, source_target_pairs={{0,14},{2,12},{4,10},{6,8},{8,6},{10,4},{12,2},{14,0},{1,15},{3,13... | collective-permute-start | bytes 294920 | tf_op jit(solution)/shard_map/ppermute | solution.py:376
  11.9 11.3 %collective-permute-start.15 = (bf16[384,128]{1,0:T(8,128)(2,1)}, bf16[384,128]{1,0:T(8,128)(2,1)S(1)}, u32[]{:S(2)}, u32[]{:S(2)}) collective-permute-start(bf16[384,128]{1,0:T(8,128)(2,1)} %get-tuple-element.62), channel_id=1, source_target_pairs={{0,2},{2,0},{4,6},{6,4},{8,10},{10,8},{12,14},{14,12},{1,3},{3,1},... | collective-permute-start | bytes 294920 | tf_op jit(solution)/shard_map/ppermute | solution.py:376
  12.5 11.4 %collective-permute-start.16 = (bf16[384,128]{1,0:T(8,128)(2,1)}, bf16[384,128]{1,0:T(8,128)(2,1)S(1)}, u32[]{:S(2)}, u32[]{:S(2)}) collective-permute-start(bf16[384,128]{1,0:T(8,128)(2,1)} %get-tuple-element.63), channel_id=1, source_target_pairs={{0,12},{2,14},{4,8},{6,10},{8,4},{10,6},{12,0},{14,2},{1,13},{3,15... | collective-permute-start | bytes 294920 | tf_op jit(solution)/shard_map/ppermute | solution.py:376
  12.6 15.9 %collective-permute-start.17 = (bf16[384,128]{1,0:T(8,128)(2,1)}, bf16[384,128]{1,0:T(8,128)(2,1)S(1)}, u32[]{:S(2)}, u32[]{:S(2)}) collective-permute-start(bf16[384,128]{1,0:T(8,128)(2,1)} %get-tuple-element.64), channel_id=1, source_target_pairs={{0,4},{2,6},{4,0},{6,2},{8,12},{10,14},{12,8},{14,10},{1,5},{3,7},... | collective-permute-start | bytes 294920 | tf_op jit(solution)/shard_map/ppermute | solution.py:376
  12.6 10.6 %copy-start.12 = (bf16[384,128]{1,0:T(8,128)(2,1)S(1)}, bf16[384,128]{1,0:T(8,128)(2,1)}, u32[]{:S(2)}) copy-start(bf16[384,128]{1,0:T(8,128)(2,1)} %get-tuple-element.66) | copy-start | bytes 294916
  12.6 10.7 %copy-start.11 = (bf16[384,128]{1,0:T(8,128)(2,1)S(1)}, bf16[384,128]{1,0:T(8,128)(2,1)}, u32[]{:S(2)}) copy-start(bf16[384,128]{1,0:T(8,128)(2,1)} %get-tuple-element.67) | copy-start | bytes 294916
  12.6 27.6 %copy-start.2 = (bf16[4,96,192]{2,1,0:T(8,128)(2,1)S(1)}, bf16[4,96,192]{2,1,0:T(8,128)(2,1)}, u32[]{:S(2)}) copy-start(bf16[4,96,192]{2,1,0:T(8,128)(2,1)} %refs_9_.5) | copy-start | bytes 442372
  12.6 27.6 %copy-start.3 = (bf16[4,96,192]{2,1,0:T(8,128)(2,1)S(1)}, bf16[4,96,192]{2,1,0:T(8,128)(2,1)}, u32[]{:S(2)}) copy-start(bf16[4,96,192]{2,1,0:T(8,128)(2,1)} %refs_11_.3) | copy-start | bytes 442372
  12.6 27.6 %copy-start.4 = (f32[4,192]{1,0:T(4,128)S(1)}, f32[4,192]{1,0:T(4,128)}, u32[]{:S(2)}) copy-start(f32[4,192]{1,0:T(4,128)} %refs_10_.3) | copy-start | bytes 9220
  12.6 27.6 %copy-start.5 = (f32[4,192]{1,0:T(4,128)S(1)}, f32[4,192]{1,0:T(4,128)}, u32[]{:S(2)}) copy-start(f32[4,192]{1,0:T(4,128)} %refs_12_.3) | copy-start | bytes 9220
  12.6 27.6 %copy-start.7 = (bf16[512,256]{1,0:T(8,128)(2,1)S(1)}, bf16[512,256]{1,0:T(8,128)(2,1)}, u32[]{:S(2)}) copy-start(bf16[512,256]{1,0:T(8,128)(2,1)} %constant.20.clone.refs_8_) | copy-start | bytes 786436
  12.6 27.6 %copy-start.10 = (bf16[384,128]{1,0:T(8,128)(2,1)S(1)}, bf16[384,128]{1,0:T(8,128)(2,1)}, u32[]{:S(2)}) copy-start(bf16[384,128]{1,0:T(8,128)(2,1)} %get-tuple-element.60.refs_0_) | copy-start | bytes 294916
  12.7 16.4 %collective-permute-start.18 = (bf16[384,128]{1,0:T(8,128)(2,1)}, bf16[384,128]{1,0:T(8,128)(2,1)S(1)}, u32[]{:S(2)}, u32[]{:S(2)}) collective-permute-start(bf16[384,128]{1,0:T(8,128)(2,1)} %get-tuple-element.65), channel_id=1, source_target_pairs={{0,10},{2,8},{4,14},{6,12},{8,2},{10,0},{12,6},{14,4},{1,11},{3,9}... | collective-permute-start | bytes 294920 | tf_op jit(solution)/shard_map/ppermute | solution.py:376
  23.2 6.7 %collective-permute-start.19 = (bf16[384,128]{1,0:T(8,128)(2,1)S(1)}, bf16[384,128]{1,0:T(8,128)(2,1)S(1)}, u32[]{:S(2)}, u32[]{:S(2)}) collective-permute-start(bf16[384,128]{1,0:T(8,128)(2,1)S(1)} %copy-done.12), channel_id=1, source_target_pairs={{0,6},{2,4},{4,2},{6,0},{8,14},{10,12},{12,10},{14,8},{1,7},{3,5},... | collective-permute-start | bytes 294920 | tf_op jit(solution)/shard_map/ppermute | solution.py:376
  23.3 13.2 %collective-permute-start.20 = (bf16[384,128]{1,0:T(8,128)(2,1)S(1)}, bf16[384,128]{1,0:T(8,128)(2,1)S(1)}, u32[]{:S(2)}, u32[]{:S(2)}) collective-permute-start(bf16[384,128]{1,0:T(8,128)(2,1)S(1)} %copy-done.11), channel_id=1, source_target_pairs={{0,8},{2,10},{4,12},{6,14},{8,0},{10,2},{12,4},{14,6},{1,9},{3,11}... | collective-permute-start | bytes 294920 | tf_op jit(solution)/shard_map/ppermute | solution.py:376
  23.9 12.7 %collective-permute-start = (bf16[384,128]{1,0:T(8,128)(2,1)}, bf16[384,128]{1,0:T(8,128)(2,1)S(1)}, u32[]{:S(2)}, u32[]{:S(2)}) collective-permute-start(bf16[384,128]{1,0:T(8,128)(2,1)} %get-tuple-element.45), channel_id=1, source_target_pairs={{0,14},{2,12},{4,10},{6,8},{8,6},{10,4},{12,2},{14,0},{1,15},{3,13... | collective-permute-start | bytes 294920 | tf_op jit(solution)/shard_map/ppermute | solution.py:376
  28.5 11.7 %collective-permute-start.1 = (bf16[384,128]{1,0:T(8,128)(2,1)}, bf16[384,128]{1,0:T(8,128)(2,1)S(1)}, u32[]{:S(2)}, u32[]{:S(2)}) collective-permute-start(bf16[384,128]{1,0:T(8,128)(2,1)} %get-tuple-element.46), channel_id=1, source_target_pairs={{0,2},{2,0},{4,6},{6,4},{8,10},{10,8},{12,14},{14,12},{1,3},{3,1},... | collective-permute-start | bytes 294920 | tf_op jit(solution)/shard_map/ppermute | solution.py:376
  29.1 18.9 %collective-permute-start.2 = (bf16[384,128]{1,0:T(8,128)(2,1)}, bf16[384,128]{1,0:T(8,128)(2,1)S(1)}, u32[]{:S(2)}, u32[]{:S(2)}) collective-permute-start(bf16[384,128]{1,0:T(8,128)(2,1)} %get-tuple-element.47), channel_id=1, source_target_pairs={{0,12},{2,14},{4,8},{6,10},{8,4},{10,6},{12,0},{14,2},{1,13},{3,15... | collective-permute-start | bytes 294920 | tf_op jit(solution)/shard_map/ppermute | solution.py:376
  29.9 20.5 %collective-permute-start.3 = (bf16[384,128]{1,0:T(8,128)(2,1)}, bf16[384,128]{1,0:T(8,128)(2,1)S(1)}, u32[]{:S(2)}, u32[]{:S(2)}) collective-permute-start(bf16[384,128]{1,0:T(8,128)(2,1)} %get-tuple-element.48), channel_id=1, source_target_pairs={{0,4},{2,6},{4,0},{6,2},{8,12},{10,14},{12,8},{14,10},{1,5},{3,7},... | collective-permute-start | bytes 294920 | tf_op jit(solution)/shard_map/ppermute | solution.py:376
  36.5 16.0 %collective-permute-start.4 = (bf16[384,128]{1,0:T(8,128)(2,1)}, bf16[384,128]{1,0:T(8,128)(2,1)S(1)}, u32[]{:S(2)}, u32[]{:S(2)}) collective-permute-start(bf16[384,128]{1,0:T(8,128)(2,1)} %get-tuple-element.49), channel_id=1, source_target_pairs={{0,10},{2,8},{4,14},{6,12},{8,2},{10,0},{12,6},{14,4},{1,11},{3,9}... | collective-permute-start | bytes 294920 | tf_op jit(solution)/shard_map/ppermute | solution.py:376
  36.5 16.9 %collective-permute-start.5 = (bf16[384,128]{1,0:T(8,128)(2,1)}, bf16[384,128]{1,0:T(8,128)(2,1)S(1)}, u32[]{:S(2)}, u32[]{:S(2)}) collective-permute-start(bf16[384,128]{1,0:T(8,128)(2,1)} %get-tuple-element.50), channel_id=1, source_target_pairs={{0,6},{2,4},{4,2},{6,0},{8,14},{10,12},{12,10},{14,8},{1,7},{3,5},... | collective-permute-start | bytes 294920 | tf_op jit(solution)/shard_map/ppermute | solution.py:376
  40.2 13.5 %collective-permute-start.6 = (bf16[384,128]{1,0:T(8,128)(2,1)}, bf16[384,128]{1,0:T(8,128)(2,1)S(1)}, u32[]{:S(2)}, u32[]{:S(2)}) collective-permute-start(bf16[384,128]{1,0:T(8,128)(2,1)} %get-tuple-element.51), channel_id=1, source_target_pairs={{0,8},{2,10},{4,12},{6,14},{8,0},{10,2},{12,4},{14,6},{1,9},{3,11}... | collective-permute-start | bytes 294920 | tf_op jit(solution)/shard_map/ppermute | solution.py:376
  40.2 16.2 %copy-start.9 = (bf16[384,128]{1,0:T(8,128)(2,1)S(1)}, bf16[384,128]{1,0:T(8,128)(2,1)}, u32[]{:S(2)}) copy-start(bf16[384,128]{1,0:T(8,128)(2,1)} %get-tuple-element.44.refs_0_) | copy-start | bytes 294916
  47.9 16.2 %collective-permute-start.21 = (bf16[432,128]{1,0:T(8,128)(2,1)S(1)}, bf16[432,128]{1,0:T(8,128)(2,1)S(1)}, u32[]{:S(2)}, u32[]{:S(2)}) collective-permute-start(bf16[432,128]{1,0:T(8,128)(2,1)S(1)} %get-tuple-element.69), channel_id=1, source_target_pairs={{0,14},{2,12},{4,10},{6,8},{8,6},{10,4},{12,2},{14,0},{1,15},{3,13... | collective-permute-start | bytes 331784 | tf_op jit(solution)/shard_map/ppermute | solution.py:376
  50.4 15.3 %collective-permute-start.22 = (bf16[432,128]{1,0:T(8,128)(2,1)S(1)}, bf16[432,128]{1,0:T(8,128)(2,1)S(1)}, u32[]{:S(2)}, u32[]{:S(2)}) collective-permute-start(bf16[432,128]{1,0:T(8,128)(2,1)S(1)} %get-tuple-element.70), channel_id=1, source_target_pairs={{0,2},{2,0},{4,6},{6,4},{8,10},{10,8},{12,14},{14,12},{1,3},{3,1},... | collective-permute-start | bytes 331784 | tf_op jit(solution)/shard_map/ppermute | solution.py:376
  52.5 14.6 %collective-permute-start.23 = (bf16[432,128]{1,0:T(8,128)(2,1)S(1)}, bf16[432,128]{1,0:T(8,128)(2,1)S(1)}, u32[]{:S(2)}, u32[]{:S(2)}) collective-permute-start(bf16[432,128]{1,0:T(8,128)(2,1)S(1)} %get-tuple-element.71), channel_id=1, source_target_pairs={{0,12},{2,14},{4,8},{6,10},{8,4},{10,6},{12,0},{14,2},{1,13},{3,15... | collective-permute-start | bytes 331784 | tf_op jit(solution)/shard_map/ppermute | solution.py:376
  53.5 16.0 %collective-permute-start.24 = (bf16[432,128]{1,0:T(8,128)(2,1)S(1)}, bf16[432,128]{1,0:T(8,128)(2,1)S(1)}, u32[]{:S(2)}, u32[]{:S(2)}) collective-permute-start(bf16[432,128]{1,0:T(8,128)(2,1)S(1)} %get-tuple-element.72), channel_id=1, source_target_pairs={{0,4},{2,6},{4,0},{6,2},{8,12},{10,14},{12,8},{14,10},{1,5},{3,7},... | collective-permute-start | bytes 331784 | tf_op jit(solution)/shard_map/ppermute | solution.py:376
  53.7 17.7 %collective-permute-start.25 = (bf16[432,128]{1,0:T(8,128)(2,1)S(1)}, bf16[432,128]{1,0:T(8,128)(2,1)S(1)}, u32[]{:S(2)}, u32[]{:S(2)}) collective-permute-start(bf16[432,128]{1,0:T(8,128)(2,1)S(1)} %get-tuple-element.73), channel_id=1, source_target_pairs={{0,10},{2,8},{4,14},{6,12},{8,2},{10,0},{12,6},{14,4},{1,11},{3,9}... | collective-permute-start | bytes 331784 | tf_op jit(solution)/shard_map/ppermute | solution.py:376
  56.4 25.7 %copy-start = (bf16[2,1440,192]{1,2,0:T(8,128)(2,1)S(1)}, bf16[2,1440,192]{1,2,0:T(8,128)(2,1)}, u32[]{:S(2)}) copy-start(bf16[2,1440,192]{1,2,0:T(8,128)(2,1)} %param.11) | copy-start | bytes 3317764
  56.4 25.7 %copy-start.1 = (bf16[2,1440,192]{1,2,0:T(8,128)(2,1)S(1)}, bf16[2,1440,192]{1,2,0:T(8,128)(2,1)}, u32[]{:S(2)}) copy-start(bf16[2,1440,192]{1,2,0:T(8,128)(2,1)} %param.12) | copy-start | bytes 3317764
  56.4 25.7 %copy-start.6 = (bf16[1024,1440]{1,0:T(8,128)(2,1)S(1)}, bf16[1024,1440]{1,0:T(8,128)(2,1)}, u32[]{:S(2)}) copy-start(bf16[1024,1440]{1,0:T(8,128)(2,1)} %constant.17.clone.refs_8_) | copy-start | bytes 8847364
  56.4 25.7 %copy-start.8 = (f32[8,128]{1,0:T(8,128)S(1)}, f32[8,128]{1,0:T(8,128)}, u32[]{:S(2)}) copy-start(f32[8,128]{1,0:T(8,128)} %constant.19.clone.refs_9_) | copy-start | bytes 12292
  64.1 9.4 %collective-permute-start.26 = (bf16[432,128]{1,0:T(8,128)(2,1)S(1)}, bf16[432,128]{1,0:T(8,128)(2,1)S(1)}, u32[]{:S(2)}, u32[]{:S(2)}) collective-permute-start(bf16[432,128]{1,0:T(8,128)(2,1)S(1)} %get-tuple-element.74), channel_id=1, source_target_pairs={{0,6},{2,4},{4,2},{6,0},{8,14},{10,12},{12,10},{14,8},{1,7},{3,5},... | collective-permute-start | bytes 331784 | tf_op jit(solution)/shard_map/ppermute | solution.py:376
  65.6 10.3 %collective-permute-start.27 = (bf16[432,128]{1,0:T(8,128)(2,1)S(1)}, bf16[432,128]{1,0:T(8,128)(2,1)S(1)}, u32[]{:S(2)}, u32[]{:S(2)}) collective-permute-start(bf16[432,128]{1,0:T(8,128)(2,1)S(1)} %get-tuple-element.75), channel_id=1, source_target_pairs={{0,8},{2,10},{4,12},{6,14},{8,0},{10,2},{12,4},{14,6},{1,9},{3,11}... | collective-permute-start | bytes 331784 | tf_op jit(solution)/shard_map/ppermute | solution.py:376
  67.1 9.7 %collective-permute-start.7 = (bf16[432,128]{1,0:T(8,128)(2,1)S(1)}, bf16[432,128]{1,0:T(8,128)(2,1)S(1)}, u32[]{:S(2)}, u32[]{:S(2)}) collective-permute-start(bf16[432,128]{1,0:T(8,128)(2,1)S(1)} %get-tuple-element.53), channel_id=1, source_target_pairs={{0,14},{2,12},{4,10},{6,8},{8,6},{10,4},{12,2},{14,0},{1,15},{3,13... | collective-permute-start | bytes 331784 | tf_op jit(solution)/shard_map/ppermute | solution.py:376
  69.5 12.6 %collective-permute-start.8 = (bf16[432,128]{1,0:T(8,128)(2,1)S(1)}, bf16[432,128]{1,0:T(8,128)(2,1)S(1)}, u32[]{:S(2)}, u32[]{:S(2)}) collective-permute-start(bf16[432,128]{1,0:T(8,128)(2,1)S(1)} %get-tuple-element.54), channel_id=1, source_target_pairs={{0,2},{2,0},{4,6},{6,4},{8,10},{10,8},{12,14},{14,12},{1,3},{3,1},... | collective-permute-start | bytes 331784 | tf_op jit(solution)/shard_map/ppermute | solution.py:376
  71.4 13.7 %collective-permute-start.9 = (bf16[432,128]{1,0:T(8,128)(2,1)S(1)}, bf16[432,128]{1,0:T(8,128)(2,1)S(1)}, u32[]{:S(2)}, u32[]{:S(2)}) collective-permute-start(bf16[432,128]{1,0:T(8,128)(2,1)S(1)} %get-tuple-element.55), channel_id=1, source_target_pairs={{0,12},{2,14},{4,8},{6,10},{8,4},{10,6},{12,0},{14,2},{1,13},{3,15... | collective-permute-start | bytes 331784 | tf_op jit(solution)/shard_map/ppermute | solution.py:376
  73.5 11.7 %collective-permute-start.10 = (bf16[432,128]{1,0:T(8,128)(2,1)S(1)}, bf16[432,128]{1,0:T(8,128)(2,1)S(1)}, u32[]{:S(2)}, u32[]{:S(2)}) collective-permute-start(bf16[432,128]{1,0:T(8,128)(2,1)S(1)} %get-tuple-element.56), channel_id=1, source_target_pairs={{0,4},{2,6},{4,0},{6,2},{8,12},{10,14},{12,8},{14,10},{1,5},{3,7},... | collective-permute-start | bytes 331784 | tf_op jit(solution)/shard_map/ppermute | solution.py:376
  75.9 9.3 %collective-permute-start.11 = (bf16[432,128]{1,0:T(8,128)(2,1)S(1)}, bf16[432,128]{1,0:T(8,128)(2,1)S(1)}, u32[]{:S(2)}, u32[]{:S(2)}) collective-permute-start(bf16[432,128]{1,0:T(8,128)(2,1)S(1)} %get-tuple-element.57), channel_id=1, source_target_pairs={{0,10},{2,8},{4,14},{6,12},{8,2},{10,0},{12,6},{14,4},{1,11},{3,9}... | collective-permute-start | bytes 331784 | tf_op jit(solution)/shard_map/ppermute | solution.py:376
  76.8 8.6 %collective-permute-start.12 = (bf16[432,128]{1,0:T(8,128)(2,1)S(1)}, bf16[432,128]{1,0:T(8,128)(2,1)S(1)}, u32[]{:S(2)}, u32[]{:S(2)}) collective-permute-start(bf16[432,128]{1,0:T(8,128)(2,1)S(1)} %get-tuple-element.58), channel_id=1, source_target_pairs={{0,6},{2,4},{4,2},{6,0},{8,14},{10,12},{12,10},{14,8},{1,7},{3,5},... | collective-permute-start | bytes 331784 | tf_op jit(solution)/shard_map/ppermute | solution.py:376
  82.0 5.6 %collective-permute-start.13 = (bf16[432,128]{1,0:T(8,128)(2,1)S(1)}, bf16[432,128]{1,0:T(8,128)(2,1)S(1)}, u32[]{:S(2)}, u32[]{:S(2)}) collective-permute-start(bf16[432,128]{1,0:T(8,128)(2,1)S(1)} %get-tuple-element.59), channel_id=1, source_target_pairs={{0,8},{2,10},{4,12},{6,14},{8,0},{10,2},{12,4},{14,6},{1,9},{3,11}... | collective-permute-start | bytes 331784 | tf_op jit(solution)/shard_map/ppermute | solution.py:376

commit v3 on v2

--- a/solution.py
+++ b/solution.py
@@ -14,7 +14,7 @@
 HALF = 64
 PACK = 16
 MIB = 1024 * 1024
-ZONAL_MIB = 60
+ZONAL_MIB = 24
 MIDDLE_MIB = 24
 INVERSE_MIB = 24
 
@@ -52,10 +52,10 @@
     return jnp.dot(former, latter, preferred_element_type=F32)
 
 
-def swap_parts(values, first_sign):
+def with_swapped(values, first_sign):
     lane = lax.broadcasted_iota(jnp.int32, (1, LANES), 1)
-    sign = jnp.where(lane < HALF, first_sign, -first_sign).astype(F32)
-    return pltpu.roll(values, HALF, axis=1) * sign
+    sign = jnp.where(lane < HALF, first_sign, -first_sign).astype(values.dtype)
+    return jnp.concatenate([values, pltpu.roll(values, HALF, axis=1) * sign], axis=0)
 
 
 def slots(pieces):
@@ -70,59 +70,67 @@
     return pltpu.CompilerParams(vmem_limit_bytes=mebibytes * MIB)
 
 
-def zonal_kernel(mine_ref, field_ref, cotangent_ref, table_ref, scale_ref, *rest):
-    outs, (rows_ref, pair_ref) = rest[:-2], rest[-2:]
-    step = pl.program_id(0)
-    lines, width, col_count = field_ref.shape
+def zonal_kernel(group, width, pieces, field_ref, cotangent_ref, table_ref, scale_ref, *refs):
+    outs, (rows_ref, columns_ref, pair_ref, row_sems, column_sems) = refs[:pieces], refs[pieces:]
+    lines = field_ref.shape[0]
     half = lines * width
-
-    @pl.when(step == 0)
-    def _():
-        rows_ref[:half] = field_ref[...].reshape(half, col_count)
-        rows_ref[half:] = cotangent_ref[...].reshape(half, col_count)
-
-    odd = jnp.bitwise_and(mine_ref[0], 1)
-    result = mm(rows_ref[...], table_ref[...])
-    for piece in range(2):
-        lanes = slice(piece * LANES, (piece + 1) * LANES)
-        pair_ref[piece, :half] = result[:half, lanes].astype(BF16)
-        pair_ref[piece, half:] = (result[half:, lanes] * scale_ref[:, lanes]).astype(BF16)
-    for place in range(len(outs) // 2):
-
-        @pl.when(step == place)
-        def _():
-            where = slots(len(outs))
-            outs[where.index(2 * place)][...] = pair_ref[odd]
-            outs[where.index(2 * place + 1)][...] = pair_ref[1 - odd]
-
-
-def zonal(mine, field, cotangent, table, scale, group, width, pieces):
+    wide = 2 * LANES
+    mine = lax.axis_index("lat")
+    pair = lax.shift_right_logical(mine, 1)
+    odd = jnp.bitwise_and(mine, 1)
+    rows = []
+    for kind, source in enumerate((field_ref, cotangent_ref)):
+        for line in range(lines):
+            index = kind * lines + line
+            copy = pltpu.make_async_copy(
+                source.at[line, group * width : (group + 1) * width, :],
+                rows_ref.at[index * width : (index + 1) * width, :],
+                row_sems.at[index],
+            )
+            copy.start()
+            rows.append(copy)
+    columns = []
+    for place in range(pieces // 2):
+        begin = pl.multiple_of(jnp.bitwise_xor(pair, place) * wide, wide)
+        copy = pltpu.make_async_copy(
+            table_ref.at[:, pl.ds(begin, wide)], columns_ref.at[place], column_sems.at[place]
+        )
+        copy.start()
+        columns.append(copy)
+    for copy in rows:
+        copy.wait()
+    where = slots(pieces)
+    for place in range(pieces // 2):
+        columns[place].wait()
+        result = mm(rows_ref[...], columns_ref[place])
+        for piece in range(2):
+            lanes = slice(piece * LANES, (piece + 1) * LANES)
+            scale = scale_ref[pl.ds(2 * jnp.bitwise_xor(pair, place) + piece, 1), :]
+            pair_ref[piece, :half] = result[:half, lanes].astype(BF16)
+            pair_ref[piece, half:] = (result[half:, lanes] * scale).astype(BF16)
+        outs[where.index(2 * place)][...] = pair_ref[odd]
+        outs[where.index(2 * place + 1)][...] = pair_ref[1 - odd]
+
+
+def zonal(field, cotangent, table, scale, group, width, pieces):
     lines, _, col_count = field.shape
     rows = 2 * lines * width
-    wide = 2 * LANES
-
-    def block_of(i, place):
-        return (0, jnp.bitwise_xor(lax.shift_right_logical(place[0], 1), i))
-
-    own = pl.BlockSpec((lines, width, col_count), lambda i, place: (0, group, 0))
+    away = pl.BlockSpec(memory_space=pltpu.HBM)
     return pl.pallas_call(
-        zonal_kernel,
-        grid_spec=pltpu.PrefetchScalarGridSpec(
-            num_scalar_prefetch=1,
-            grid=(pieces // 2,),
-            in_specs=[
-                own,
-                own,
-                pl.BlockSpec((col_count, wide), block_of),
-                pl.BlockSpec((1, wide), block_of),
-            ],
-            out_specs=[pl.BlockSpec((rows, LANES), lambda i, place: (0, 0)) for _ in range(pieces)],
-            scratch_shapes=[pltpu.VMEM((rows, col_count), BF16), pltpu.VMEM((2, rows, LANES), BF16)],
-        ),
+        functools.partial(zonal_kernel, group, width, pieces),
+        in_specs=[away, away, away, whole(*scale.shape)],
+        out_specs=[whole(rows, LANES) for _ in range(pieces)],
         out_shape=[jax.ShapeDtypeStruct((rows, LANES), BF16) for _ in range(pieces)],
+        scratch_shapes=[
+            pltpu.VMEM((rows, col_count), BF16),
+            pltpu.VMEM((pieces // 2, col_count, 2 * LANES), BF16),
+            pltpu.VMEM((2, rows, LANES), BF16),
+            pltpu.SemaphoreType.DMA((2 * lines,)),
+            pltpu.SemaphoreType.DMA((pieces // 2,)),
+        ],
         compiler_params=limits(ZONAL_MIB),
         cost_estimate=pl.CostEstimate(flops=4 * 10**9, bytes_accessed=4 * MIB, transcendentals=0),
-    )(mine, field, cotangent, table, scale)
+    )(field, cotangent, table, scale)
 
 
 def inverse_kernel(pieces, given, group, *refs):
@@ -208,26 +216,16 @@
 
 
 def meridian(load, mixer, first_sign, channels, store):
-    count = mixer.shape[1] // PACK
+    count = mixer.shape[0] // PACK
     for start in range(0, channels, 2 * PACK):
-        pair = jnp.concatenate(
-            [load(start + shift).reshape(count * PACK, LANES) for shift in (0, PACK)], axis=1
-        )
-        both = mm(mixer[...], pair)
+        pair = [
+            with_swapped(load(start + shift).reshape(count * PACK, LANES), first_sign)
+            for shift in (0, PACK)
+        ]
+        both = mm(mixer[...], side_by_side(pair))
         for index in range(2):
-            half = both[:, index * LANES : (index + 1) * LANES]
-            value = half[: count * PACK] + swap_parts(half[count * PACK :], first_sign)
+            value = both[:, index * LANES : (index + 1) * LANES]
             store(start + index * PACK, value.reshape(count, PACK, LANES))
-
-
-def complex_dot(weights, operand, first_sign):
-    width = weights.shape[0] // 2
-    both = mm(weights, jnp.concatenate(operand, axis=1))
-    return [
-        both[:width, i * LANES : (i + 1) * LANES]
-        + swap_parts(both[width:, i * LANES : (i + 1) * LANES], first_sign)
-        for i in range(len(operand))
-    ]
 
 
 def nt(former, latter):
@@ -245,9 +243,10 @@
     return jnp.where(lane < HALF, tall[:width], tall[width:])
 
 
-def stacked(weight):
+def forth(weight):
     width = weight.shape[0]
-    return jnp.concatenate([weight[:, :width], weight[:, width:]], axis=0)
+    turned = weight.T
+    return side_by_side([turned[:width], turned[width:]])
 
 
 def middle_kernel(group, groups, normalizer, pieces, *refs):
@@ -266,8 +265,7 @@
             adjoint_ref[row] = block[(lines + line) * width : (lines + line + 1) * width]
 
     first, second = first_ref[index], second_ref[index]
-    first_ahead, second_ahead = first.T, second.T
-    first_back, second_back = stacked(first), stacked(second)
+    first_ahead, second_ahead = forth(first), forth(second)
     first_bias, second_bias = bias_lanes(first_bias_ref, index), bias_lanes(second_bias_ref, index)
 
     def keep(start, value):
@@ -282,38 +280,39 @@
 
     first_sum = jnp.zeros((width, 2 * width), F32)
     second_sum = jnp.zeros((width, 2 * width), F32)
-    for row in range(0, count, 2):
-        both = range(2)
-        inputs = [harm_ref[row + i] for i in both]
-        pre = complex_dot(first_ahead, inputs, -1.0)
+    step = 2
+    for row in range(0, count, step):
+        members = range(step)
+
+        def lanes_of(wide):
+            return [wide[:, i * LANES : (i + 1) * LANES] for i in members]
+
+        inputs = [harm_ref[row + i] for i in members]
+        pre = lanes_of(mm(first_ahead, side_by_side([with_swapped(x, -1.0) for x in inputs])))
         hidden, slope = [], []
-        for i in both:
+        for i in members:
             v = pre[i] + first_bias
             square = v * v
-            tangent = jnp.tanh(GELU_SCALE * (v + GELU_CUBIC * square * v))
-            outer = 0.5 * (1.0 + tangent)
-            inner = GELU_SCALE * (1.0 + 3.0 * GELU_CUBIC * square)
+            tangent = jnp.tanh(v * (GELU_SCALE + GELU_SCALE * GELU_CUBIC * square))
+            outer = 0.5 + 0.5 * tangent
+            inner = 0.5 * GELU_SCALE + 1.5 * GELU_SCALE * GELU_CUBIC * square
             hidden.append((v * outer).astype(BF16))
-            slope.append(outer + 0.5 * v * (1.0 - tangent * tangent) * inner)
-        pre = complex_dot(second_ahead, hidden, -1.0)
-        exact = []
-        for i in both:
+            slope.append(outer + v * (1.0 - tangent * tangent) * inner)
+        pre = lanes_of(mm(second_ahead, side_by_side([with_swapped(x, -1.0) for x in hidden])))
+        second_adjoint = []
+        for i in members:
             v = pre[i] + second_bias
             squashed = jnp.tanh(v * (1.0 / SHRINK))
             shrunk_ref[row + i] = (v - SHRINK * squashed).astype(BF16)
-            exact.append(exact_ref[row + i] * (squashed * squashed))
-        second_adjoint = [a.astype(BF16) for a in exact]
-        turned = [swap_parts(a, 1.0).astype(BF16) for a in exact]
-        pairs = jnp.concatenate([side_by_side(second_adjoint), side_by_side(turned)], axis=0)
+            second_adjoint.append((exact_ref[row + i] * (squashed * squashed)).astype(BF16))
+        pairs = side_by_side([with_swapped(x, 1.0) for x in second_adjoint])
         second_sum += nt(side_by_side(hidden), pairs)
-        back = complex_dot(second_back, second_adjoint, 1.0)
-        exact = [back[i] * slope[i] for i in both]
-        first_adjoint = [a.astype(BF16) for a in exact]
-        turned = [swap_parts(a, 1.0).astype(BF16) for a in exact]
-        pairs = jnp.concatenate([side_by_side(first_adjoint), side_by_side(turned)], axis=0)
+        back = lanes_of(mm(second, pairs))
+        first_adjoint = [(back[i] * slope[i]).astype(BF16) for i in members]
+        pairs = side_by_side([with_swapped(x, 1.0) for x in first_adjoint])
         first_sum += nt(side_by_side(inputs), pairs)
-        back = complex_dot(first_back, first_adjoint, 1.0)
-        for i in both:
+        back = lanes_of(mm(first, pairs))
+        for i in members:
             harm_ref[row + i] = back[i].astype(BF16)
 
     sums_ref[0, :width] = first_sum * normalizer
@@ -405,18 +404,16 @@
     cosine, sines = meridian_waves(row_count)
     unit = np.eye(PACK, dtype=np.float32)
     mixer = np.concatenate(
-        [np.kron(cosine.astype(np.float32), unit), np.kron(sines.astype(np.float32), unit)], axis=0
+        [np.kron(cosine.astype(np.float32), unit), np.kron(sines.astype(np.float32), unit)], axis=1
     ).astype(BF16)
     ahead, back = jnp.asarray(table), jnp.asarray(np.ascontiguousarray(table.T))
-    wide_factor = jnp.asarray(factor.reshape(1, 2 * KW))
     tall_factor = jnp.asarray(factor.reshape(lat_count, 2 * sub_count))
     mixer = jnp.asarray(mixer)
     normalizer = 1.0 / math.sqrt(row_count * KW)
-    mine = lax.axis_index("lat").astype(jnp.int32).reshape(1)
     field, cotangent = field.transpose(0, 2, 1), cotangent.transpose(0, 2, 1)
 
     arrived = [
-        swap_blocks(zonal(mine, field, cotangent, ahead, wide_factor, group, width, lat_count))
+        swap_blocks(zonal(field, cotangent, ahead, tall_factor, group, width, lat_count))
         for group in range(groups)
     ]
     returned = [

time: 91 us -> 93.7 us (1.030)
  local copies, waits for them, and re-layouts: 0.07 us -> 5.09 us
  Pallas kernels: 31.9 us -> 27.3 us
  starting transfers between devices: 43.8 us -> 45.1 us
  waiting for transfers between devices: 14.1 us -> 15.1 us
    unnamed x26 -> x24, local copies, waits for them, and re-layouts: 0.07 us -> 5.09 us
    pallas_call x2, Pallas kernels: 10.6 us -> 8.13 us  [zonal(): pl.pallas_call(functools.partial(zonal_kernel, group, width, pieces), in_...]
    pallas_call x2, Pallas kernels: 15.3 us -> 13.1 us  [middle(): pl.pallas_call(functools.partial(middle_kernel, group, groups, normalizer...]
    ppermute x28, starting transfers between devices: 43.8 us -> 45.1 us  [pass_to(): lax.ppermute(block, 'lat', [(place, place ^ shift) for place in range(cou...]
    ppermute x28, waiting for transfers between devices: 14.1 us -> 15.1 us  [pass_to(): lax.ppermute(block, 'lat', [(place, place ^ shift) for place in range(cou...]
  transfers between devices with their start and end apart: 28 -> 28, of which waited for: 7 -> 5; matrix products, arithmetic and copies ran while one was open for 0% -> 0% of each run, Pallas kernels for 26% -> 22%
where the time goes in v3:
time: 93.7 us; the launch traced here: 93.4 us
  starting transfers between devices  45.1 us (48%)
  Pallas kernels  27.3 us (29%)
  waiting for transfers between devices  15.1 us (16%)
  local copies, waits for them, and re-layouts  5.09 us (5%)
    ppermute x28, starting transfers between devices, pass_to(): lax.ppermute(block, 'lat', [(place, place ^ shift) for place in range(cou...  45.1 us
    ppermute x28, waiting for transfers between devices, pass_to(): lax.ppermute(block, 'lat', [(place, place ^ shift) for place in range(cou...  15.1 us
    pallas_call x2, Pallas kernels, middle(): pl.pallas_call(functools.partial(middle_kernel, group, groups, normalizer...  13.1 us
    pallas_call x2, Pallas kernels, zonal(): pl.pallas_call(functools.partial(zonal_kernel, group, width, pieces), in_...  8.13 us
    pallas_call x2, Pallas kernels, inverse(): pl.pallas_call(functools.partial(inverse_kernel, pieces, len(before), gro...  6.05 us
    unnamed x24, local copies, waits for them, and re-layouts  5.09 us
  transfers between devices with their start and end apart: 28, of which 5 were waited for; matrix products, arithmetic and copies ran while one was open for 0% of the time, Pallas kernels for 22%

profile of v3, /device:TPU:0, one launch (start us, length us, event | category | flops | bytes accessed | tf_op | source)
XLA Modules:
  0.0 93.4 jit_solution(5075783674536581029)
XLA Ops:
  0.6 0.0 copy-start
  0.6 1.3 %copy-done = bf16[2,1440,192]{1,2,0:T(8,128)(2,1)S(1)} copy-done((bf16[2,1440,192]{1,2,0:T(8,128)(2,1)S(1)}, bf16[2,1440,192]{1,2,0:T(8,128)(2,1)}, u32[]{:S(2)}) %copy-start) | copy-done | bytes 1105944
  1.9 1.3 %copy-done.2 = bf16[2,1440,192]{1,2,0:T(8,128)(2,1)S(1)} copy-done((bf16[2,1440,192]{1,2,0:T(8,128)(2,1)S(1)}, bf16[2,1440,192]{1,2,0:T(8,128)(2,1)}, u32[]{:S(2)}) %copy-start.2) | copy-done | bytes 1105944
  3.2 1.8 %copy-done.9 = bf16[1440,1024]{1,0:T(8,128)(2,1)S(1)} copy-done((bf16[1440,1024]{1,0:T(8,128)(2,1)S(1)}, bf16[1440,1024]{1,0:T(8,128)(2,1)}, u32[]{:S(2)}) %copy-start.9) | copy-done | bytes 2949144
  5.0 0.7 copy-done.11
  5.7 4.0 %shard_map.131 = (bf16[384,128]{1,0:T(8,128)(2,1)S(1)}, bf16[384,128]{1,0:T(8,128)(2,1)S(1)}, bf16[384,128]{1,0:T(8,128)(2,1)S(1)}, bf16[384,128]{1,0:T(8,128)(2...) custom-call(bf16[2,192,1440]{2,1,0:T(8,128)(2,1)S(1)} %bitcast.4, ...), custom_call_target="tpu_custom_call" | custom-call | flops 4000000000 | bytes 4194304 | tf_op jit(solution)/shard_map/pallas_call | solution.py:119
  9.7 6.1 %collective-permute-start.14 = (bf16[384,128]{1,0:T(8,128)(2,1)S(1)}, bf16[384,128]{1,0:T(8,128)(2,1)S(1)}, u32[]{:S(2)}, u32[]{:S(2)}) collective-permute-start(bf16[384,128]{1,0:T(8,128)(2,1)S(1)} %get-tuple-element.61), channel_id=1, source_target_pairs={{0,14},{2,12},{4,10},{6,8},{8,6},{10,4},{12,2},{14,0},{1,15},{3,13... | collective-permute-start | bytes 294920 | tf_op jit(solution)/shard_map/ppermute | solution.py:375
  15.7 0.5 collective-permute-start.15
  16.2 0.2 collective-permute-start.16
  16.4 0.0 collective-permute-start.17
  16.4 0.0 copy-start.7
  16.4 0.0 copy-start.10
  16.4 5.3 %collective-permute-start.18 = (bf16[384,128]{1,0:T(8,128)(2,1)S(1)}, bf16[384,128]{1,0:T(8,128)(2,1)S(1)}, u32[]{:S(2)}, u32[]{:S(2)}) collective-permute-start(bf16[384,128]{1,0:T(8,128)(2,1)S(1)} %get-tuple-element.65), channel_id=1, source_target_pairs={{0,10},{2,8},{4,14},{6,12},{8,2},{10,0},{12,6},{14,4},{1,11},{3,9}... | collective-permute-start | bytes 294920 | tf_op jit(solution)/shard_map/ppermute | solution.py:375
  21.7 4.2 %shard_map.129 = (bf16[384,128]{1,0:T(8,128)(2,1)S(1)}, bf16[384,128]{1,0:T(8,128)(2,1)S(1)}, bf16[384,128]{1,0:T(8,128)(2,1)S(1)}, bf16[384,128]{1,0:T(8,128)(2...) custom-call(bf16[2,192,1440]{2,1,0:T(8,128)(2,1)S(1)} %bitcast.5, ...), custom_call_target="tpu_custom_call" | custom-call | flops 4000000000 | bytes 4194304 | tf_op jit(solution)/shard_map/pallas_call | solution.py:119
  25.9 0.0 collective-permute-done.14.refs_1_
  25.9 0.1 collective-permute-start.19
  26.0 0.7 collective-permute-start.20
  26.7 4.6 %collective-permute-start = (bf16[384,128]{1,0:T(8,128)(2,1)S(1)}, bf16[384,128]{1,0:T(8,128)(2,1)S(1)}, u32[]{:S(2)}, u32[]{:S(2)}) collective-permute-start(bf16[384,128]{1,0:T(8,128)(2,1)S(1)} %get-tuple-element.45), channel_id=1, source_target_pairs={{0,14},{2,12},{4,10},{6,8},{8,6},{10,4},{12,2},{14,0},{1,15},{3,13... | collective-permute-start | bytes 294920 | tf_op jit(solution)/shard_map/ppermute | solution.py:375
  31.2 0.5 collective-permute-start.1
  31.8 0.4 collective-permute-start.2
  32.2 0.6 collective-permute-done.19.refs_6_
  32.8 0.3 collective-permute-start.3
  33.1 6.2 %collective-permute-done.20.refs_7_ = bf16[384,128]{1,0:T(8,128)(2,1)S(1)} collective-permute-done((bf16[384,128]{1,0:T(8,128)(2,1)S(1)}, bf16[384,128]{1,0:T(8,128)(2,1)S(1)}, u32[]{:S(2)}, u32[]{:S(2)}) %collective-permute-start.20) | collective-permute-done | bytes 98336 | tf_op jit(solution)/shard_map/ppermute | solution.py:375
  39.4 3.7 %collective-permute-start.5 = (bf16[384,128]{1,0:T(8,128)(2,1)S(1)}, bf16[384,128]{1,0:T(8,128)(2,1)S(1)}, u32[]{:S(2)}, u32[]{:S(2)}) collective-permute-start(bf16[384,128]{1,0:T(8,128)(2,1)S(1)} %get-tuple-element.50), channel_id=1, source_target_pairs={{0,6},{2,4},{4,2},{6,0},{8,14},{10,12},{12,10},{14,8},{1,7},{3,5},... | collective-permute-start | bytes 294920 | tf_op jit(solution)/shard_map/ppermute | solution.py:375
  43.0 0.0 collective-permute-done.1.refs_2_
  43.1 6.5 %shard_map.132 = (bf16[432,128]{1,0:T(8,128)(2,1)S(1)}, bf16[432,128]{1,0:T(8,128)(2,1)S(1)}, bf16[432,128]{1,0:T(8,128)(2,1)S(1)}, bf16[432,128]{1,0:T(8,128)(2...) custom-call(bf16[384,128]{1,0:T(8,128)(2,1)S(1)} %get-tuple-element., ...), custom_call_target="tpu_custom_call" | custom-call | flops 7000000000 | bytes 4194304 | tf_op jit(solution)/shard_map/pallas_call | solution.py:349
  49.6 2.4 %collective-permute-start.21 = (bf16[432,128]{1,0:T(8,128)(2,1)S(1)}, bf16[432,128]{1,0:T(8,128)(2,1)S(1)}, u32[]{:S(2)}, u32[]{:S(2)}) collective-permute-start(bf16[432,128]{1,0:T(8,128)(2,1)S(1)} %get-tuple-element.69), channel_id=1, source_target_pairs={{0,14},{2,12},{4,10},{6,8},{8,6},{10,4},{12,2},{14,0},{1,15},{3,13... | collective-permute-start | bytes 331784 | tf_op jit(solution)/shard_map/ppermute | solution.py:375
  52.1 1.0 %collective-permute-start.22 = (bf16[432,128]{1,0:T(8,128)(2,1)S(1)}, bf16[432,128]{1,0:T(8,128)(2,1)S(1)}, u32[]{:S(2)}, u32[]{:S(2)}) collective-permute-start(bf16[432,128]{1,0:T(8,128)(2,1)S(1)} %get-tuple-element.70), channel_id=1, source_target_pairs={{0,2},{2,0},{4,6},{6,4},{8,10},{10,8},{12,14},{14,12},{1,3},{3,1},... | collective-permute-start | bytes 331784 | tf_op jit(solution)/shard_map/ppermute | solution.py:375
  53.1 1.9 %collective-permute-start.23 = (bf16[432,128]{1,0:T(8,128)(2,1)S(1)}, bf16[432,128]{1,0:T(8,128)(2,1)S(1)}, u32[]{:S(2)}, u32[]{:S(2)}) collective-permute-start(bf16[432,128]{1,0:T(8,128)(2,1)S(1)} %get-tuple-element.71), channel_id=1, source_target_pairs={{0,12},{2,14},{4,8},{6,10},{8,4},{10,6},{12,0},{14,2},{1,13},{3,15... | collective-permute-start | bytes 331784 | tf_op jit(solution)/shard_map/ppermute | solution.py:375
  55.0 0.0 collective-permute-done.5.refs_6_
  55.0 0.6 collective-permute-start.24
  55.6 2.3 %collective-permute-start.25 = (bf16[432,128]{1,0:T(8,128)(2,1)S(1)}, bf16[432,128]{1,0:T(8,128)(2,1)S(1)}, u32[]{:S(2)}, u32[]{:S(2)}) collective-permute-start(bf16[432,128]{1,0:T(8,128)(2,1)S(1)} %get-tuple-element.73), channel_id=1, source_target_pairs={{0,10},{2,8},{4,14},{6,12},{8,2},{10,0},{12,6},{14,4},{1,11},{3,9}... | collective-permute-start | bytes 331784 | tf_op jit(solution)/shard_map/ppermute | solution.py:375
  57.9 6.5 %shard_map.130 = (bf16[432,128]{1,0:T(8,128)(2,1)S(1)}, bf16[432,128]{1,0:T(8,128)(2,1)S(1)}, bf16[432,128]{1,0:T(8,128)(2,1)S(1)}, bf16[432,128]{1,0:T(8,128)(2...) custom-call(bf16[384,128]{1,0:T(8,128)(2,1)S(1)} %get-tuple-element., ...), custom_call_target="tpu_custom_call" | custom-call | flops 7000000000 | bytes 4194304 | tf_op jit(solution)/shard_map/pallas_call | solution.py:349
  64.5 1.2 %collective-permute-start.26 = (bf16[432,128]{1,0:T(8,128)(2,1)S(1)}, bf16[432,128]{1,0:T(8,128)(2,1)S(1)}, u32[]{:S(2)}, u32[]{:S(2)}) collective-permute-start(bf16[432,128]{1,0:T(8,128)(2,1)S(1)} %get-tuple-element.74), channel_id=1, source_target_pairs={{0,6},{2,4},{4,2},{6,0},{8,14},{10,12},{12,10},{14,8},{1,7},{3,5},... | collective-permute-start | bytes 331784 | tf_op jit(solution)/shard_map/ppermute | solution.py:375
  65.7 0.0 collective-permute-done.22.refs_2_
  65.7 1.8 %collective-permute-start.27 = (bf16[432,128]{1,0:T(8,128)(2,1)S(1)}, bf16[432,128]{1,0:T(8,128)(2,1)S(1)}, u32[]{:S(2)}, u32[]{:S(2)}) collective-permute-start(bf16[432,128]{1,0:T(8,128)(2,1)S(1)} %get-tuple-element.75), channel_id=1, source_target_pairs={{0,8},{2,10},{4,12},{6,14},{8,0},{10,2},{12,4},{14,6},{1,9},{3,11}... | collective-permute-start | bytes 331784 | tf_op jit(solution)/shard_map/ppermute | solution.py:375
  67.5 0.0 collective-permute-done.23.refs_3_
  67.5 2.3 %collective-permute-start.7 = (bf16[432,128]{1,0:T(8,128)(2,1)S(1)}, bf16[432,128]{1,0:T(8,128)(2,1)S(1)}, u32[]{:S(2)}, u32[]{:S(2)}) collective-permute-start(bf16[432,128]{1,0:T(8,128)(2,1)S(1)} %get-tuple-element.53), channel_id=1, source_target_pairs={{0,14},{2,12},{4,10},{6,8},{8,6},{10,4},{12,2},{14,0},{1,15},{3,13... | collective-permute-start | bytes 331784 | tf_op jit(solution)/shard_map/ppermute | solution.py:375
  69.9 0.0 collective-permute-done.24.refs_4_
  69.9 1.0 %collective-permute-start.8 = (bf16[432,128]{1,0:T(8,128)(2,1)S(1)}, bf16[432,128]{1,0:T(8,128)(2,1)S(1)}, u32[]{:S(2)}, u32[]{:S(2)}) collective-permute-start(bf16[432,128]{1,0:T(8,128)(2,1)S(1)} %get-tuple-element.54), channel_id=1, source_target_pairs={{0,2},{2,0},{4,6},{6,4},{8,10},{10,8},{12,14},{14,12},{1,3},{3,1},... | collective-permute-start | bytes 331784 | tf_op jit(solution)/shard_map/ppermute | solution.py:375
  70.9 0.0 collective-permute-done.25.refs_5_
  70.9 1.9 %collective-permute-start.9 = (bf16[432,128]{1,0:T(8,128)(2,1)S(1)}, bf16[432,128]{1,0:T(8,128)(2,1)S(1)}, u32[]{:S(2)}, u32[]{:S(2)}) collective-permute-start(bf16[432,128]{1,0:T(8,128)(2,1)S(1)} %get-tuple-element.55), channel_id=1, source_target_pairs={{0,12},{2,14},{4,8},{6,10},{8,4},{10,6},{12,0},{14,2},{1,13},{3,15... | collective-permute-start | bytes 331784 | tf_op jit(solution)/shard_map/ppermute | solution.py:375
  72.8 5.7 %collective-permute-done.27.refs_7_ = bf16[432,128]{1,0:T(8,128)(2,1)S(1)} collective-permute-done((bf16[432,128]{1,0:T(8,128)(2,1)S(1)}, bf16[432,128]{1,0:T(8,128)(2,1)S(1)}, u32[]{:S(2)}, u32[]{:S(2)}) %collective-permute-start.27) | collective-permute-done | bytes 110624 | tf_op jit(solution)/shard_map/ppermute | solution.py:375
  78.5 6.3 %collective-permute-start.12 = (bf16[432,128]{1,0:T(8,128)(2,1)S(1)}, bf16[432,128]{1,0:T(8,128)(2,1)S(1)}, u32[]{:S(2)}, u32[]{:S(2)}) collective-permute-start(bf16[432,128]{1,0:T(8,128)(2,1)S(1)} %get-tuple-element.58), channel_id=1, source_target_pairs={{0,6},{2,4},{4,2},{6,0},{8,14},{10,12},{12,10},{14,8},{1,7},{3,5},... | collective-permute-start | bytes 331784 | tf_op jit(solution)/shard_map/ppermute | solution.py:375
  84.8 3.0 %shard_map.133 = (bf16[2,192,1440]{2,1,0:T(8,128)(2,1)}, bf16[2,192,1440]{2,1,0:T(8,128)(2,1)}, f32[2,2304]{1,0:T(2,128)S(1)}, f32[2,2304]{1,0:T(2,128)S(1)}) custom-call(bf16[432,128]{1,0:T(8,128)(2,1)S(1)} %get-tuple-element.68.refs_0_, bf16[432,128]{1,0:T(8,128)(2,1)S(1)} %collective-permute-done.21.refs_1_, ...), custom_call_target="tpu_custom_call" | custom-call | flops 4000000000 | bytes 5242880 | tf_op jit(solution)/shard_map/pallas_call | solution.py:197
  87.8 0.2 collective-permute-done.12.refs_6_
  88.0 2.4 %collective-permute-done.13.refs_7_ = bf16[432,128]{1,0:T(8,128)(2,1)S(1)} collective-permute-done((bf16[432,128]{1,0:T(8,128)(2,1)S(1)}, bf16[432,128]{1,0:T(8,128)(2,1)S(1)}, u32[]{:S(2)}, u32[]{:S(2)}) %collective-permute-start.13) | collective-permute-done | bytes 110624 | tf_op jit(solution)/shard_map/ppermute | solution.py:375
  90.4 3.0 %shard_map.134 = (bf16[2,192,1440]{2,1,0:T(8,128)(2,1)}, bf16[2,192,1440]{2,1,0:T(8,128)(2,1)}, f32[2,2304]{1,0:T(2,128)}, f32[2,2304]{1,0:T(2,128)}) custom-call(bf16[432,128]{1,0:T(8,128)(2,1)S(1)} %get-tuple-element.52.refs_0_, bf16[432,128]{1,0:T(8,128)(2,1)S(1)} %collective-permute-done.7.refs_1_, ...), custom_call_target="tpu_custom_call", output_to_operand_aliasing={{0}: (12, {}), {1}: (13, {})} | custom-call | flops 4000000000 | bytes 5242880 | tf_op jit(solution)/shard_map/pallas_call | solution.py:197
  (38 shorter events, 0.1 us)
Async XLA Ops:
  0.6 1.3 %copy-start = (bf16[2,1440,192]{1,2,0:T(8,128)(2,1)S(1)}, bf16[2,1440,192]{1,2,0:T(8,128)(2,1)}, u32[]{:S(2)}) copy-start(bf16[2,1440,192]{1,2,0:T(8,128)(2,1)} %param.10) | copy-start | bytes 3317764
  1.9 1.3 %copy-start.2 = (bf16[2,1440,192]{1,2,0:T(8,128)(2,1)S(1)}, bf16[2,1440,192]{1,2,0:T(8,128)(2,1)}, u32[]{:S(2)}) copy-start(bf16[2,1440,192]{1,2,0:T(8,128)(2,1)} %param.11) | copy-start | bytes 3317764
  3.2 1.8 %copy-start.9 = (bf16[1440,1024]{1,0:T(8,128)(2,1)S(1)}, bf16[1440,1024]{1,0:T(8,128)(2,1)}, u32[]{:S(2)}) copy-start(bf16[1440,1024]{1,0:T(8,128)(2,1)} %constant.8.clone.table_ref) | copy-start | bytes 8847364
  5.0 0.7 copy-start.11
  9.7 16.2 %collective-permute-start.14 = (bf16[384,128]{1,0:T(8,128)(2,1)S(1)}, bf16[384,128]{1,0:T(8,128)(2,1)S(1)}, u32[]{:S(2)}, u32[]{:S(2)}) collective-permute-start(bf16[384,128]{1,0:T(8,128)(2,1)S(1)} %get-tuple-element.61), channel_id=1, source_target_pairs={{0,14},{2,12},{4,10},{6,8},{8,6},{10,4},{12,2},{14,0},{1,15},{3,13... | collective-permute-start | bytes 294920 | tf_op jit(solution)/shard_map/ppermute | solution.py:375
  15.7 10.2 %collective-permute-start.15 = (bf16[384,128]{1,0:T(8,128)(2,1)S(1)}, bf16[384,128]{1,0:T(8,128)(2,1)S(1)}, u32[]{:S(2)}, u32[]{:S(2)}) collective-permute-start(bf16[384,128]{1,0:T(8,128)(2,1)S(1)} %get-tuple-element.62), channel_id=1, source_target_pairs={{0,2},{2,0},{4,6},{6,4},{8,10},{10,8},{12,14},{14,12},{1,3},{3,1},... | collective-permute-start | bytes 294920 | tf_op jit(solution)/shard_map/ppermute | solution.py:375
  16.2 10.4 %collective-permute-start.16 = (bf16[384,128]{1,0:T(8,128)(2,1)S(1)}, bf16[384,128]{1,0:T(8,128)(2,1)S(1)}, u32[]{:S(2)}, u32[]{:S(2)}) collective-permute-start(bf16[384,128]{1,0:T(8,128)(2,1)S(1)} %get-tuple-element.63), channel_id=1, source_target_pairs={{0,12},{2,14},{4,8},{6,10},{8,4},{10,6},{12,0},{14,2},{1,13},{3,15... | collective-permute-start | bytes 294920 | tf_op jit(solution)/shard_map/ppermute | solution.py:375
  16.4 14.9 %collective-permute-start.17 = (bf16[384,128]{1,0:T(8,128)(2,1)S(1)}, bf16[384,128]{1,0:T(8,128)(2,1)S(1)}, u32[]{:S(2)}, u32[]{:S(2)}) collective-permute-start(bf16[384,128]{1,0:T(8,128)(2,1)S(1)} %get-tuple-element.64), channel_id=1, source_target_pairs={{0,4},{2,6},{4,0},{6,2},{8,12},{10,14},{12,8},{14,10},{1,5},{3,7},... | collective-permute-start | bytes 294920 | tf_op jit(solution)/shard_map/ppermute | solution.py:375
  16.4 26.6 %copy-start.4 = (bf16[4,96,192]{2,1,0:T(8,128)(2,1)S(1)}, bf16[4,96,192]{2,1,0:T(8,128)(2,1)}, u32[]{:S(2)}) copy-start(bf16[4,96,192]{2,1,0:T(8,128)(2,1)} %refs_9_.5) | copy-start | bytes 442372
  16.4 26.6 %copy-start.5 = (bf16[4,96,192]{2,1,0:T(8,128)(2,1)S(1)}, bf16[4,96,192]{2,1,0:T(8,128)(2,1)}, u32[]{:S(2)}) copy-start(bf16[4,96,192]{2,1,0:T(8,128)(2,1)} %refs_11_.3) | copy-start | bytes 442372
  16.4 26.6 %copy-start.6 = (f32[4,192]{1,0:T(4,128)S(1)}, f32[4,192]{1,0:T(4,128)}, u32[]{:S(2)}) copy-start(f32[4,192]{1,0:T(4,128)} %refs_10_.3) | copy-start | bytes 9220
  16.4 26.7 %copy-start.7 = (f32[4,192]{1,0:T(4,128)S(1)}, f32[4,192]{1,0:T(4,128)}, u32[]{:S(2)}) copy-start(f32[4,192]{1,0:T(4,128)} %refs_12_.3) | copy-start | bytes 9220
  16.4 26.7 %copy-start.10 = (bf16[256,512]{1,0:T(8,128)(2,1)S(1)}, bf16[256,512]{1,0:T(8,128)(2,1)}, u32[]{:S(2)}) copy-start(bf16[256,512]{1,0:T(8,128)(2,1)} %constant.11.clone.refs_8_) | copy-start | bytes 786436
  16.4 15.4 %collective-permute-start.18 = (bf16[384,128]{1,0:T(8,128)(2,1)S(1)}, bf16[384,128]{1,0:T(8,128)(2,1)S(1)}, u32[]{:S(2)}, u32[]{:S(2)}) collective-permute-start(bf16[384,128]{1,0:T(8,128)(2,1)S(1)} %get-tuple-element.65), channel_id=1, source_target_pairs={{0,10},{2,8},{4,14},{6,12},{8,2},{10,0},{12,6},{14,4},{1,11},{3,9}... | collective-permute-start | bytes 294920 | tf_op jit(solution)/shard_map/ppermute | solution.py:375
  25.9 6.9 %collective-permute-start.19 = (bf16[384,128]{1,0:T(8,128)(2,1)S(1)}, bf16[384,128]{1,0:T(8,128)(2,1)S(1)}, u32[]{:S(2)}, u32[]{:S(2)}) collective-permute-start(bf16[384,128]{1,0:T(8,128)(2,1)S(1)} %get-tuple-element.66), channel_id=1, source_target_pairs={{0,6},{2,4},{4,2},{6,0},{8,14},{10,12},{12,10},{14,8},{1,7},{3,5},... | collective-permute-start | bytes 294920 | tf_op jit(solution)/shard_map/ppermute | solution.py:375
  26.0 13.4 %collective-permute-start.20 = (bf16[384,128]{1,0:T(8,128)(2,1)S(1)}, bf16[384,128]{1,0:T(8,128)(2,1)S(1)}, u32[]{:S(2)}, u32[]{:S(2)}) collective-permute-start(bf16[384,128]{1,0:T(8,128)(2,1)S(1)} %get-tuple-element.67), channel_id=1, source_target_pairs={{0,8},{2,10},{4,12},{6,14},{8,0},{10,2},{12,4},{14,6},{1,9},{3,11}... | collective-permute-start | bytes 294920 | tf_op jit(solution)/shard_map/ppermute | solution.py:375
  26.7 12.7 %collective-permute-start = (bf16[384,128]{1,0:T(8,128)(2,1)S(1)}, bf16[384,128]{1,0:T(8,128)(2,1)S(1)}, u32[]{:S(2)}, u32[]{:S(2)}) collective-permute-start(bf16[384,128]{1,0:T(8,128)(2,1)S(1)} %get-tuple-element.45), channel_id=1, source_target_pairs={{0,14},{2,12},{4,10},{6,8},{8,6},{10,4},{12,2},{14,0},{1,15},{3,13... | collective-permute-start | bytes 294920 | tf_op jit(solution)/shard_map/ppermute | solution.py:375
  31.2 11.8 %collective-permute-start.1 = (bf16[384,128]{1,0:T(8,128)(2,1)S(1)}, bf16[384,128]{1,0:T(8,128)(2,1)S(1)}, u32[]{:S(2)}, u32[]{:S(2)}) collective-permute-start(bf16[384,128]{1,0:T(8,128)(2,1)S(1)} %get-tuple-element.46), channel_id=1, source_target_pairs={{0,2},{2,0},{4,6},{6,4},{8,10},{10,8},{12,14},{14,12},{1,3},{3,1},... | collective-permute-start | bytes 294920 | tf_op jit(solution)/shard_map/ppermute | solution.py:375
  31.8 17.8 %collective-permute-start.2 = (bf16[384,128]{1,0:T(8,128)(2,1)S(1)}, bf16[384,128]{1,0:T(8,128)(2,1)S(1)}, u32[]{:S(2)}, u32[]{:S(2)}) collective-permute-start(bf16[384,128]{1,0:T(8,128)(2,1)S(1)} %get-tuple-element.47), channel_id=1, source_target_pairs={{0,12},{2,14},{4,8},{6,10},{8,4},{10,6},{12,0},{14,2},{1,13},{3,15... | collective-permute-start | bytes 294920 | tf_op jit(solution)/shard_map/ppermute | solution.py:375
  32.8 19.3 %collective-permute-start.3 = (bf16[384,128]{1,0:T(8,128)(2,1)S(1)}, bf16[384,128]{1,0:T(8,128)(2,1)S(1)}, u32[]{:S(2)}, u32[]{:S(2)}) collective-permute-start(bf16[384,128]{1,0:T(8,128)(2,1)S(1)} %get-tuple-element.48), channel_id=1, source_target_pairs={{0,4},{2,6},{4,0},{6,2},{8,12},{10,14},{12,8},{14,10},{1,5},{3,7},... | collective-permute-start | bytes 294920 | tf_op jit(solution)/shard_map/ppermute | solution.py:375
  39.4 13.7 %collective-permute-start.4 = (bf16[384,128]{1,0:T(8,128)(2,1)S(1)}, bf16[384,128]{1,0:T(8,128)(2,1)S(1)}, u32[]{:S(2)}, u32[]{:S(2)}) collective-permute-start(bf16[384,128]{1,0:T(8,128)(2,1)S(1)} %get-tuple-element.49), channel_id=1, source_target_pairs={{0,10},{2,8},{4,14},{6,12},{8,2},{10,0},{12,6},{14,4},{1,11},{3,9}... | collective-permute-start | bytes 294920 | tf_op jit(solution)/shard_map/ppermute | solution.py:375
  39.4 15.6 %collective-permute-start.5 = (bf16[384,128]{1,0:T(8,128)(2,1)S(1)}, bf16[384,128]{1,0:T(8,128)(2,1)S(1)}, u32[]{:S(2)}, u32[]{:S(2)}) collective-permute-start(bf16[384,128]{1,0:T(8,128)(2,1)S(1)} %get-tuple-element.50), channel_id=1, source_target_pairs={{0,6},{2,4},{4,2},{6,0},{8,14},{10,12},{12,10},{14,8},{1,7},{3,5},... | collective-permute-start | bytes 294920 | tf_op jit(solution)/shard_map/ppermute | solution.py:375
  43.0 12.6 %collective-permute-start.6 = (bf16[384,128]{1,0:T(8,128)(2,1)S(1)}, bf16[384,128]{1,0:T(8,128)(2,1)S(1)}, u32[]{:S(2)}, u32[]{:S(2)}) collective-permute-start(bf16[384,128]{1,0:T(8,128)(2,1)S(1)} %get-tuple-element.51), channel_id=1, source_target_pairs={{0,8},{2,10},{4,12},{6,14},{8,0},{10,2},{12,4},{14,6},{1,9},{3,11}... | collective-permute-start | bytes 294920 | tf_op jit(solution)/shard_map/ppermute | solution.py:375
  49.6 14.8 %collective-permute-start.21 = (bf16[432,128]{1,0:T(8,128)(2,1)S(1)}, bf16[432,128]{1,0:T(8,128)(2,1)S(1)}, u32[]{:S(2)}, u32[]{:S(2)}) collective-permute-start(bf16[432,128]{1,0:T(8,128)(2,1)S(1)} %get-tuple-element.69), channel_id=1, source_target_pairs={{0,14},{2,12},{4,10},{6,8},{8,6},{10,4},{12,2},{14,0},{1,15},{3,13... | collective-permute-start | bytes 331784 | tf_op jit(solution)/shard_map/ppermute | solution.py:375
  52.1 13.6 %collective-permute-start.22 = (bf16[432,128]{1,0:T(8,128)(2,1)S(1)}, bf16[432,128]{1,0:T(8,128)(2,1)S(1)}, u32[]{:S(2)}, u32[]{:S(2)}) collective-permute-start(bf16[432,128]{1,0:T(8,128)(2,1)S(1)} %get-tuple-element.70), channel_id=1, source_target_pairs={{0,2},{2,0},{4,6},{6,4},{8,10},{10,8},{12,14},{14,12},{1,3},{3,1},... | collective-permute-start | bytes 331784 | tf_op jit(solution)/shard_map/ppermute | solution.py:375
  53.1 14.5 %collective-permute-start.23 = (bf16[432,128]{1,0:T(8,128)(2,1)S(1)}, bf16[432,128]{1,0:T(8,128)(2,1)S(1)}, u32[]{:S(2)}, u32[]{:S(2)}) collective-permute-start(bf16[432,128]{1,0:T(8,128)(2,1)S(1)} %get-tuple-element.71), channel_id=1, source_target_pairs={{0,12},{2,14},{4,8},{6,10},{8,4},{10,6},{12,0},{14,2},{1,13},{3,15... | collective-permute-start | bytes 331784 | tf_op jit(solution)/shard_map/ppermute | solution.py:375
  55.0 14.9 %collective-permute-start.24 = (bf16[432,128]{1,0:T(8,128)(2,1)S(1)}, bf16[432,128]{1,0:T(8,128)(2,1)S(1)}, u32[]{:S(2)}, u32[]{:S(2)}) collective-permute-start(bf16[432,128]{1,0:T(8,128)(2,1)S(1)} %get-tuple-element.72), channel_id=1, source_target_pairs={{0,4},{2,6},{4,0},{6,2},{8,12},{10,14},{12,8},{14,10},{1,5},{3,7},... | collective-permute-start | bytes 331784 | tf_op jit(solution)/shard_map/ppermute | solution.py:375
  55.6 15.2 %collective-permute-start.25 = (bf16[432,128]{1,0:T(8,128)(2,1)S(1)}, bf16[432,128]{1,0:T(8,128)(2,1)S(1)}, u32[]{:S(2)}, u32[]{:S(2)}) collective-permute-start(bf16[432,128]{1,0:T(8,128)(2,1)S(1)} %get-tuple-element.73), channel_id=1, source_target_pairs={{0,10},{2,8},{4,14},{6,12},{8,2},{10,0},{12,6},{14,4},{1,11},{3,9}... | collective-permute-start | bytes 331784 | tf_op jit(solution)/shard_map/ppermute | solution.py:375
  57.9 26.8 %copy-start.1 = (bf16[2,1440,192]{1,2,0:T(8,128)(2,1)S(1)}, bf16[2,1440,192]{1,2,0:T(8,128)(2,1)}, u32[]{:S(2)}) copy-start(bf16[2,1440,192]{1,2,0:T(8,128)(2,1)} %param.10) | copy-start | bytes 3317764
  57.9 26.8 %copy-start.3 = (bf16[2,1440,192]{1,2,0:T(8,128)(2,1)S(1)}, bf16[2,1440,192]{1,2,0:T(8,128)(2,1)}, u32[]{:S(2)}) copy-start(bf16[2,1440,192]{1,2,0:T(8,128)(2,1)} %param.11) | copy-start | bytes 3317764
  57.9 26.8 %copy-start.8 = (bf16[1024,1440]{1,0:T(8,128)(2,1)S(1)}, bf16[1024,1440]{1,0:T(8,128)(2,1)}, u32[]{:S(2)}) copy-start(bf16[1024,1440]{1,0:T(8,128)(2,1)} %constant.9.clone.refs_8_) | copy-start | bytes 8847364
  64.5 8.3 %collective-permute-start.26 = (bf16[432,128]{1,0:T(8,128)(2,1)S(1)}, bf16[432,128]{1,0:T(8,128)(2,1)S(1)}, u32[]{:S(2)}, u32[]{:S(2)}) collective-permute-start(bf16[432,128]{1,0:T(8,128)(2,1)S(1)} %get-tuple-element.74), channel_id=1, source_target_pairs={{0,6},{2,4},{4,2},{6,0},{8,14},{10,12},{12,10},{14,8},{1,7},{3,5},... | collective-permute-start | bytes 331784 | tf_op jit(solution)/shard_map/ppermute | solution.py:375
  65.7 12.8 %collective-permute-start.27 = (bf16[432,128]{1,0:T(8,128)(2,1)S(1)}, bf16[432,128]{1,0:T(8,128)(2,1)S(1)}, u32[]{:S(2)}, u32[]{:S(2)}) collective-permute-start(bf16[432,128]{1,0:T(8,128)(2,1)S(1)} %get-tuple-element.75), channel_id=1, source_target_pairs={{0,8},{2,10},{4,12},{6,14},{8,0},{10,2},{12,4},{14,6},{1,9},{3,11}... | collective-permute-start | bytes 331784 | tf_op jit(solution)/shard_map/ppermute | solution.py:375
  67.5 11.0 %collective-permute-start.7 = (bf16[432,128]{1,0:T(8,128)(2,1)S(1)}, bf16[432,128]{1,0:T(8,128)(2,1)S(1)}, u32[]{:S(2)}, u32[]{:S(2)}) collective-permute-start(bf16[432,128]{1,0:T(8,128)(2,1)S(1)} %get-tuple-element.53), channel_id=1, source_target_pairs={{0,14},{2,12},{4,10},{6,8},{8,6},{10,4},{12,2},{14,0},{1,15},{3,13... | collective-permute-start | bytes 331784 | tf_op jit(solution)/shard_map/ppermute | solution.py:375
  69.9 14.9 %collective-permute-start.8 = (bf16[432,128]{1,0:T(8,128)(2,1)S(1)}, bf16[432,128]{1,0:T(8,128)(2,1)S(1)}, u32[]{:S(2)}, u32[]{:S(2)}) collective-permute-start(bf16[432,128]{1,0:T(8,128)(2,1)S(1)} %get-tuple-element.54), channel_id=1, source_target_pairs={{0,2},{2,0},{4,6},{6,4},{8,10},{10,8},{12,14},{14,12},{1,3},{3,1},... | collective-permute-start | bytes 331784 | tf_op jit(solution)/shard_map/ppermute | solution.py:375
  70.9 17.0 %collective-permute-start.9 = (bf16[432,128]{1,0:T(8,128)(2,1)S(1)}, bf16[432,128]{1,0:T(8,128)(2,1)S(1)}, u32[]{:S(2)}, u32[]{:S(2)}) collective-permute-start(bf16[432,128]{1,0:T(8,128)(2,1)S(1)} %get-tuple-element.55), channel_id=1, source_target_pairs={{0,12},{2,14},{4,8},{6,10},{8,4},{10,6},{12,0},{14,2},{1,13},{3,15... | collective-permute-start | bytes 331784 | tf_op jit(solution)/shard_map/ppermute | solution.py:375
  72.8 15.0 %collective-permute-start.10 = (bf16[432,128]{1,0:T(8,128)(2,1)S(1)}, bf16[432,128]{1,0:T(8,128)(2,1)S(1)}, u32[]{:S(2)}, u32[]{:S(2)}) collective-permute-start(bf16[432,128]{1,0:T(8,128)(2,1)S(1)} %get-tuple-element.56), channel_id=1, source_target_pairs={{0,4},{2,6},{4,0},{6,2},{8,12},{10,14},{12,8},{14,10},{1,5},{3,7},... | collective-permute-start | bytes 331784 | tf_op jit(solution)/shard_map/ppermute | solution.py:375
  78.5 9.3 %collective-permute-start.11 = (bf16[432,128]{1,0:T(8,128)(2,1)S(1)}, bf16[432,128]{1,0:T(8,128)(2,1)S(1)}, u32[]{:S(2)}, u32[]{:S(2)}) collective-permute-start(bf16[432,128]{1,0:T(8,128)(2,1)S(1)} %get-tuple-element.57), channel_id=1, source_target_pairs={{0,10},{2,8},{4,14},{6,12},{8,2},{10,0},{12,6},{14,4},{1,11},{3,9}... | collective-permute-start | bytes 331784 | tf_op jit(solution)/shard_map/ppermute | solution.py:375
  78.5 9.5 %collective-permute-start.12 = (bf16[432,128]{1,0:T(8,128)(2,1)S(1)}, bf16[432,128]{1,0:T(8,128)(2,1)S(1)}, u32[]{:S(2)}, u32[]{:S(2)}) collective-permute-start(bf16[432,128]{1,0:T(8,128)(2,1)S(1)} %get-tuple-element.58), channel_id=1, source_target_pairs={{0,6},{2,4},{4,2},{6,0},{8,14},{10,12},{12,10},{14,8},{1,7},{3,5},... | collective-permute-start | bytes 331784 | tf_op jit(solution)/shard_map/ppermute | solution.py:375
  84.7 5.6 %collective-permute-start.13 = (bf16[432,128]{1,0:T(8,128)(2,1)S(1)}, bf16[432,128]{1,0:T(8,128)(2,1)S(1)}, u32[]{:S(2)}, u32[]{:S(2)}) collective-permute-start(bf16[432,128]{1,0:T(8,128)(2,1)S(1)} %get-tuple-element.59), channel_id=1, source_target_pairs={{0,8},{2,10},{4,12},{6,14},{8,0},{10,2},{12,4},{14,6},{1,9},{3,11}... | collective-permute-start | bytes 331784 | tf_op jit(solution)/shard_map/ppermute | solution.py:375

commit v4 on v2

--- a/solution.py
+++ b/solution.py
@@ -52,10 +52,10 @@
     return jnp.dot(former, latter, preferred_element_type=F32)
 
 
-def swap_parts(values, first_sign):
+def with_swapped(values, first_sign):
     lane = lax.broadcasted_iota(jnp.int32, (1, LANES), 1)
-    sign = jnp.where(lane < HALF, first_sign, -first_sign).astype(F32)
-    return pltpu.roll(values, HALF, axis=1) * sign
+    sign = jnp.where(lane < HALF, first_sign, -first_sign).astype(values.dtype)
+    return jnp.concatenate([values, pltpu.roll(values, HALF, axis=1) * sign], axis=0)
 
 
 def slots(pieces):
@@ -82,7 +82,7 @@
         rows_ref[half:] = cotangent_ref[...].reshape(half, col_count)
 
     odd = jnp.bitwise_and(mine_ref[0], 1)
-    result = mm(rows_ref[...], table_ref[...])
+    result = mm(rows_ref[...], table_ref[0])
     for piece in range(2):
         lanes = slice(piece * LANES, (piece + 1) * LANES)
         pair_ref[piece, :half] = result[:half, lanes].astype(BF16)
@@ -102,7 +102,7 @@
     wide = 2 * LANES
 
     def block_of(i, place):
-        return (0, jnp.bitwise_xor(lax.shift_right_logical(place[0], 1), i))
+        return jnp.bitwise_xor(lax.shift_right_logical(place[0], 1), i)
 
     own = pl.BlockSpec((lines, width, col_count), lambda i, place: (0, group, 0))
     return pl.pallas_call(
@@ -113,14 +113,14 @@
             in_specs=[
                 own,
                 own,
-                pl.BlockSpec((col_count, wide), block_of),
-                pl.BlockSpec((1, wide), block_of),
+                pl.BlockSpec((1, col_count, wide), lambda i, place: (block_of(i, place), 0, 0)),
+                pl.BlockSpec((1, wide), lambda i, place: (0, block_of(i, place))),
             ],
             out_specs=[pl.BlockSpec((rows, LANES), lambda i, place: (0, 0)) for _ in range(pieces)],
             scratch_shapes=[pltpu.VMEM((rows, col_count), BF16), pltpu.VMEM((2, rows, LANES), BF16)],
         ),
         out_shape=[jax.ShapeDtypeStruct((rows, LANES), BF16) for _ in range(pieces)],
-        compiler_params=limits(ZONAL_MIB),
+        compiler_params=limits(ZONAL_MIB if group == 0 else MIDDLE_MIB),
         cost_estimate=pl.CostEstimate(flops=4 * 10**9, bytes_accessed=4 * MIB, transcendentals=0),
     )(mine, field, cotangent, table, scale)
 
@@ -208,26 +208,16 @@
 
 
 def meridian(load, mixer, first_sign, channels, store):
-    count = mixer.shape[1] // PACK
+    count = mixer.shape[0] // PACK
     for start in range(0, channels, 2 * PACK):
-        pair = jnp.concatenate(
-            [load(start + shift).reshape(count * PACK, LANES) for shift in (0, PACK)], axis=1
-        )
-        both = mm(mixer[...], pair)
+        pair = [
+            with_swapped(load(start + shift).reshape(count * PACK, LANES), first_sign)
+            for shift in (0, PACK)
+        ]
+        both = mm(mixer[...], side_by_side(pair))
         for index in range(2):
-            half = both[:, index * LANES : (index + 1) * LANES]
-            value = half[: count * PACK] + swap_parts(half[count * PACK :], first_sign)
+            value = both[:, index * LANES : (index + 1) * LANES]
             store(start + index * PACK, value.reshape(count, PACK, LANES))
-
-
-def complex_dot(weights, operand, first_sign):
-    width = weights.shape[0] // 2
-    both = mm(weights, jnp.concatenate(operand, axis=1))
-    return [
-        both[:width, i * LANES : (i + 1) * LANES]
-        + swap_parts(both[width:, i * LANES : (i + 1) * LANES], first_sign)
-        for i in range(len(operand))
-    ]
 
 
 def nt(former, latter):
@@ -245,9 +235,10 @@
     return jnp.where(lane < HALF, tall[:width], tall[width:])
 
 
-def stacked(weight):
+def forth(weight):
     width = weight.shape[0]
-    return jnp.concatenate([weight[:, :width], weight[:, width:]], axis=0)
+    turned = weight.T
+    return side_by_side([turned[:width], turned[width:]])
 
 
 def middle_kernel(group, groups, normalizer, pieces, *refs):
@@ -266,8 +257,7 @@
             adjoint_ref[row] = block[(lines + line) * width : (lines + line + 1) * width]
 
     first, second = first_ref[index], second_ref[index]
-    first_ahead, second_ahead = first.T, second.T
-    first_back, second_back = stacked(first), stacked(second)
+    first_ahead, second_ahead = forth(first), forth(second)
     first_bias, second_bias = bias_lanes(first_bias_ref, index), bias_lanes(second_bias_ref, index)
 
     def keep(start, value):
@@ -282,38 +272,39 @@
 
     first_sum = jnp.zeros((width, 2 * width), F32)
     second_sum = jnp.zeros((width, 2 * width), F32)
-    for row in range(0, count, 2):
-        both = range(2)
-        inputs = [harm_ref[row + i] for i in both]
-        pre = complex_dot(first_ahead, inputs, -1.0)
+    step = 4
+    for row in range(0, count, step):
+        members = range(step)
+
+        def lanes_of(wide):
+            return [wide[:, i * LANES : (i + 1) * LANES] for i in members]
+
+        inputs = [harm_ref[row + i] for i in members]
+        pre = lanes_of(mm(first_ahead, side_by_side([with_swapped(x, -1.0) for x in inputs])))
         hidden, slope = [], []
-        for i in both:
+        for i in members:
             v = pre[i] + first_bias
             square = v * v
-            tangent = jnp.tanh(GELU_SCALE * (v + GELU_CUBIC * square * v))
-            outer = 0.5 * (1.0 + tangent)
-            inner = GELU_SCALE * (1.0 + 3.0 * GELU_CUBIC * square)
+            tangent = jnp.tanh(v * (GELU_SCALE + GELU_SCALE * GELU_CUBIC * square))
+            outer = 0.5 + 0.5 * tangent
+            inner = 0.5 * GELU_SCALE + 1.5 * GELU_SCALE * GELU_CUBIC * square
             hidden.append((v * outer).astype(BF16))
-            slope.append(outer + 0.5 * v * (1.0 - tangent * tangent) * inner)
-        pre = complex_dot(second_ahead, hidden, -1.0)
-        exact = []
-        for i in both:
+            slope.append(outer + v * (1.0 - tangent * tangent) * inner)
+        pre = lanes_of(mm(second_ahead, side_by_side([with_swapped(x, -1.0) for x in hidden])))
+        second_adjoint = []
+        for i in members:
             v = pre[i] + second_bias
             squashed = jnp.tanh(v * (1.0 / SHRINK))
             shrunk_ref[row + i] = (v - SHRINK * squashed).astype(BF16)
-            exact.append(exact_ref[row + i] * (squashed * squashed))
-        second_adjoint = [a.astype(BF16) for a in exact]
-        turned = [swap_parts(a, 1.0).astype(BF16) for a in exact]
-        pairs = jnp.concatenate([side_by_side(second_adjoint), side_by_side(turned)], axis=0)
+            second_adjoint.append((exact_ref[row + i] * (squashed * squashed)).astype(BF16))
+        pairs = side_by_side([with_swapped(x, 1.0) for x in second_adjoint])
         second_sum += nt(side_by_side(hidden), pairs)
-        back = complex_dot(second_back, second_adjoint, 1.0)
-        exact = [back[i] * slope[i] for i in both]
-        first_adjoint = [a.astype(BF16) for a in exact]
-        turned = [swap_parts(a, 1.0).astype(BF16) for a in exact]
-        pairs = jnp.concatenate([side_by_side(first_adjoint), side_by_side(turned)], axis=0)
+        back = lanes_of(mm(second, pairs))
+        first_adjoint = [(back[i] * slope[i]).astype(BF16) for i in members]
+        pairs = side_by_side([with_swapped(x, 1.0) for x in first_adjoint])
         first_sum += nt(side_by_side(inputs), pairs)
-        back = complex_dot(first_back, first_adjoint, 1.0)
-        for i in both:
+        back = lanes_of(mm(first, pairs))
+        for i in members:
             harm_ref[row + i] = back[i].astype(BF16)
 
     sums_ref[0, :width] = first_sum * normalizer
@@ -405,9 +396,10 @@
     cosine, sines = meridian_waves(row_count)
     unit = np.eye(PACK, dtype=np.float32)
     mixer = np.concatenate(
-        [np.kron(cosine.astype(np.float32), unit), np.kron(sines.astype(np.float32), unit)], axis=0
+        [np.kron(cosine.astype(np.float32), unit), np.kron(sines.astype(np.float32), unit)], axis=1
     ).astype(BF16)
-    ahead, back = jnp.asarray(table), jnp.asarray(np.ascontiguousarray(table.T))
+    chunks = table.reshape(col_count, lat_count // 2, 2 * LANES).transpose(1, 0, 2)
+    ahead, back = jnp.asarray(np.ascontiguousarray(chunks)), jnp.asarray(np.ascontiguousarray(table.T))
     wide_factor = jnp.asarray(factor.reshape(1, 2 * KW))
     tall_factor = jnp.asarray(factor.reshape(lat_count, 2 * sub_count))
     mixer = jnp.asarray(mixer)

time: 91 us -> 86.2 us (0.947)
  Pallas kernels: 31.9 us -> 22.3 us
  starting transfers between devices: 43.8 us -> 46.4 us
  local copies, waits for them, and re-layouts: 0.07 us -> 1.88 us
    pallas_call x2, Pallas kernels: 15.3 us -> 8.54 us  [middle(): pl.pallas_call(functools.partial(middle_kernel, group, groups, normalizer...]
    pallas_call x2, Pallas kernels: 10.6 us -> 7.67 us  [zonal(): pl.pallas_call(zonal_kernel, grid_spec=pltpu.PrefetchScalarGridSpec(num_s...]
    ppermute x28, starting transfers between devices: 43.8 us -> 46.4 us  [pass_to(): lax.ppermute(block, 'lat', [(place, place ^ shift) for place in range(cou...]
    unnamed x26 -> x28, local copies, waits for them, and re-layouts: 0.07 us -> 1.88 us
  transfers between devices with their start and end apart: 28 -> 28, of which waited for: 7 -> 4; matrix products, arithmetic and copies ran while one was open for 0% -> 0% of each run, Pallas kernels for 26% -> 16%
where the time goes in v4:
time: 86.2 us; the launch traced here: 86 us
  starting transfers between devices  46.4 us (54%)
  Pallas kernels  22.3 us (26%)
  waiting for transfers between devices  14.6 us (17%)
  local copies, waits for them, and re-layouts  1.88 us (2%)
    ppermute x28, starting transfers between devices, pass_to(): lax.ppermute(block, 'lat', [(place, place ^ shift) for place in range(cou...  46.4 us
    ppermute x28, waiting for transfers between devices, pass_to(): lax.ppermute(block, 'lat', [(place, place ^ shift) for place in range(cou...  14.6 us
    pallas_call x2, Pallas kernels, middle(): pl.pallas_call(functools.partial(middle_kernel, group, groups, normalizer...  8.54 us
    pallas_call x2, Pallas kernels, zonal(): pl.pallas_call(zonal_kernel, grid_spec=pltpu.PrefetchScalarGridSpec(num_s...  7.67 us
    pallas_call x2, Pallas kernels, inverse(): pl.pallas_call(functools.partial(inverse_kernel, pieces, len(before), gro...  6.05 us
    unnamed x28, local copies, waits for them, and re-layouts  1.88 us
  transfers between devices with their start and end apart: 28, of which 4 were waited for; matrix products, arithmetic and copies ran while one was open for 0% of the time, Pallas kernels for 16%

profile of v4, /device:TPU:0, one launch (start us, length us, event | category | flops | bytes accessed | tf_op | source)
XLA Modules:
  0.0 86.0 jit_solution(6829695538532603359)
XLA Ops:
  0.7 0.0 copy-start.10
  0.7 5.4 %shard_map.140 = (bf16[384,128]{1,0:T(8,128)(2,1)}, bf16[384,128]{1,0:T(8,128)(2,1)}, bf16[384,128]{1,0:T(8,128)(2,1)}, bf16[384,128]{1,0:T(8,128)(2,1)}, bf16[3...) custom-call(s32[1]{0:T(128)} %bitcast.mine_ref, ...), custom_call_target="tpu_custom_call" | custom-call | flops 4000000000 | bytes 4194304 | tf_op jit(solution)/shard_map/pallas_call | solution.py:108
  6.1 6.0 %collective-permute-start.14 = (bf16[384,128]{1,0:T(8,128)(2,1)}, bf16[384,128]{1,0:T(8,128)(2,1)S(1)}, u32[]{:S(2)}, u32[]{:S(2)}) collective-permute-start(bf16[384,128]{1,0:T(8,128)(2,1)} %get-tuple-element.61), channel_id=1, source_target_pairs={{0,14},{2,12},{4,10},{6,8},{8,6},{10,4},{12,2},{14,0},{1,15},{3,13... | collective-permute-start | bytes 294920 | tf_op jit(solution)/shard_map/ppermute | solution.py:367
  12.1 0.5 collective-permute-start.15
  12.6 0.1 collective-permute-start.16
  12.7 0.0 collective-permute-start.17
  12.7 0.0 copy-start.5
  12.7 5.3 %collective-permute-start.18 = (bf16[384,128]{1,0:T(8,128)(2,1)}, bf16[384,128]{1,0:T(8,128)(2,1)S(1)}, u32[]{:S(2)}, u32[]{:S(2)}) collective-permute-start(bf16[384,128]{1,0:T(8,128)(2,1)} %get-tuple-element.65), channel_id=1, source_target_pairs={{0,10},{2,8},{4,14},{6,12},{8,2},{10,0},{12,6},{14,4},{1,11},{3,9}... | collective-permute-start | bytes 294920 | tf_op jit(solution)/shard_map/ppermute | solution.py:367
  18.0 1.8 %copy-done.7 = bf16[4,1440,256]{2,1,0:T(8,128)(2,1)S(1)} copy-done((bf16[4,1440,256]{2,1,0:T(8,128)(2,1)S(1)}, bf16[4,1440,256]{2,1,0:T(8,128)(2,1)}, u32[]{:S(2)}) %copy-start.7) | copy-done | bytes 2949144
  19.8 2.3 %shard_map.138 = (bf16[384,128]{1,0:T(8,128)(2,1)S(1)}, bf16[384,128]{1,0:T(8,128)(2,1)S(1)}, bf16[384,128]{1,0:T(8,128)(2,1)S(1)}, bf16[384,128]{1,0:T(8,128)(2...) custom-call(s32[1]{0:T(128)} %bitcast.mine_ref, ...), custom_call_target="tpu_custom_call" | custom-call | flops 4000000000 | bytes 4194304 | tf_op jit(solution)/shard_map/pallas_call | solution.py:108
  22.1 0.1 collective-permute-start.19
  22.2 0.0 collective-permute-done.15.refs_2_
  22.2 0.6 collective-permute-start.20
  22.9 0.0 collective-permute-done.16.refs_3_
  22.9 4.6 %collective-permute-start = (bf16[384,128]{1,0:T(8,128)(2,1)S(1)}, bf16[384,128]{1,0:T(8,128)(2,1)S(1)}, u32[]{:S(2)}, u32[]{:S(2)}) collective-permute-start(bf16[384,128]{1,0:T(8,128)(2,1)S(1)} %get-tuple-element.45), channel_id=1, source_target_pairs={{0,14},{2,12},{4,10},{6,8},{8,6},{10,4},{12,2},{14,0},{1,15},{3,13... | collective-permute-start | bytes 294920 | tf_op jit(solution)/shard_map/ppermute | solution.py:367
  27.5 0.5 collective-permute-start.1
  28.0 0.0 collective-permute-done.18.refs_5_
  28.0 1.0 %collective-permute-start.2 = (bf16[384,128]{1,0:T(8,128)(2,1)S(1)}, bf16[384,128]{1,0:T(8,128)(2,1)S(1)}, u32[]{:S(2)}, u32[]{:S(2)}) collective-permute-start(bf16[384,128]{1,0:T(8,128)(2,1)S(1)} %get-tuple-element.47), channel_id=1, source_target_pairs={{0,12},{2,14},{4,8},{6,10},{8,4},{10,6},{12,0},{14,2},{1,13},{3,15... | collective-permute-start | bytes 294920 | tf_op jit(solution)/shard_map/ppermute | solution.py:367
  29.0 0.7 collective-permute-start.3
  29.7 5.8 %collective-permute-done.20.refs_7_ = bf16[384,128]{1,0:T(8,128)(2,1)S(1)} collective-permute-done((bf16[384,128]{1,0:T(8,128)(2,1)S(1)}, bf16[384,128]{1,0:T(8,128)(2,1)S(1)}, u32[]{:S(2)}, u32[]{:S(2)}) %collective-permute-start.20) | collective-permute-done | bytes 98336 | tf_op jit(solution)/shard_map/ppermute | solution.py:367
  35.6 4.0 %collective-permute-start.5 = (bf16[384,128]{1,0:T(8,128)(2,1)S(1)}, bf16[384,128]{1,0:T(8,128)(2,1)S(1)}, u32[]{:S(2)}, u32[]{:S(2)}) collective-permute-start(bf16[384,128]{1,0:T(8,128)(2,1)S(1)} %get-tuple-element.50), channel_id=1, source_target_pairs={{0,6},{2,4},{4,2},{6,0},{8,14},{10,12},{12,10},{14,8},{1,7},{3,5},... | collective-permute-start | bytes 294920 | tf_op jit(solution)/shard_map/ppermute | solution.py:367
  39.5 0.0 collective-permute-done.1.refs_2_
  39.5 0.0 collective-permute-start.6
  39.6 4.3 %shard_map.141 = (bf16[432,128]{1,0:T(8,128)(2,1)S(1)}, bf16[432,128]{1,0:T(8,128)(2,1)S(1)}, bf16[432,128]{1,0:T(8,128)(2,1)S(1)}, bf16[432,128]{1,0:T(8,128)(2...) custom-call(bf16[384,128]{1,0:T(8,128)(2,1)S(1)} %copy-done.11, ...), custom_call_target="tpu_custom_call" | custom-call | flops 7000000000 | bytes 4194304 | tf_op jit(solution)/shard_map/pallas_call | solution.py:341
  43.9 0.0 collective-permute-done.2.refs_3_
  43.9 2.4 %collective-permute-start.21 = (bf16[432,128]{1,0:T(8,128)(2,1)S(1)}, bf16[432,128]{1,0:T(8,128)(2,1)S(1)}, u32[]{:S(2)}, u32[]{:S(2)}) collective-permute-start(bf16[432,128]{1,0:T(8,128)(2,1)S(1)} %get-tuple-element.69), channel_id=1, source_target_pairs={{0,14},{2,12},{4,10},{6,8},{8,6},{10,4},{12,2},{14,0},{1,15},{3,13... | collective-permute-start | bytes 331784 | tf_op jit(solution)/shard_map/ppermute | solution.py:367
  46.3 1.0 %collective-permute-start.22 = (bf16[432,128]{1,0:T(8,128)(2,1)S(1)}, bf16[432,128]{1,0:T(8,128)(2,1)S(1)}, u32[]{:S(2)}, u32[]{:S(2)}) collective-permute-start(bf16[432,128]{1,0:T(8,128)(2,1)S(1)} %get-tuple-element.70), channel_id=1, source_target_pairs={{0,2},{2,0},{4,6},{6,4},{8,10},{10,8},{12,14},{14,12},{1,3},{3,1},... | collective-permute-start | bytes 331784 | tf_op jit(solution)/shard_map/ppermute | solution.py:367
  47.3 0.0 collective-permute-done.4.refs_5_
  47.3 1.9 %collective-permute-start.23 = (bf16[432,128]{1,0:T(8,128)(2,1)S(1)}, bf16[432,128]{1,0:T(8,128)(2,1)S(1)}, u32[]{:S(2)}, u32[]{:S(2)}) collective-permute-start(bf16[432,128]{1,0:T(8,128)(2,1)S(1)} %get-tuple-element.71), channel_id=1, source_target_pairs={{0,12},{2,14},{4,8},{6,10},{8,4},{10,6},{12,0},{14,2},{1,13},{3,15... | collective-permute-start | bytes 331784 | tf_op jit(solution)/shard_map/ppermute | solution.py:367
  49.3 0.6 collective-permute-start.24
  49.9 0.0 collective-permute-done.6.refs_7_
  49.9 2.3 %collective-permute-start.25 = (bf16[432,128]{1,0:T(8,128)(2,1)S(1)}, bf16[432,128]{1,0:T(8,128)(2,1)S(1)}, u32[]{:S(2)}, u32[]{:S(2)}) collective-permute-start(bf16[432,128]{1,0:T(8,128)(2,1)S(1)} %get-tuple-element.73), channel_id=1, source_target_pairs={{0,10},{2,8},{4,14},{6,12},{8,2},{10,0},{12,6},{14,4},{1,11},{3,9}... | collective-permute-start | bytes 331784 | tf_op jit(solution)/shard_map/ppermute | solution.py:367
  52.2 4.3 %shard_map.139 = (bf16[432,128]{1,0:T(8,128)(2,1)S(1)}, bf16[432,128]{1,0:T(8,128)(2,1)S(1)}, bf16[432,128]{1,0:T(8,128)(2,1)S(1)}, bf16[432,128]{1,0:T(8,128)(2...) custom-call(bf16[384,128]{1,0:T(8,128)(2,1)S(1)} %get-tuple-element., ...), custom_call_target="tpu_custom_call" | custom-call | flops 7000000000 | bytes 4194304 | tf_op jit(solution)/shard_map/pallas_call | solution.py:341
  56.5 1.2 %collective-permute-start.26 = (bf16[432,128]{1,0:T(8,128)(2,1)S(1)}, bf16[432,128]{1,0:T(8,128)(2,1)S(1)}, u32[]{:S(2)}, u32[]{:S(2)}) collective-permute-start(bf16[432,128]{1,0:T(8,128)(2,1)S(1)} %get-tuple-element.74), channel_id=1, source_target_pairs={{0,6},{2,4},{4,2},{6,0},{8,14},{10,12},{12,10},{14,8},{1,7},{3,5},... | collective-permute-start | bytes 331784 | tf_op jit(solution)/shard_map/ppermute | solution.py:367
  57.7 0.0 collective-permute-done.22.refs_2_
  57.7 1.8 %collective-permute-start.27 = (bf16[432,128]{1,0:T(8,128)(2,1)S(1)}, bf16[432,128]{1,0:T(8,128)(2,1)S(1)}, u32[]{:S(2)}, u32[]{:S(2)}) collective-permute-start(bf16[432,128]{1,0:T(8,128)(2,1)S(1)} %get-tuple-element.75), channel_id=1, source_target_pairs={{0,8},{2,10},{4,12},{6,14},{8,0},{10,2},{12,4},{14,6},{1,9},{3,11}... | collective-permute-start | bytes 331784 | tf_op jit(solution)/shard_map/ppermute | solution.py:367
  59.5 0.0 collective-permute-done.23.refs_3_
  59.5 2.4 %collective-permute-start.7 = (bf16[432,128]{1,0:T(8,128)(2,1)S(1)}, bf16[432,128]{1,0:T(8,128)(2,1)S(1)}, u32[]{:S(2)}, u32[]{:S(2)}) collective-permute-start(bf16[432,128]{1,0:T(8,128)(2,1)S(1)} %get-tuple-element.53), channel_id=1, source_target_pairs={{0,14},{2,12},{4,10},{6,8},{8,6},{10,4},{12,2},{14,0},{1,15},{3,13... | collective-permute-start | bytes 331784 | tf_op jit(solution)/shard_map/ppermute | solution.py:367
  61.8 1.0 %collective-permute-start.8 = (bf16[432,128]{1,0:T(8,128)(2,1)S(1)}, bf16[432,128]{1,0:T(8,128)(2,1)S(1)}, u32[]{:S(2)}, u32[]{:S(2)}) collective-permute-start(bf16[432,128]{1,0:T(8,128)(2,1)S(1)} %get-tuple-element.54), channel_id=1, source_target_pairs={{0,2},{2,0},{4,6},{6,4},{8,10},{10,8},{12,14},{14,12},{1,3},{3,1},... | collective-permute-start | bytes 331784 | tf_op jit(solution)/shard_map/ppermute | solution.py:367
  62.8 3.1 %collective-permute-done.25.refs_5_ = bf16[432,128]{1,0:T(8,128)(2,1)S(1)} collective-permute-done((bf16[432,128]{1,0:T(8,128)(2,1)S(1)}, bf16[432,128]{1,0:T(8,128)(2,1)S(1)}, u32[]{:S(2)}, u32[]{:S(2)}) %collective-permute-start.25) | collective-permute-done | bytes 110624 | tf_op jit(solution)/shard_map/ppermute | solution.py:367
  65.9 1.8 %collective-permute-start.9 = (bf16[432,128]{1,0:T(8,128)(2,1)S(1)}, bf16[432,128]{1,0:T(8,128)(2,1)S(1)}, u32[]{:S(2)}, u32[]{:S(2)}) collective-permute-start(bf16[432,128]{1,0:T(8,128)(2,1)S(1)} %get-tuple-element.55), channel_id=1, source_target_pairs={{0,12},{2,14},{4,8},{6,10},{8,4},{10,6},{12,0},{14,2},{1,13},{3,15... | collective-permute-start | bytes 331784 | tf_op jit(solution)/shard_map/ppermute | solution.py:367
  67.7 2.2 %collective-permute-done.27.refs_7_ = bf16[432,128]{1,0:T(8,128)(2,1)S(1)} collective-permute-done((bf16[432,128]{1,0:T(8,128)(2,1)S(1)}, bf16[432,128]{1,0:T(8,128)(2,1)S(1)}, u32[]{:S(2)}, u32[]{:S(2)}) %collective-permute-start.27) | collective-permute-done | bytes 110624 | tf_op jit(solution)/shard_map/ppermute | solution.py:367
  69.9 1.3 %collective-permute-start.11 = (bf16[432,128]{1,0:T(8,128)(2,1)S(1)}, bf16[432,128]{1,0:T(8,128)(2,1)S(1)}, u32[]{:S(2)}, u32[]{:S(2)}) collective-permute-start(bf16[432,128]{1,0:T(8,128)(2,1)S(1)} %get-tuple-element.57), channel_id=1, source_target_pairs={{0,10},{2,8},{4,14},{6,12},{8,2},{10,0},{12,6},{14,4},{1,11},{3,9}... | collective-permute-start | bytes 331784 | tf_op jit(solution)/shard_map/ppermute | solution.py:367
  71.1 5.4 %collective-permute-start.12 = (bf16[432,128]{1,0:T(8,128)(2,1)S(1)}, bf16[432,128]{1,0:T(8,128)(2,1)S(1)}, u32[]{:S(2)}, u32[]{:S(2)}) collective-permute-start(bf16[432,128]{1,0:T(8,128)(2,1)S(1)} %get-tuple-element.58), channel_id=1, source_target_pairs={{0,6},{2,4},{4,2},{6,0},{8,14},{10,12},{12,10},{14,8},{1,7},{3,5},... | collective-permute-start | bytes 331784 | tf_op jit(solution)/shard_map/ppermute | solution.py:367
  76.5 3.0 %shard_map.142 = (bf16[2,192,1440]{2,1,0:T(8,128)(2,1)}, bf16[2,192,1440]{2,1,0:T(8,128)(2,1)}, f32[2,2304]{1,0:T(2,128)S(1)}, f32[2,2304]{1,0:T(2,128)S(1)}) custom-call(bf16[432,128]{1,0:T(8,128)(2,1)S(1)} %get-tuple-element.68.refs_0_, bf16[432,128]{1,0:T(8,128)(2,1)S(1)} %collective-permute-done.21.refs_1_, ...), custom_call_target="tpu_custom_call" | custom-call | flops 4000000000 | bytes 5242880 | tf_op jit(solution)/shard_map/pallas_call | solution.py:189
  79.5 3.4 %collective-permute-done.11.refs_5_ = bf16[432,128]{1,0:T(8,128)(2,1)S(1)} collective-permute-done((bf16[432,128]{1,0:T(8,128)(2,1)S(1)}, bf16[432,128]{1,0:T(8,128)(2,1)S(1)}, u32[]{:S(2)}, u32[]{:S(2)}) %collective-permute-start.11) | collective-permute-done | bytes 110624 | tf_op jit(solution)/shard_map/ppermute | solution.py:367
  82.9 0.0 collective-permute-done.13.refs_7_
  83.0 3.0 %shard_map.143 = (bf16[2,192,1440]{2,1,0:T(8,128)(2,1)}, bf16[2,192,1440]{2,1,0:T(8,128)(2,1)}, f32[2,2304]{1,0:T(2,128)}, f32[2,2304]{1,0:T(2,128)}) custom-call(bf16[432,128]{1,0:T(8,128)(2,1)S(1)} %get-tuple-element.52.refs_0_, bf16[432,128]{1,0:T(8,128)(2,1)S(1)} %collective-permute-done.7.refs_1_, ...), custom_call_target="tpu_custom_call", output_to_operand_aliasing={{0}: (12, {}), {1}: (13, {})} | custom-call | flops 4000000000 | bytes 5242880 | tf_op jit(solution)/shard_map/pallas_call | solution.py:189
  (42 shorter events, 0.1 us)
Async XLA Ops:
  0.6 17.4 %copy-start = (bf16[2,1440,192]{1,2,0:T(8,128)(2,1)S(1)}, bf16[2,1440,192]{1,2,0:T(8,128)(2,1)}, u32[]{:S(2)}) copy-start(bf16[2,1440,192]{1,2,0:T(8,128)(2,1)} %param.11) | copy-start | bytes 3317764
  0.6 17.3 %copy-start.1 = (bf16[2,1440,192]{1,2,0:T(8,128)(2,1)S(1)}, bf16[2,1440,192]{1,2,0:T(8,128)(2,1)}, u32[]{:S(2)}) copy-start(bf16[2,1440,192]{1,2,0:T(8,128)(2,1)} %param.12) | copy-start | bytes 3317764
  0.7 17.3 %copy-start.10 = (f32[1,1024]{1,0:T(1,128)S(1)}, f32[1,1024]{1,0:T(1,128)}, u32[]{:S(2)}) copy-start(f32[1,1024]{1,0:T(1,128)} %constant.18.clone.scale_ref) | copy-start | bytes 12292
  6.1 16.1 %collective-permute-start.14 = (bf16[384,128]{1,0:T(8,128)(2,1)}, bf16[384,128]{1,0:T(8,128)(2,1)S(1)}, u32[]{:S(2)}, u32[]{:S(2)}) collective-permute-start(bf16[384,128]{1,0:T(8,128)(2,1)} %get-tuple-element.61), channel_id=1, source_target_pairs={{0,14},{2,12},{4,10},{6,8},{8,6},{10,4},{12,2},{14,0},{1,15},{3,13... | collective-permute-start | bytes 294920 | tf_op jit(solution)/shard_map/ppermute | solution.py:367
  12.1 10.2 %collective-permute-start.15 = (bf16[384,128]{1,0:T(8,128)(2,1)}, bf16[384,128]{1,0:T(8,128)(2,1)S(1)}, u32[]{:S(2)}, u32[]{:S(2)}) collective-permute-start(bf16[384,128]{1,0:T(8,128)(2,1)} %get-tuple-element.62), channel_id=1, source_target_pairs={{0,2},{2,0},{4,6},{6,4},{8,10},{10,8},{12,14},{14,12},{1,3},{3,1},... | collective-permute-start | bytes 294920 | tf_op jit(solution)/shard_map/ppermute | solution.py:367
  12.6 10.3 %collective-permute-start.16 = (bf16[384,128]{1,0:T(8,128)(2,1)}, bf16[384,128]{1,0:T(8,128)(2,1)S(1)}, u32[]{:S(2)}, u32[]{:S(2)}) collective-permute-start(bf16[384,128]{1,0:T(8,128)(2,1)} %get-tuple-element.63), channel_id=1, source_target_pairs={{0,12},{2,14},{4,8},{6,10},{8,4},{10,6},{12,0},{14,2},{1,13},{3,15... | collective-permute-start | bytes 294920 | tf_op jit(solution)/shard_map/ppermute | solution.py:367
  12.7 14.8 %collective-permute-start.17 = (bf16[384,128]{1,0:T(8,128)(2,1)}, bf16[384,128]{1,0:T(8,128)(2,1)S(1)}, u32[]{:S(2)}, u32[]{:S(2)}) collective-permute-start(bf16[384,128]{1,0:T(8,128)(2,1)} %get-tuple-element.64), channel_id=1, source_target_pairs={{0,4},{2,6},{4,0},{6,2},{8,12},{10,14},{12,8},{14,10},{1,5},{3,7},... | collective-permute-start | bytes 294920 | tf_op jit(solution)/shard_map/ppermute | solution.py:367
  12.7 26.8 %copy-start.2 = (bf16[4,96,192]{2,1,0:T(8,128)(2,1)S(1)}, bf16[4,96,192]{2,1,0:T(8,128)(2,1)}, u32[]{:S(2)}) copy-start(bf16[4,96,192]{2,1,0:T(8,128)(2,1)} %refs_9_.5) | copy-start | bytes 442372
  12.7 26.9 %copy-start.3 = (bf16[4,96,192]{2,1,0:T(8,128)(2,1)S(1)}, bf16[4,96,192]{2,1,0:T(8,128)(2,1)}, u32[]{:S(2)}) copy-start(bf16[4,96,192]{2,1,0:T(8,128)(2,1)} %refs_11_.3) | copy-start | bytes 442372
  12.7 26.9 %copy-start.4 = (f32[4,192]{1,0:T(4,128)S(1)}, f32[4,192]{1,0:T(4,128)}, u32[]{:S(2)}) copy-start(f32[4,192]{1,0:T(4,128)} %refs_10_.3) | copy-start | bytes 9220
  12.7 26.9 %copy-start.5 = (f32[4,192]{1,0:T(4,128)S(1)}, f32[4,192]{1,0:T(4,128)}, u32[]{:S(2)}) copy-start(f32[4,192]{1,0:T(4,128)} %refs_12_.3) | copy-start | bytes 9220
  12.7 15.3 %collective-permute-start.18 = (bf16[384,128]{1,0:T(8,128)(2,1)}, bf16[384,128]{1,0:T(8,128)(2,1)S(1)}, u32[]{:S(2)}, u32[]{:S(2)}) collective-permute-start(bf16[384,128]{1,0:T(8,128)(2,1)} %get-tuple-element.65), channel_id=1, source_target_pairs={{0,10},{2,8},{4,14},{6,12},{8,2},{10,0},{12,6},{14,4},{1,11},{3,9}... | collective-permute-start | bytes 294920 | tf_op jit(solution)/shard_map/ppermute | solution.py:367
  18.0 1.8 %copy-start.7 = (bf16[4,1440,256]{2,1,0:T(8,128)(2,1)S(1)}, bf16[4,1440,256]{2,1,0:T(8,128)(2,1)}, u32[]{:S(2)}) copy-start(bf16[4,1440,256]{2,1,0:T(8,128)(2,1)} %constant.16.clone.table_ref) | copy-start | bytes 8847364
  19.8 2.3 %copy-start.13 = (bf16[384,128]{1,0:T(8,128)(2,1)S(1)}, bf16[384,128]{1,0:T(8,128)(2,1)}, u32[]{:S(2)}) copy-start(bf16[384,128]{1,0:T(8,128)(2,1)} %get-tuple-element.66) | copy-start | bytes 294916
  19.8 2.4 %copy-start.12 = (bf16[384,128]{1,0:T(8,128)(2,1)S(1)}, bf16[384,128]{1,0:T(8,128)(2,1)}, u32[]{:S(2)}) copy-start(bf16[384,128]{1,0:T(8,128)(2,1)} %get-tuple-element.67) | copy-start | bytes 294916
  19.8 19.8 %copy-start.8 = (bf16[256,512]{1,0:T(8,128)(2,1)S(1)}, bf16[256,512]{1,0:T(8,128)(2,1)}, u32[]{:S(2)}) copy-start(bf16[256,512]{1,0:T(8,128)(2,1)} %constant.20.clone.refs_8_) | copy-start | bytes 786436
  19.8 19.8 %copy-start.11 = (bf16[384,128]{1,0:T(8,128)(2,1)S(1)}, bf16[384,128]{1,0:T(8,128)(2,1)}, u32[]{:S(2)}) copy-start(bf16[384,128]{1,0:T(8,128)(2,1)} %get-tuple-element.60.refs_0_) | copy-start | bytes 294916
  22.1 6.9 %collective-permute-start.19 = (bf16[384,128]{1,0:T(8,128)(2,1)S(1)}, bf16[384,128]{1,0:T(8,128)(2,1)S(1)}, u32[]{:S(2)}, u32[]{:S(2)}) collective-permute-start(bf16[384,128]{1,0:T(8,128)(2,1)S(1)} %copy-done.13), channel_id=1, source_target_pairs={{0,6},{2,4},{4,2},{6,0},{8,14},{10,12},{12,10},{14,8},{1,7},{3,5},... | collective-permute-start | bytes 294920 | tf_op jit(solution)/shard_map/ppermute | solution.py:367
  22.2 13.3 %collective-permute-start.20 = (bf16[384,128]{1,0:T(8,128)(2,1)S(1)}, bf16[384,128]{1,0:T(8,128)(2,1)S(1)}, u32[]{:S(2)}, u32[]{:S(2)}) collective-permute-start(bf16[384,128]{1,0:T(8,128)(2,1)S(1)} %copy-done.12), channel_id=1, source_target_pairs={{0,8},{2,10},{4,12},{6,14},{8,0},{10,2},{12,4},{14,6},{1,9},{3,11}... | collective-permute-start | bytes 294920 | tf_op jit(solution)/shard_map/ppermute | solution.py:367
  22.9 12.7 %collective-permute-start = (bf16[384,128]{1,0:T(8,128)(2,1)S(1)}, bf16[384,128]{1,0:T(8,128)(2,1)S(1)}, u32[]{:S(2)}, u32[]{:S(2)}) collective-permute-start(bf16[384,128]{1,0:T(8,128)(2,1)S(1)} %get-tuple-element.45), channel_id=1, source_target_pairs={{0,14},{2,12},{4,10},{6,8},{8,6},{10,4},{12,2},{14,0},{1,15},{3,13... | collective-permute-start | bytes 294920 | tf_op jit(solution)/shard_map/ppermute | solution.py:367
  27.5 12.0 %collective-permute-start.1 = (bf16[384,128]{1,0:T(8,128)(2,1)S(1)}, bf16[384,128]{1,0:T(8,128)(2,1)S(1)}, u32[]{:S(2)}, u32[]{:S(2)}) collective-permute-start(bf16[384,128]{1,0:T(8,128)(2,1)S(1)} %get-tuple-element.46), channel_id=1, source_target_pairs={{0,2},{2,0},{4,6},{6,4},{8,10},{10,8},{12,14},{14,12},{1,3},{3,1},... | collective-permute-start | bytes 294920 | tf_op jit(solution)/shard_map/ppermute | solution.py:367
  28.0 15.8 %collective-permute-start.2 = (bf16[384,128]{1,0:T(8,128)(2,1)S(1)}, bf16[384,128]{1,0:T(8,128)(2,1)S(1)}, u32[]{:S(2)}, u32[]{:S(2)}) collective-permute-start(bf16[384,128]{1,0:T(8,128)(2,1)S(1)} %get-tuple-element.47), channel_id=1, source_target_pairs={{0,12},{2,14},{4,8},{6,10},{8,4},{10,6},{12,0},{14,2},{1,13},{3,15... | collective-permute-start | bytes 294920 | tf_op jit(solution)/shard_map/ppermute | solution.py:367
  29.0 17.3 %collective-permute-start.3 = (bf16[384,128]{1,0:T(8,128)(2,1)S(1)}, bf16[384,128]{1,0:T(8,128)(2,1)S(1)}, u32[]{:S(2)}, u32[]{:S(2)}) collective-permute-start(bf16[384,128]{1,0:T(8,128)(2,1)S(1)} %get-tuple-element.48), channel_id=1, source_target_pairs={{0,4},{2,6},{4,0},{6,2},{8,12},{10,14},{12,8},{14,10},{1,5},{3,7},... | collective-permute-start | bytes 294920 | tf_op jit(solution)/shard_map/ppermute | solution.py:367
  35.6 11.7 %collective-permute-start.4 = (bf16[384,128]{1,0:T(8,128)(2,1)S(1)}, bf16[384,128]{1,0:T(8,128)(2,1)S(1)}, u32[]{:S(2)}, u32[]{:S(2)}) collective-permute-start(bf16[384,128]{1,0:T(8,128)(2,1)S(1)} %get-tuple-element.49), channel_id=1, source_target_pairs={{0,10},{2,8},{4,14},{6,12},{8,2},{10,0},{12,6},{14,4},{1,11},{3,9}... | collective-permute-start | bytes 294920 | tf_op jit(solution)/shard_map/ppermute | solution.py:367
  35.6 13.7 %collective-permute-start.5 = (bf16[384,128]{1,0:T(8,128)(2,1)S(1)}, bf16[384,128]{1,0:T(8,128)(2,1)S(1)}, u32[]{:S(2)}, u32[]{:S(2)}) collective-permute-start(bf16[384,128]{1,0:T(8,128)(2,1)S(1)} %get-tuple-element.50), channel_id=1, source_target_pairs={{0,6},{2,4},{4,2},{6,0},{8,14},{10,12},{12,10},{14,8},{1,7},{3,5},... | collective-permute-start | bytes 294920 | tf_op jit(solution)/shard_map/ppermute | solution.py:367
  39.5 10.3 %collective-permute-start.6 = (bf16[384,128]{1,0:T(8,128)(2,1)S(1)}, bf16[384,128]{1,0:T(8,128)(2,1)S(1)}, u32[]{:S(2)}, u32[]{:S(2)}) collective-permute-start(bf16[384,128]{1,0:T(8,128)(2,1)S(1)} %get-tuple-element.51), channel_id=1, source_target_pairs={{0,8},{2,10},{4,12},{6,14},{8,0},{10,2},{12,4},{14,6},{1,9},{3,11}... | collective-permute-start | bytes 294920 | tf_op jit(solution)/shard_map/ppermute | solution.py:367
  43.9 12.6 %collective-permute-start.21 = (bf16[432,128]{1,0:T(8,128)(2,1)S(1)}, bf16[432,128]{1,0:T(8,128)(2,1)S(1)}, u32[]{:S(2)}, u32[]{:S(2)}) collective-permute-start(bf16[432,128]{1,0:T(8,128)(2,1)S(1)} %get-tuple-element.69), channel_id=1, source_target_pairs={{0,14},{2,12},{4,10},{6,8},{8,6},{10,4},{12,2},{14,0},{1,15},{3,13... | collective-permute-start | bytes 331784 | tf_op jit(solution)/shard_map/ppermute | solution.py:367
  46.3 11.4 %collective-permute-start.22 = (bf16[432,128]{1,0:T(8,128)(2,1)S(1)}, bf16[432,128]{1,0:T(8,128)(2,1)S(1)}, u32[]{:S(2)}, u32[]{:S(2)}) collective-permute-start(bf16[432,128]{1,0:T(8,128)(2,1)S(1)} %get-tuple-element.70), channel_id=1, source_target_pairs={{0,2},{2,0},{4,6},{6,4},{8,10},{10,8},{12,14},{14,12},{1,3},{3,1},... | collective-permute-start | bytes 331784 | tf_op jit(solution)/shard_map/ppermute | solution.py:367
  47.3 12.2 %collective-permute-start.23 = (bf16[432,128]{1,0:T(8,128)(2,1)S(1)}, bf16[432,128]{1,0:T(8,128)(2,1)S(1)}, u32[]{:S(2)}, u32[]{:S(2)}) collective-permute-start(bf16[432,128]{1,0:T(8,128)(2,1)S(1)} %get-tuple-element.71), channel_id=1, source_target_pairs={{0,12},{2,14},{4,8},{6,10},{8,4},{10,6},{12,0},{14,2},{1,13},{3,15... | collective-permute-start | bytes 331784 | tf_op jit(solution)/shard_map/ppermute | solution.py:367
  49.3 12.6 %collective-permute-start.24 = (bf16[432,128]{1,0:T(8,128)(2,1)S(1)}, bf16[432,128]{1,0:T(8,128)(2,1)S(1)}, u32[]{:S(2)}, u32[]{:S(2)}) collective-permute-start(bf16[432,128]{1,0:T(8,128)(2,1)S(1)} %get-tuple-element.72), channel_id=1, source_target_pairs={{0,4},{2,6},{4,0},{6,2},{8,12},{10,14},{12,8},{14,10},{1,5},{3,7},... | collective-permute-start | bytes 331784 | tf_op jit(solution)/shard_map/ppermute | solution.py:367
  49.9 16.0 %collective-permute-start.25 = (bf16[432,128]{1,0:T(8,128)(2,1)S(1)}, bf16[432,128]{1,0:T(8,128)(2,1)S(1)}, u32[]{:S(2)}, u32[]{:S(2)}) collective-permute-start(bf16[432,128]{1,0:T(8,128)(2,1)S(1)} %get-tuple-element.73), channel_id=1, source_target_pairs={{0,10},{2,8},{4,14},{6,12},{8,2},{10,0},{12,6},{14,4},{1,11},{3,9}... | collective-permute-start | bytes 331784 | tf_op jit(solution)/shard_map/ppermute | solution.py:367
  52.2 24.3 %copy-start.6 = (bf16[1024,1440]{1,0:T(8,128)(2,1)S(1)}, bf16[1024,1440]{1,0:T(8,128)(2,1)}, u32[]{:S(2)}) copy-start(bf16[1024,1440]{1,0:T(8,128)(2,1)} %constant.17.clone.refs_8_) | copy-start | bytes 8847364
  52.2 24.3 %copy-start.9 = (f32[8,128]{1,0:T(8,128)S(1)}, f32[8,128]{1,0:T(8,128)}, u32[]{:S(2)}) copy-start(f32[8,128]{1,0:T(8,128)} %constant.19.clone.refs_9_) | copy-start | bytes 12292
  56.5 11.2 %collective-permute-start.26 = (bf16[432,128]{1,0:T(8,128)(2,1)S(1)}, bf16[432,128]{1,0:T(8,128)(2,1)S(1)}, u32[]{:S(2)}, u32[]{:S(2)}) collective-permute-start(bf16[432,128]{1,0:T(8,128)(2,1)S(1)} %get-tuple-element.74), channel_id=1, source_target_pairs={{0,6},{2,4},{4,2},{6,0},{8,14},{10,12},{12,10},{14,8},{1,7},{3,5},... | collective-permute-start | bytes 331784 | tf_op jit(solution)/shard_map/ppermute | solution.py:367
  57.7 12.2 %collective-permute-start.27 = (bf16[432,128]{1,0:T(8,128)(2,1)S(1)}, bf16[432,128]{1,0:T(8,128)(2,1)S(1)}, u32[]{:S(2)}, u32[]{:S(2)}) collective-permute-start(bf16[432,128]{1,0:T(8,128)(2,1)S(1)} %get-tuple-element.75), channel_id=1, source_target_pairs={{0,8},{2,10},{4,12},{6,14},{8,0},{10,2},{12,4},{14,6},{1,9},{3,11}... | collective-permute-start | bytes 331784 | tf_op jit(solution)/shard_map/ppermute | solution.py:367
  59.5 11.7 %collective-permute-start.7 = (bf16[432,128]{1,0:T(8,128)(2,1)S(1)}, bf16[432,128]{1,0:T(8,128)(2,1)S(1)}, u32[]{:S(2)}, u32[]{:S(2)}) collective-permute-start(bf16[432,128]{1,0:T(8,128)(2,1)S(1)} %get-tuple-element.53), channel_id=1, source_target_pairs={{0,14},{2,12},{4,10},{6,8},{8,6},{10,4},{12,2},{14,0},{1,15},{3,13... | collective-permute-start | bytes 331784 | tf_op jit(solution)/shard_map/ppermute | solution.py:367
  61.8 14.7 %collective-permute-start.8 = (bf16[432,128]{1,0:T(8,128)(2,1)S(1)}, bf16[432,128]{1,0:T(8,128)(2,1)S(1)}, u32[]{:S(2)}, u32[]{:S(2)}) collective-permute-start(bf16[432,128]{1,0:T(8,128)(2,1)S(1)} %get-tuple-element.54), channel_id=1, source_target_pairs={{0,2},{2,0},{4,6},{6,4},{8,10},{10,8},{12,14},{14,12},{1,3},{3,1},... | collective-permute-start | bytes 331784 | tf_op jit(solution)/shard_map/ppermute | solution.py:367
  65.9 13.7 %collective-permute-start.9 = (bf16[432,128]{1,0:T(8,128)(2,1)S(1)}, bf16[432,128]{1,0:T(8,128)(2,1)S(1)}, u32[]{:S(2)}, u32[]{:S(2)}) collective-permute-start(bf16[432,128]{1,0:T(8,128)(2,1)S(1)} %get-tuple-element.55), channel_id=1, source_target_pairs={{0,12},{2,14},{4,8},{6,10},{8,4},{10,6},{12,0},{14,2},{1,13},{3,15... | collective-permute-start | bytes 331784 | tf_op jit(solution)/shard_map/ppermute | solution.py:367
  67.7 11.9 %collective-permute-start.10 = (bf16[432,128]{1,0:T(8,128)(2,1)S(1)}, bf16[432,128]{1,0:T(8,128)(2,1)S(1)}, u32[]{:S(2)}, u32[]{:S(2)}) collective-permute-start(bf16[432,128]{1,0:T(8,128)(2,1)S(1)} %get-tuple-element.56), channel_id=1, source_target_pairs={{0,4},{2,6},{4,0},{6,2},{8,12},{10,14},{12,8},{14,10},{1,5},{3,7},... | collective-permute-start | bytes 331784 | tf_op jit(solution)/shard_map/ppermute | solution.py:367
  69.9 13.1 %collective-permute-start.11 = (bf16[432,128]{1,0:T(8,128)(2,1)S(1)}, bf16[432,128]{1,0:T(8,128)(2,1)S(1)}, u32[]{:S(2)}, u32[]{:S(2)}) collective-permute-start(bf16[432,128]{1,0:T(8,128)(2,1)S(1)} %get-tuple-element.57), channel_id=1, source_target_pairs={{0,10},{2,8},{4,14},{6,12},{8,2},{10,0},{12,6},{14,4},{1,11},{3,9}... | collective-permute-start | bytes 331784 | tf_op jit(solution)/shard_map/ppermute | solution.py:367
  71.1 11.8 %collective-permute-start.12 = (bf16[432,128]{1,0:T(8,128)(2,1)S(1)}, bf16[432,128]{1,0:T(8,128)(2,1)S(1)}, u32[]{:S(2)}, u32[]{:S(2)}) collective-permute-start(bf16[432,128]{1,0:T(8,128)(2,1)S(1)} %get-tuple-element.58), channel_id=1, source_target_pairs={{0,6},{2,4},{4,2},{6,0},{8,14},{10,12},{12,10},{14,8},{1,7},{3,5},... | collective-permute-start | bytes 331784 | tf_op jit(solution)/shard_map/ppermute | solution.py:367
  76.5 6.5 %collective-permute-start.13 = (bf16[432,128]{1,0:T(8,128)(2,1)S(1)}, bf16[432,128]{1,0:T(8,128)(2,1)S(1)}, u32[]{:S(2)}, u32[]{:S(2)}) collective-permute-start(bf16[432,128]{1,0:T(8,128)(2,1)S(1)} %get-tuple-element.59), channel_id=1, source_target_pairs={{0,8},{2,10},{4,12},{6,14},{8,0},{10,2},{12,4},{14,6},{1,9},{3,11}... | collective-permute-start | bytes 331784 | tf_op jit(solution)/shard_map/ppermute | solution.py:367

commit v5 on v4

--- a/solution.py
+++ b/solution.py
@@ -12,6 +12,7 @@
 KW = 512
 LANES = 128
 HALF = 64
+CHUNK = 512
 PACK = 16
 MIB = 1024 * 1024
 ZONAL_MIB = 60
@@ -129,29 +130,44 @@
     blocks = refs[:pieces]
     table_ref, scale_ref, field_ref, cotangent_ref = refs[pieces : pieces + 4]
     before = refs[pieces + 4 : pieces + 4 + given]
-    mixed_ref, gradient_ref, first_ref, second_ref, modes_ref = refs[pieces + 4 + given :]
+    mixed_ref, gradient_ref, first_ref, second_ref = refs[pieces + 4 + given : pieces + 8 + given]
+    modes_ref, results_ref, flat_ref, sems, flat_sems = refs[pieces + 8 + given :]
     rows = modes_ref.shape[1]
     half = rows // 2
-
-    @pl.when(pl.program_id(0) == 0)
-    def _():
-        mine = lax.axis_index("lat")
-        for block, shift in zip(blocks, slots(pieces)):
-            place = relative(mine, shift)
-            scale = scale_ref[pl.ds(place, 1), :]
-            modes_ref[place, :half] = (block[:half].astype(F32) * scale).astype(BF16)
-            modes_ref[place, half:] = block[half:rows]
-        total = blocks[0][rows:].astype(F32)
-        for block in blocks[1:]:
-            total += block[rows:].astype(F32)
-        spread_gradient(total, 0, group, before[2:3], first_ref)
-        spread_gradient(total, 1, group, before[3:4], second_ref)
+    _, lines, width, col_count = results_ref.shape
+    own = slice(group * width, (group + 1) * width)
+    mine = lax.axis_index("lat")
+    for block, shift in zip(blocks, slots(pieces)):
+        place = relative(mine, shift)
+        scale = scale_ref[pl.ds(place, 1), :]
+        modes_ref[place, :half] = (block[:half].astype(F32) * scale).astype(BF16)
+        modes_ref[place, half:] = block[half:rows]
 
     modes = jnp.concatenate([modes_ref[piece] for piece in range(pieces)], axis=1)
-    result = mm(modes, table_ref[...])
-    shape = field_ref.shape
-    mixed_ref[...] = (field_ref[...].astype(F32) + result[:half].reshape(shape)).astype(BF16)
-    gradient_ref[...] = (cotangent_ref[...].astype(F32) + result[half:].reshape(shape)).astype(BF16)
+    copies = []
+    for chunk, begin in enumerate(range(0, col_count, CHUNK)):
+        columns = slice(begin, min(begin + CHUNK, col_count))
+        result = mm(modes, table_ref[:, columns])
+        for kind, (base, out) in enumerate(((field_ref, mixed_ref), (cotangent_ref, gradient_ref))):
+            part = result[kind * half : (kind + 1) * half].reshape(lines, width, -1)
+            results_ref[kind, :, :, columns] = (base[:, own, columns].astype(F32) + part).astype(BF16)
+            copy = pltpu.make_async_copy(
+                results_ref.at[kind, :, :, columns], out.at[:, own, columns], sems.at[chunk, kind]
+            )
+            copy.start()
+            copies.append(copy)
+        if begin == 0:
+            total = blocks[0][rows:].astype(F32)
+            for block in blocks[1:]:
+                total += block[rows:].astype(F32)
+            for kind, out in enumerate((first_ref, second_ref)):
+                spread_gradient(total, kind, group, before[2 + kind : 3 + kind], flat_ref.at[kind])
+                copy = pltpu.make_async_copy(flat_ref.at[kind], out, flat_sems.at[kind])
+                copy.start()
+                copies.append(copy)
+
+    for copy in copies:
+        copy.wait()
 
 
 def spread_gradient(total, kind, group, before, out_ref):
@@ -162,6 +178,8 @@
         lines.append(total[kind * PACK + line : kind * PACK + line + 1])
         lines.append(total[2 * PACK + line : 2 * PACK + line + 1, kind * HALF : (kind + 1) * HALF])
     out_ref[group : group + 1] = jnp.concatenate(lines, axis=1)
+    for member in range(group + 1, out_ref.shape[0]):
+        out_ref[member : member + 1] = jnp.zeros((1, out_ref.shape[1]), F32)
 
 
 def pack_gradients(sums_ref, packed_ref):
@@ -178,29 +196,24 @@
 
 def inverse(blocks, table, scale, field, cotangent, group, groups, gradient_size, before):
     pieces = len(blocks)
-    kept, col_count = table.shape
-    lines, channels, _ = field.shape
+    lines, channels, col_count = field.shape
     width = channels // groups
-    rows = 2 * lines * width
-    wide = 512
-    own = pl.BlockSpec((lines, width, wide), lambda i: (0, group, i))
     anywhere = pl.BlockSpec(memory_space=pl.ANY)
-    gradient = pl.BlockSpec((groups, gradient_size), lambda i: (0, 0))
+    gradient = whole(groups, gradient_size)
     return pl.pallas_call(
         functools.partial(inverse_kernel, pieces, len(before), group),
-        grid=(pl.cdiv(col_count, wide),),
-        in_specs=[pl.BlockSpec(block.shape, lambda i: (0, 0)) for block in blocks]
-        + [
-            pl.BlockSpec((kept, wide), lambda i: (0, i)),
-            pl.BlockSpec(scale.shape, lambda i: (0, 0)),
-            own,
-            own,
-        ]
+        in_specs=[whole(*a.shape) for a in (*blocks, table, scale, field, cotangent)]
         + ([anywhere, anywhere, gradient, gradient] if before else []),
-        out_specs=[own, own, gradient, gradient],
+        out_specs=[anywhere] * 4,
         out_shape=[jax.ShapeDtypeStruct(field.shape, BF16) for _ in range(2)]
         + [jax.ShapeDtypeStruct((groups, gradient_size), F32) for _ in range(2)],
-        scratch_shapes=[pltpu.VMEM((pieces, rows, LANES), BF16)],
+        scratch_shapes=[
+            pltpu.VMEM((pieces, 2 * lines * width, LANES), BF16),
+            pltpu.VMEM((2, lines, width, col_count), BF16),
+            pltpu.VMEM((2, groups, gradient_size), F32),
+            pltpu.SemaphoreType.DMA((pl.cdiv(col_count, CHUNK), 2)),
+            pltpu.SemaphoreType.DMA((2,)),
+        ],
         input_output_aliases={pieces + 4 + i: i for i in range(2)} if before else {},
         compiler_params=limits(INVERSE_MIB),
         cost_estimate=pl.CostEstimate(flops=4 * 10**9, bytes_accessed=5 * MIB, transcendentals=0),

time: 86.2 us -> 85.7 us (level)
  no operation moved by 1% of the time
where the time goes in v5:
time: 85.7 us; the launch traced here: 85.6 us
  starting transfers between devices  46.4 us (54%)
  Pallas kernels  21.6 us (25%)
  waiting for transfers between devices  14.8 us (17%)
  local copies, waits for them, and re-layouts  1.88 us (2%)
  between operations  0.87 us (1%)
    ppermute x28, starting transfers between devices, pass_to(): lax.ppermute(block, 'lat', [(place, place ^ shift) for place in range(cou...  46.4 us
    ppermute x28, waiting for transfers between devices, pass_to(): lax.ppermute(block, 'lat', [(place, place ^ shift) for place in range(cou...  14.8 us
    pallas_call x2, Pallas kernels, middle(): pl.pallas_call(functools.partial(middle_kernel, group, groups, normalizer...  8.54 us
    pallas_call x2, Pallas kernels, zonal(): pl.pallas_call(zonal_kernel, grid_spec=pltpu.PrefetchScalarGridSpec(num_s...  7.67 us
    pallas_call x2, Pallas kernels, inverse(): pl.pallas_call(functools.partial(inverse_kernel, pieces, len(before), gro...  5.36 us
    unnamed x28, local copies, waits for them, and re-layouts  1.88 us
  transfers between devices with their start and end apart: 28, of which 4 were waited for; matrix products, arithmetic and copies ran while one was open for 0% of the time, Pallas kernels for 16%

profile of v5, /device:TPU:0, one launch (start us, length us, event | category | flops | bytes accessed | tf_op | source)
XLA Modules:
  0.0 85.6 jit_solution(13146286589401194023)
XLA Ops:
  0.7 0.0 copy-start.10
  0.7 5.4 %shard_map.140 = (bf16[384,128]{1,0:T(8,128)(2,1)}, bf16[384,128]{1,0:T(8,128)(2,1)}, bf16[384,128]{1,0:T(8,128)(2,1)}, bf16[384,128]{1,0:T(8,128)(2,1)}, bf16[3...) custom-call(s32[1]{0:T(128)} %bitcast.mine_ref, ...), custom_call_target="tpu_custom_call" | custom-call | flops 4000000000 | bytes 4194304 | tf_op jit(solution)/shard_map/pallas_call | solution.py:109
  6.1 6.0 %collective-permute-start.14 = (bf16[384,128]{1,0:T(8,128)(2,1)}, bf16[384,128]{1,0:T(8,128)(2,1)S(1)}, u32[]{:S(2)}, u32[]{:S(2)}) collective-permute-start(bf16[384,128]{1,0:T(8,128)(2,1)} %get-tuple-element.61), channel_id=1, source_target_pairs={{0,14},{2,12},{4,10},{6,8},{8,6},{10,4},{12,2},{14,0},{1,15},{3,13... | collective-permute-start | bytes 294920 | tf_op jit(solution)/shard_map/ppermute | solution.py:380
  12.1 0.5 collective-permute-start.15
  12.6 0.1 collective-permute-start.16
  12.7 0.0 collective-permute-start.17
  12.7 0.0 copy-start.5
  12.7 5.3 %collective-permute-start.18 = (bf16[384,128]{1,0:T(8,128)(2,1)}, bf16[384,128]{1,0:T(8,128)(2,1)S(1)}, u32[]{:S(2)}, u32[]{:S(2)}) collective-permute-start(bf16[384,128]{1,0:T(8,128)(2,1)} %get-tuple-element.65), channel_id=1, source_target_pairs={{0,10},{2,8},{4,14},{6,12},{8,2},{10,0},{12,6},{14,4},{1,11},{3,9}... | collective-permute-start | bytes 294920 | tf_op jit(solution)/shard_map/ppermute | solution.py:380
  18.0 1.8 %copy-done.7 = bf16[4,1440,256]{2,1,0:T(8,128)(2,1)S(1)} copy-done((bf16[4,1440,256]{2,1,0:T(8,128)(2,1)S(1)}, bf16[4,1440,256]{2,1,0:T(8,128)(2,1)}, u32[]{:S(2)}) %copy-start.7) | copy-done | bytes 2949144
  19.8 2.3 %shard_map.138 = (bf16[384,128]{1,0:T(8,128)(2,1)S(1)}, bf16[384,128]{1,0:T(8,128)(2,1)S(1)}, bf16[384,128]{1,0:T(8,128)(2,1)S(1)}, bf16[384,128]{1,0:T(8,128)(2...) custom-call(s32[1]{0:T(128)} %bitcast.mine_ref, ...), custom_call_target="tpu_custom_call" | custom-call | flops 4000000000 | bytes 4194304 | tf_op jit(solution)/shard_map/pallas_call | solution.py:109
  22.1 0.1 collective-permute-start.19
  22.2 0.0 collective-permute-done.15.refs_2_
  22.2 0.6 collective-permute-start.20
  22.9 0.0 collective-permute-done.16.refs_3_
  22.9 4.6 %collective-permute-start = (bf16[384,128]{1,0:T(8,128)(2,1)S(1)}, bf16[384,128]{1,0:T(8,128)(2,1)S(1)}, u32[]{:S(2)}, u32[]{:S(2)}) collective-permute-start(bf16[384,128]{1,0:T(8,128)(2,1)S(1)} %get-tuple-element.45), channel_id=1, source_target_pairs={{0,14},{2,12},{4,10},{6,8},{8,6},{10,4},{12,2},{14,0},{1,15},{3,13... | collective-permute-start | bytes 294920 | tf_op jit(solution)/shard_map/ppermute | solution.py:380
  27.5 0.0 collective-permute-done.17.refs_4_
  27.5 0.5 collective-permute-start.1
  28.0 0.0 collective-permute-done.18.refs_5_
  28.0 1.0 %collective-permute-start.2 = (bf16[384,128]{1,0:T(8,128)(2,1)S(1)}, bf16[384,128]{1,0:T(8,128)(2,1)S(1)}, u32[]{:S(2)}, u32[]{:S(2)}) collective-permute-start(bf16[384,128]{1,0:T(8,128)(2,1)S(1)} %get-tuple-element.47), channel_id=1, source_target_pairs={{0,12},{2,14},{4,8},{6,10},{8,4},{10,6},{12,0},{14,2},{1,13},{3,15... | collective-permute-start | bytes 294920 | tf_op jit(solution)/shard_map/ppermute | solution.py:380
  29.0 0.7 collective-permute-start.3
  29.7 5.8 %collective-permute-done.20.refs_7_ = bf16[384,128]{1,0:T(8,128)(2,1)S(1)} collective-permute-done((bf16[384,128]{1,0:T(8,128)(2,1)S(1)}, bf16[384,128]{1,0:T(8,128)(2,1)S(1)}, u32[]{:S(2)}, u32[]{:S(2)}) %collective-permute-start.20) | collective-permute-done | bytes 98336 | tf_op jit(solution)/shard_map/ppermute | solution.py:380
  35.6 0.0 collective-permute-start.4
  35.6 4.0 %collective-permute-start.5 = (bf16[384,128]{1,0:T(8,128)(2,1)S(1)}, bf16[384,128]{1,0:T(8,128)(2,1)S(1)}, u32[]{:S(2)}, u32[]{:S(2)}) collective-permute-start(bf16[384,128]{1,0:T(8,128)(2,1)S(1)} %get-tuple-element.50), channel_id=1, source_target_pairs={{0,6},{2,4},{4,2},{6,0},{8,14},{10,12},{12,10},{14,8},{1,7},{3,5},... | collective-permute-start | bytes 294920 | tf_op jit(solution)/shard_map/ppermute | solution.py:380
  39.6 4.3 %shard_map.141 = (bf16[432,128]{1,0:T(8,128)(2,1)S(1)}, bf16[432,128]{1,0:T(8,128)(2,1)S(1)}, bf16[432,128]{1,0:T(8,128)(2,1)S(1)}, bf16[432,128]{1,0:T(8,128)(2...) custom-call(bf16[384,128]{1,0:T(8,128)(2,1)S(1)} %copy-done.11, ...), custom_call_target="tpu_custom_call" | custom-call | flops 7000000000 | bytes 4194304 | tf_op jit(solution)/shard_map/pallas_call | solution.py:354
  43.9 0.0 collective-permute-done.2.refs_3_
  43.9 2.4 %collective-permute-start.21 = (bf16[432,128]{1,0:T(8,128)(2,1)S(1)}, bf16[432,128]{1,0:T(8,128)(2,1)S(1)}, u32[]{:S(2)}, u32[]{:S(2)}) collective-permute-start(bf16[432,128]{1,0:T(8,128)(2,1)S(1)} %get-tuple-element.69), channel_id=1, source_target_pairs={{0,14},{2,12},{4,10},{6,8},{8,6},{10,4},{12,2},{14,0},{1,15},{3,13... | collective-permute-start | bytes 331784 | tf_op jit(solution)/shard_map/ppermute | solution.py:380
  46.3 1.0 %collective-permute-start.22 = (bf16[432,128]{1,0:T(8,128)(2,1)S(1)}, bf16[432,128]{1,0:T(8,128)(2,1)S(1)}, u32[]{:S(2)}, u32[]{:S(2)}) collective-permute-start(bf16[432,128]{1,0:T(8,128)(2,1)S(1)} %get-tuple-element.70), channel_id=1, source_target_pairs={{0,2},{2,0},{4,6},{6,4},{8,10},{10,8},{12,14},{14,12},{1,3},{3,1},... | collective-permute-start | bytes 331784 | tf_op jit(solution)/shard_map/ppermute | solution.py:380
  47.3 0.0 collective-permute-done.4.refs_5_
  47.3 1.9 %collective-permute-start.23 = (bf16[432,128]{1,0:T(8,128)(2,1)S(1)}, bf16[432,128]{1,0:T(8,128)(2,1)S(1)}, u32[]{:S(2)}, u32[]{:S(2)}) collective-permute-start(bf16[432,128]{1,0:T(8,128)(2,1)S(1)} %get-tuple-element.71), channel_id=1, source_target_pairs={{0,12},{2,14},{4,8},{6,10},{8,4},{10,6},{12,0},{14,2},{1,13},{3,15... | collective-permute-start | bytes 331784 | tf_op jit(solution)/shard_map/ppermute | solution.py:380
  49.3 0.6 collective-permute-start.24
  49.9 2.3 %collective-permute-start.25 = (bf16[432,128]{1,0:T(8,128)(2,1)S(1)}, bf16[432,128]{1,0:T(8,128)(2,1)S(1)}, u32[]{:S(2)}, u32[]{:S(2)}) collective-permute-start(bf16[432,128]{1,0:T(8,128)(2,1)S(1)} %get-tuple-element.73), channel_id=1, source_target_pairs={{0,10},{2,8},{4,14},{6,12},{8,2},{10,0},{12,6},{14,4},{1,11},{3,9}... | collective-permute-start | bytes 331784 | tf_op jit(solution)/shard_map/ppermute | solution.py:380
  52.2 4.3 %shard_map.139 = (bf16[432,128]{1,0:T(8,128)(2,1)S(1)}, bf16[432,128]{1,0:T(8,128)(2,1)S(1)}, bf16[432,128]{1,0:T(8,128)(2,1)S(1)}, bf16[432,128]{1,0:T(8,128)(2...) custom-call(bf16[384,128]{1,0:T(8,128)(2,1)S(1)} %get-tuple-element., ...), custom_call_target="tpu_custom_call" | custom-call | flops 7000000000 | bytes 4194304 | tf_op jit(solution)/shard_map/pallas_call | solution.py:354
  56.5 1.2 %collective-permute-start.26 = (bf16[432,128]{1,0:T(8,128)(2,1)S(1)}, bf16[432,128]{1,0:T(8,128)(2,1)S(1)}, u32[]{:S(2)}, u32[]{:S(2)}) collective-permute-start(bf16[432,128]{1,0:T(8,128)(2,1)S(1)} %get-tuple-element.74), channel_id=1, source_target_pairs={{0,6},{2,4},{4,2},{6,0},{8,14},{10,12},{12,10},{14,8},{1,7},{3,5},... | collective-permute-start | bytes 331784 | tf_op jit(solution)/shard_map/ppermute | solution.py:380
  57.7 1.8 %collective-permute-start.27 = (bf16[432,128]{1,0:T(8,128)(2,1)S(1)}, bf16[432,128]{1,0:T(8,128)(2,1)S(1)}, u32[]{:S(2)}, u32[]{:S(2)}) collective-permute-start(bf16[432,128]{1,0:T(8,128)(2,1)S(1)} %get-tuple-element.75), channel_id=1, source_target_pairs={{0,8},{2,10},{4,12},{6,14},{8,0},{10,2},{12,4},{14,6},{1,9},{3,11}... | collective-permute-start | bytes 331784 | tf_op jit(solution)/shard_map/ppermute | solution.py:380
  59.5 0.0 collective-permute-done.23.refs_3_
  59.5 2.4 %collective-permute-start.7 = (bf16[432,128]{1,0:T(8,128)(2,1)S(1)}, bf16[432,128]{1,0:T(8,128)(2,1)S(1)}, u32[]{:S(2)}, u32[]{:S(2)}) collective-permute-start(bf16[432,128]{1,0:T(8,128)(2,1)S(1)} %get-tuple-element.53), channel_id=1, source_target_pairs={{0,14},{2,12},{4,10},{6,8},{8,6},{10,4},{12,2},{14,0},{1,15},{3,13... | collective-permute-start | bytes 331784 | tf_op jit(solution)/shard_map/ppermute | solution.py:380
  61.8 0.0 collective-permute-done.24.refs_4_
  61.8 1.0 %collective-permute-start.8 = (bf16[432,128]{1,0:T(8,128)(2,1)S(1)}, bf16[432,128]{1,0:T(8,128)(2,1)S(1)}, u32[]{:S(2)}, u32[]{:S(2)}) collective-permute-start(bf16[432,128]{1,0:T(8,128)(2,1)S(1)} %get-tuple-element.54), channel_id=1, source_target_pairs={{0,2},{2,0},{4,6},{6,4},{8,10},{10,8},{12,14},{14,12},{1,3},{3,1},... | collective-permute-start | bytes 331784 | tf_op jit(solution)/shard_map/ppermute | solution.py:380
  62.8 3.1 %collective-permute-done.25.refs_5_ = bf16[432,128]{1,0:T(8,128)(2,1)S(1)} collective-permute-done((bf16[432,128]{1,0:T(8,128)(2,1)S(1)}, bf16[432,128]{1,0:T(8,128)(2,1)S(1)}, u32[]{:S(2)}, u32[]{:S(2)}) %collective-permute-start.25) | collective-permute-done | bytes 110624 | tf_op jit(solution)/shard_map/ppermute | solution.py:380
  65.9 1.8 %collective-permute-start.9 = (bf16[432,128]{1,0:T(8,128)(2,1)S(1)}, bf16[432,128]{1,0:T(8,128)(2,1)S(1)}, u32[]{:S(2)}, u32[]{:S(2)}) collective-permute-start(bf16[432,128]{1,0:T(8,128)(2,1)S(1)} %get-tuple-element.55), channel_id=1, source_target_pairs={{0,12},{2,14},{4,8},{6,10},{8,4},{10,6},{12,0},{14,2},{1,13},{3,15... | collective-permute-start | bytes 331784 | tf_op jit(solution)/shard_map/ppermute | solution.py:380
  67.7 0.0 collective-permute-done.26.refs_6_
  67.7 2.2 %collective-permute-done.27.refs_7_ = bf16[432,128]{1,0:T(8,128)(2,1)S(1)} collective-permute-done((bf16[432,128]{1,0:T(8,128)(2,1)S(1)}, bf16[432,128]{1,0:T(8,128)(2,1)S(1)}, u32[]{:S(2)}, u32[]{:S(2)}) %collective-permute-start.27) | collective-permute-done | bytes 110624 | tf_op jit(solution)/shard_map/ppermute | solution.py:380
  69.9 1.3 %collective-permute-start.11 = (bf16[432,128]{1,0:T(8,128)(2,1)S(1)}, bf16[432,128]{1,0:T(8,128)(2,1)S(1)}, u32[]{:S(2)}, u32[]{:S(2)}) collective-permute-start(bf16[432,128]{1,0:T(8,128)(2,1)S(1)} %get-tuple-element.57), channel_id=1, source_target_pairs={{0,10},{2,8},{4,14},{6,12},{8,2},{10,0},{12,6},{14,4},{1,11},{3,9}... | collective-permute-start | bytes 331784 | tf_op jit(solution)/shard_map/ppermute | solution.py:380
  71.1 5.4 %collective-permute-start.12 = (bf16[432,128]{1,0:T(8,128)(2,1)S(1)}, bf16[432,128]{1,0:T(8,128)(2,1)S(1)}, u32[]{:S(2)}, u32[]{:S(2)}) collective-permute-start(bf16[432,128]{1,0:T(8,128)(2,1)S(1)} %get-tuple-element.58), channel_id=1, source_target_pairs={{0,6},{2,4},{4,2},{6,0},{8,14},{10,12},{12,10},{14,8},{1,7},{3,5},... | collective-permute-start | bytes 331784 | tf_op jit(solution)/shard_map/ppermute | solution.py:380
  76.5 2.8 %shard_map.142 = (bf16[2,192,1440]{2,1,0:T(8,128)(2,1)}, bf16[2,192,1440]{2,1,0:T(8,128)(2,1)}, f32[2,2304]{1,0:T(2,128)S(1)}, f32[2,2304]{1,0:T(2,128)S(1)}) custom-call(bf16[432,128]{1,0:T(8,128)(2,1)S(1)} %get-tuple-element.68.refs_0_, bf16[432,128]{1,0:T(8,128)(2,1)S(1)} %collective-permute-done.21.refs_1_, ...), custom_call_target="tpu_custom_call" | custom-call | flops 4000000000 | bytes 5242880 | tf_op jit(solution)/shard_map/pallas_call | solution.py:203
  79.3 3.6 %collective-permute-done.11.refs_5_ = bf16[432,128]{1,0:T(8,128)(2,1)S(1)} collective-permute-done((bf16[432,128]{1,0:T(8,128)(2,1)S(1)}, bf16[432,128]{1,0:T(8,128)(2,1)S(1)}, u32[]{:S(2)}, u32[]{:S(2)}) %collective-permute-start.11) | collective-permute-done | bytes 110624 | tf_op jit(solution)/shard_map/ppermute | solution.py:380
  82.9 0.0 collective-permute-done.13.refs_7_
  83.0 2.6 %shard_map.143 = (bf16[2,192,1440]{2,1,0:T(8,128)(2,1)}, bf16[2,192,1440]{2,1,0:T(8,128)(2,1)}, f32[2,2304]{1,0:T(2,128)}, f32[2,2304]{1,0:T(2,128)}) custom-call(bf16[432,128]{1,0:T(8,128)(2,1)S(1)} %get-tuple-element.52.refs_0_, bf16[432,128]{1,0:T(8,128)(2,1)S(1)} %collective-permute-done.7.refs_1_, ...), custom_call_target="tpu_custom_call", output_to_operand_aliasing={{0}: (12, {}), {1}: (13, {})} | custom-call | flops 4000000000 | bytes 5242880 | tf_op jit(solution)/shard_map/pallas_call | solution.py:203
  (42 shorter events, 0.1 us)
Async XLA Ops:
  0.6 17.4 %copy-start = (bf16[2,1440,192]{1,2,0:T(8,128)(2,1)S(1)}, bf16[2,1440,192]{1,2,0:T(8,128)(2,1)}, u32[]{:S(2)}) copy-start(bf16[2,1440,192]{1,2,0:T(8,128)(2,1)} %param.11) | copy-start | bytes 3317764
  0.6 17.3 %copy-start.1 = (bf16[2,1440,192]{1,2,0:T(8,128)(2,1)S(1)}, bf16[2,1440,192]{1,2,0:T(8,128)(2,1)}, u32[]{:S(2)}) copy-start(bf16[2,1440,192]{1,2,0:T(8,128)(2,1)} %param.12) | copy-start | bytes 3317764
  0.7 17.3 %copy-start.10 = (f32[1,1024]{1,0:T(1,128)S(1)}, f32[1,1024]{1,0:T(1,128)}, u32[]{:S(2)}) copy-start(f32[1,1024]{1,0:T(1,128)} %constant.18.clone.scale_ref) | copy-start | bytes 12292
  6.1 16.1 %collective-permute-start.14 = (bf16[384,128]{1,0:T(8,128)(2,1)}, bf16[384,128]{1,0:T(8,128)(2,1)S(1)}, u32[]{:S(2)}, u32[]{:S(2)}) collective-permute-start(bf16[384,128]{1,0:T(8,128)(2,1)} %get-tuple-element.61), channel_id=1, source_target_pairs={{0,14},{2,12},{4,10},{6,8},{8,6},{10,4},{12,2},{14,0},{1,15},{3,13... | collective-permute-start | bytes 294920 | tf_op jit(solution)/shard_map/ppermute | solution.py:380
  12.1 10.2 %collective-permute-start.15 = (bf16[384,128]{1,0:T(8,128)(2,1)}, bf16[384,128]{1,0:T(8,128)(2,1)S(1)}, u32[]{:S(2)}, u32[]{:S(2)}) collective-permute-start(bf16[384,128]{1,0:T(8,128)(2,1)} %get-tuple-element.62), channel_id=1, source_target_pairs={{0,2},{2,0},{4,6},{6,4},{8,10},{10,8},{12,14},{14,12},{1,3},{3,1},... | collective-permute-start | bytes 294920 | tf_op jit(solution)/shard_map/ppermute | solution.py:380
  12.6 10.3 %collective-permute-start.16 = (bf16[384,128]{1,0:T(8,128)(2,1)}, bf16[384,128]{1,0:T(8,128)(2,1)S(1)}, u32[]{:S(2)}, u32[]{:S(2)}) collective-permute-start(bf16[384,128]{1,0:T(8,128)(2,1)} %get-tuple-element.63), channel_id=1, source_target_pairs={{0,12},{2,14},{4,8},{6,10},{8,4},{10,6},{12,0},{14,2},{1,13},{3,15... | collective-permute-start | bytes 294920 | tf_op jit(solution)/shard_map/ppermute | solution.py:380
  12.7 14.8 %collective-permute-start.17 = (bf16[384,128]{1,0:T(8,128)(2,1)}, bf16[384,128]{1,0:T(8,128)(2,1)S(1)}, u32[]{:S(2)}, u32[]{:S(2)}) collective-permute-start(bf16[384,128]{1,0:T(8,128)(2,1)} %get-tuple-element.64), channel_id=1, source_target_pairs={{0,4},{2,6},{4,0},{6,2},{8,12},{10,14},{12,8},{14,10},{1,5},{3,7},... | collective-permute-start | bytes 294920 | tf_op jit(solution)/shard_map/ppermute | solution.py:380
  12.7 26.8 %copy-start.2 = (bf16[4,96,192]{2,1,0:T(8,128)(2,1)S(1)}, bf16[4,96,192]{2,1,0:T(8,128)(2,1)}, u32[]{:S(2)}) copy-start(bf16[4,96,192]{2,1,0:T(8,128)(2,1)} %refs_9_.5) | copy-start | bytes 442372
  12.7 26.9 %copy-start.3 = (bf16[4,96,192]{2,1,0:T(8,128)(2,1)S(1)}, bf16[4,96,192]{2,1,0:T(8,128)(2,1)}, u32[]{:S(2)}) copy-start(bf16[4,96,192]{2,1,0:T(8,128)(2,1)} %refs_11_.3) | copy-start | bytes 442372
  12.7 26.9 %copy-start.4 = (f32[4,192]{1,0:T(4,128)S(1)}, f32[4,192]{1,0:T(4,128)}, u32[]{:S(2)}) copy-start(f32[4,192]{1,0:T(4,128)} %refs_10_.3) | copy-start | bytes 9220
  12.7 26.9 %copy-start.5 = (f32[4,192]{1,0:T(4,128)S(1)}, f32[4,192]{1,0:T(4,128)}, u32[]{:S(2)}) copy-start(f32[4,192]{1,0:T(4,128)} %refs_12_.3) | copy-start | bytes 9220
  12.7 15.3 %collective-permute-start.18 = (bf16[384,128]{1,0:T(8,128)(2,1)}, bf16[384,128]{1,0:T(8,128)(2,1)S(1)}, u32[]{:S(2)}, u32[]{:S(2)}) collective-permute-start(bf16[384,128]{1,0:T(8,128)(2,1)} %get-tuple-element.65), channel_id=1, source_target_pairs={{0,10},{2,8},{4,14},{6,12},{8,2},{10,0},{12,6},{14,4},{1,11},{3,9}... | collective-permute-start | bytes 294920 | tf_op jit(solution)/shard_map/ppermute | solution.py:380
  18.0 1.8 %copy-start.7 = (bf16[4,1440,256]{2,1,0:T(8,128)(2,1)S(1)}, bf16[4,1440,256]{2,1,0:T(8,128)(2,1)}, u32[]{:S(2)}) copy-start(bf16[4,1440,256]{2,1,0:T(8,128)(2,1)} %constant.16.clone.table_ref) | copy-start | bytes 8847364
  19.8 2.3 %copy-start.13 = (bf16[384,128]{1,0:T(8,128)(2,1)S(1)}, bf16[384,128]{1,0:T(8,128)(2,1)}, u32[]{:S(2)}) copy-start(bf16[384,128]{1,0:T(8,128)(2,1)} %get-tuple-element.66) | copy-start | bytes 294916
  19.8 2.4 %copy-start.12 = (bf16[384,128]{1,0:T(8,128)(2,1)S(1)}, bf16[384,128]{1,0:T(8,128)(2,1)}, u32[]{:S(2)}) copy-start(bf16[384,128]{1,0:T(8,128)(2,1)} %get-tuple-element.67) | copy-start | bytes 294916
  19.8 19.8 %copy-start.8 = (bf16[256,512]{1,0:T(8,128)(2,1)S(1)}, bf16[256,512]{1,0:T(8,128)(2,1)}, u32[]{:S(2)}) copy-start(bf16[256,512]{1,0:T(8,128)(2,1)} %constant.20.clone.refs_8_) | copy-start | bytes 786436
  19.8 19.8 %copy-start.11 = (bf16[384,128]{1,0:T(8,128)(2,1)S(1)}, bf16[384,128]{1,0:T(8,128)(2,1)}, u32[]{:S(2)}) copy-start(bf16[384,128]{1,0:T(8,128)(2,1)} %get-tuple-element.60.refs_0_) | copy-start | bytes 294916
  22.1 6.9 %collective-permute-start.19 = (bf16[384,128]{1,0:T(8,128)(2,1)S(1)}, bf16[384,128]{1,0:T(8,128)(2,1)S(1)}, u32[]{:S(2)}, u32[]{:S(2)}) collective-permute-start(bf16[384,128]{1,0:T(8,128)(2,1)S(1)} %copy-done.13), channel_id=1, source_target_pairs={{0,6},{2,4},{4,2},{6,0},{8,14},{10,12},{12,10},{14,8},{1,7},{3,5},... | collective-permute-start | bytes 294920 | tf_op jit(solution)/shard_map/ppermute | solution.py:380
  22.2 13.3 %collective-permute-start.20 = (bf16[384,128]{1,0:T(8,128)(2,1)S(1)}, bf16[384,128]{1,0:T(8,128)(2,1)S(1)}, u32[]{:S(2)}, u32[]{:S(2)}) collective-permute-start(bf16[384,128]{1,0:T(8,128)(2,1)S(1)} %copy-done.12), channel_id=1, source_target_pairs={{0,8},{2,10},{4,12},{6,14},{8,0},{10,2},{12,4},{14,6},{1,9},{3,11}... | collective-permute-start | bytes 294920 | tf_op jit(solution)/shard_map/ppermute | solution.py:380
  22.9 12.7 %collective-permute-start = (bf16[384,128]{1,0:T(8,128)(2,1)S(1)}, bf16[384,128]{1,0:T(8,128)(2,1)S(1)}, u32[]{:S(2)}, u32[]{:S(2)}) collective-permute-start(bf16[384,128]{1,0:T(8,128)(2,1)S(1)} %get-tuple-element.45), channel_id=1, source_target_pairs={{0,14},{2,12},{4,10},{6,8},{8,6},{10,4},{12,2},{14,0},{1,15},{3,13... | collective-permute-start | bytes 294920 | tf_op jit(solution)/shard_map/ppermute | solution.py:380
  27.5 12.0 %collective-permute-start.1 = (bf16[384,128]{1,0:T(8,128)(2,1)S(1)}, bf16[384,128]{1,0:T(8,128)(2,1)S(1)}, u32[]{:S(2)}, u32[]{:S(2)}) collective-permute-start(bf16[384,128]{1,0:T(8,128)(2,1)S(1)} %get-tuple-element.46), channel_id=1, source_target_pairs={{0,2},{2,0},{4,6},{6,4},{8,10},{10,8},{12,14},{14,12},{1,3},{3,1},... | collective-permute-start | bytes 294920 | tf_op jit(solution)/shard_map/ppermute | solution.py:380
  28.0 15.8 %collective-permute-start.2 = (bf16[384,128]{1,0:T(8,128)(2,1)S(1)}, bf16[384,128]{1,0:T(8,128)(2,1)S(1)}, u32[]{:S(2)}, u32[]{:S(2)}) collective-permute-start(bf16[384,128]{1,0:T(8,128)(2,1)S(1)} %get-tuple-element.47), channel_id=1, source_target_pairs={{0,12},{2,14},{4,8},{6,10},{8,4},{10,6},{12,0},{14,2},{1,13},{3,15... | collective-permute-start | bytes 294920 | tf_op jit(solution)/shard_map/ppermute | solution.py:380
  29.0 17.3 %collective-permute-start.3 = (bf16[384,128]{1,0:T(8,128)(2,1)S(1)}, bf16[384,128]{1,0:T(8,128)(2,1)S(1)}, u32[]{:S(2)}, u32[]{:S(2)}) collective-permute-start(bf16[384,128]{1,0:T(8,128)(2,1)S(1)} %get-tuple-element.48), channel_id=1, source_target_pairs={{0,4},{2,6},{4,0},{6,2},{8,12},{10,14},{12,8},{14,10},{1,5},{3,7},... | collective-permute-start | bytes 294920 | tf_op jit(solution)/shard_map/ppermute | solution.py:380
  35.6 11.7 %collective-permute-start.4 = (bf16[384,128]{1,0:T(8,128)(2,1)S(1)}, bf16[384,128]{1,0:T(8,128)(2,1)S(1)}, u32[]{:S(2)}, u32[]{:S(2)}) collective-permute-start(bf16[384,128]{1,0:T(8,128)(2,1)S(1)} %get-tuple-element.49), channel_id=1, source_target_pairs={{0,10},{2,8},{4,14},{6,12},{8,2},{10,0},{12,6},{14,4},{1,11},{3,9}... | collective-permute-start | bytes 294920 | tf_op jit(solution)/shard_map/ppermute | solution.py:380
  35.6 13.7 %collective-permute-start.5 = (bf16[384,128]{1,0:T(8,128)(2,1)S(1)}, bf16[384,128]{1,0:T(8,128)(2,1)S(1)}, u32[]{:S(2)}, u32[]{:S(2)}) collective-permute-start(bf16[384,128]{1,0:T(8,128)(2,1)S(1)} %get-tuple-element.50), channel_id=1, source_target_pairs={{0,6},{2,4},{4,2},{6,0},{8,14},{10,12},{12,10},{14,8},{1,7},{3,5},... | collective-permute-start | bytes 294920 | tf_op jit(solution)/shard_map/ppermute | solution.py:380
  39.5 10.3 %collective-permute-start.6 = (bf16[384,128]{1,0:T(8,128)(2,1)S(1)}, bf16[384,128]{1,0:T(8,128)(2,1)S(1)}, u32[]{:S(2)}, u32[]{:S(2)}) collective-permute-start(bf16[384,128]{1,0:T(8,128)(2,1)S(1)} %get-tuple-element.51), channel_id=1, source_target_pairs={{0,8},{2,10},{4,12},{6,14},{8,0},{10,2},{12,4},{14,6},{1,9},{3,11}... | collective-permute-start | bytes 294920 | tf_op jit(solution)/shard_map/ppermute | solution.py:380
  43.9 12.6 %collective-permute-start.21 = (bf16[432,128]{1,0:T(8,128)(2,1)S(1)}, bf16[432,128]{1,0:T(8,128)(2,1)S(1)}, u32[]{:S(2)}, u32[]{:S(2)}) collective-permute-start(bf16[432,128]{1,0:T(8,128)(2,1)S(1)} %get-tuple-element.69), channel_id=1, source_target_pairs={{0,14},{2,12},{4,10},{6,8},{8,6},{10,4},{12,2},{14,0},{1,15},{3,13... | collective-permute-start | bytes 331784 | tf_op jit(solution)/shard_map/ppermute | solution.py:380
  46.3 11.4 %collective-permute-start.22 = (bf16[432,128]{1,0:T(8,128)(2,1)S(1)}, bf16[432,128]{1,0:T(8,128)(2,1)S(1)}, u32[]{:S(2)}, u32[]{:S(2)}) collective-permute-start(bf16[432,128]{1,0:T(8,128)(2,1)S(1)} %get-tuple-element.70), channel_id=1, source_target_pairs={{0,2},{2,0},{4,6},{6,4},{8,10},{10,8},{12,14},{14,12},{1,3},{3,1},... | collective-permute-start | bytes 331784 | tf_op jit(solution)/shard_map/ppermute | solution.py:380
  47.3 12.2 %collective-permute-start.23 = (bf16[432,128]{1,0:T(8,128)(2,1)S(1)}, bf16[432,128]{1,0:T(8,128)(2,1)S(1)}, u32[]{:S(2)}, u32[]{:S(2)}) collective-permute-start(bf16[432,128]{1,0:T(8,128)(2,1)S(1)} %get-tuple-element.71), channel_id=1, source_target_pairs={{0,12},{2,14},{4,8},{6,10},{8,4},{10,6},{12,0},{14,2},{1,13},{3,15... | collective-permute-start | bytes 331784 | tf_op jit(solution)/shard_map/ppermute | solution.py:380
  49.3 12.6 %collective-permute-start.24 = (bf16[432,128]{1,0:T(8,128)(2,1)S(1)}, bf16[432,128]{1,0:T(8,128)(2,1)S(1)}, u32[]{:S(2)}, u32[]{:S(2)}) collective-permute-start(bf16[432,128]{1,0:T(8,128)(2,1)S(1)} %get-tuple-element.72), channel_id=1, source_target_pairs={{0,4},{2,6},{4,0},{6,2},{8,12},{10,14},{12,8},{14,10},{1,5},{3,7},... | collective-permute-start | bytes 331784 | tf_op jit(solution)/shard_map/ppermute | solution.py:380
  49.9 16.0 %collective-permute-start.25 = (bf16[432,128]{1,0:T(8,128)(2,1)S(1)}, bf16[432,128]{1,0:T(8,128)(2,1)S(1)}, u32[]{:S(2)}, u32[]{:S(2)}) collective-permute-start(bf16[432,128]{1,0:T(8,128)(2,1)S(1)} %get-tuple-element.73), channel_id=1, source_target_pairs={{0,10},{2,8},{4,14},{6,12},{8,2},{10,0},{12,6},{14,4},{1,11},{3,9}... | collective-permute-start | bytes 331784 | tf_op jit(solution)/shard_map/ppermute | solution.py:380
  52.2 24.3 %copy-start.6 = (bf16[1024,1440]{1,0:T(8,128)(2,1)S(1)}, bf16[1024,1440]{1,0:T(8,128)(2,1)}, u32[]{:S(2)}) copy-start(bf16[1024,1440]{1,0:T(8,128)(2,1)} %constant.17.clone.refs_8_) | copy-start | bytes 8847364
  52.2 24.3 %copy-start.9 = (f32[8,128]{1,0:T(8,128)S(1)}, f32[8,128]{1,0:T(8,128)}, u32[]{:S(2)}) copy-start(f32[8,128]{1,0:T(8,128)} %constant.19.clone.refs_9_) | copy-start | bytes 12292
  56.5 11.2 %collective-permute-start.26 = (bf16[432,128]{1,0:T(8,128)(2,1)S(1)}, bf16[432,128]{1,0:T(8,128)(2,1)S(1)}, u32[]{:S(2)}, u32[]{:S(2)}) collective-permute-start(bf16[432,128]{1,0:T(8,128)(2,1)S(1)} %get-tuple-element.74), channel_id=1, source_target_pairs={{0,6},{2,4},{4,2},{6,0},{8,14},{10,12},{12,10},{14,8},{1,7},{3,5},... | collective-permute-start | bytes 331784 | tf_op jit(solution)/shard_map/ppermute | solution.py:380
  57.7 12.2 %collective-permute-start.27 = (bf16[432,128]{1,0:T(8,128)(2,1)S(1)}, bf16[432,128]{1,0:T(8,128)(2,1)S(1)}, u32[]{:S(2)}, u32[]{:S(2)}) collective-permute-start(bf16[432,128]{1,0:T(8,128)(2,1)S(1)} %get-tuple-element.75), channel_id=1, source_target_pairs={{0,8},{2,10},{4,12},{6,14},{8,0},{10,2},{12,4},{14,6},{1,9},{3,11}... | collective-permute-start | bytes 331784 | tf_op jit(solution)/shard_map/ppermute | solution.py:380
  59.5 11.7 %collective-permute-start.7 = (bf16[432,128]{1,0:T(8,128)(2,1)S(1)}, bf16[432,128]{1,0:T(8,128)(2,1)S(1)}, u32[]{:S(2)}, u32[]{:S(2)}) collective-permute-start(bf16[432,128]{1,0:T(8,128)(2,1)S(1)} %get-tuple-element.53), channel_id=1, source_target_pairs={{0,14},{2,12},{4,10},{6,8},{8,6},{10,4},{12,2},{14,0},{1,15},{3,13... | collective-permute-start | bytes 331784 | tf_op jit(solution)/shard_map/ppermute | solution.py:380
  61.8 14.7 %collective-permute-start.8 = (bf16[432,128]{1,0:T(8,128)(2,1)S(1)}, bf16[432,128]{1,0:T(8,128)(2,1)S(1)}, u32[]{:S(2)}, u32[]{:S(2)}) collective-permute-start(bf16[432,128]{1,0:T(8,128)(2,1)S(1)} %get-tuple-element.54), channel_id=1, source_target_pairs={{0,2},{2,0},{4,6},{6,4},{8,10},{10,8},{12,14},{14,12},{1,3},{3,1},... | collective-permute-start | bytes 331784 | tf_op jit(solution)/shard_map/ppermute | solution.py:380
  65.9 13.4 %collective-permute-start.9 = (bf16[432,128]{1,0:T(8,128)(2,1)S(1)}, bf16[432,128]{1,0:T(8,128)(2,1)S(1)}, u32[]{:S(2)}, u32[]{:S(2)}) collective-permute-start(bf16[432,128]{1,0:T(8,128)(2,1)S(1)} %get-tuple-element.55), channel_id=1, source_target_pairs={{0,12},{2,14},{4,8},{6,10},{8,4},{10,6},{12,0},{14,2},{1,13},{3,15... | collective-permute-start | bytes 331784 | tf_op jit(solution)/shard_map/ppermute | solution.py:380
  67.7 11.6 %collective-permute-start.10 = (bf16[432,128]{1,0:T(8,128)(2,1)S(1)}, bf16[432,128]{1,0:T(8,128)(2,1)S(1)}, u32[]{:S(2)}, u32[]{:S(2)}) collective-permute-start(bf16[432,128]{1,0:T(8,128)(2,1)S(1)} %get-tuple-element.56), channel_id=1, source_target_pairs={{0,4},{2,6},{4,0},{6,2},{8,12},{10,14},{12,8},{14,10},{1,5},{3,7},... | collective-permute-start | bytes 331784 | tf_op jit(solution)/shard_map/ppermute | solution.py:380
  69.9 13.1 %collective-permute-start.11 = (bf16[432,128]{1,0:T(8,128)(2,1)S(1)}, bf16[432,128]{1,0:T(8,128)(2,1)S(1)}, u32[]{:S(2)}, u32[]{:S(2)}) collective-permute-start(bf16[432,128]{1,0:T(8,128)(2,1)S(1)} %get-tuple-element.57), channel_id=1, source_target_pairs={{0,10},{2,8},{4,14},{6,12},{8,2},{10,0},{12,6},{14,4},{1,11},{3,9}... | collective-permute-start | bytes 331784 | tf_op jit(solution)/shard_map/ppermute | solution.py:380
  71.1 11.8 %collective-permute-start.12 = (bf16[432,128]{1,0:T(8,128)(2,1)S(1)}, bf16[432,128]{1,0:T(8,128)(2,1)S(1)}, u32[]{:S(2)}, u32[]{:S(2)}) collective-permute-start(bf16[432,128]{1,0:T(8,128)(2,1)S(1)} %get-tuple-element.58), channel_id=1, source_target_pairs={{0,6},{2,4},{4,2},{6,0},{8,14},{10,12},{12,10},{14,8},{1,7},{3,5},... | collective-permute-start | bytes 331784 | tf_op jit(solution)/shard_map/ppermute | solution.py:380
  76.5 6.5 %collective-permute-start.13 = (bf16[432,128]{1,0:T(8,128)(2,1)S(1)}, bf16[432,128]{1,0:T(8,128)(2,1)S(1)}, u32[]{:S(2)}, u32[]{:S(2)}) collective-permute-start(bf16[432,128]{1,0:T(8,128)(2,1)S(1)} %get-tuple-element.59), channel_id=1, source_target_pairs={{0,8},{2,10},{4,12},{6,14},{8,0},{10,2},{12,4},{14,6},{1,9},{3,11}... | collective-permute-start | bytes 331784 | tf_op jit(solution)/shard_map/ppermute | solution.py:380
